TPU v7x, 32 devices: a whole 2x2x4 slice. The times are simulated.
32 devices in a mesh: row: 4 (over y, x), col: 8 (over z, core).
Axes of the slice: x: 2, y: 2, z: 4, core: 2. Of those that a mesh axis runs over, the one named last changes fastest.
Arguments:
- density: bfloat16 [8, 64, 16384], P('row', None, 'col'), may hold values from -0.8984375 to 0.8984375
- density_rows: int32 [8, 8, 32], replicated, may hold values from 0 to 48, as said below
- square_rows: int32 [8, 8, 32], replicated, may hold values from 0 to 48, as said below
- panel_shift: int32 [8], replicated, may hold values from 0 to 48
Outputs:
- purified: float32 [8, 64, 16384], P('row', None, 'col')
Inputs may be any that keep to these rules, and one draw needn't show every extreme that they name: `density_rows`: for every tile, 32 distinct block rows in increasing order. `square_rows`: for every tile, 32 distinct block rows in increasing order.
All inputs are finite; a program needn't handle non-finite values.
Results may differ from a plain program's by a relative error of at most 0.0029.
Values may be sent and summed in bfloat16 or wider, within the bound.
No kernel may reach another device: no remote copies, remote signals or barrier semaphores. Data moves between devices by JAX's collectives and lax.ppermute only.
A program may use at most 64 MiB of HBM per device.

v0:
```python
import jax
import jax.numpy as jnp
from jax import lax
from jax.sharding import PartitionSpec as P

PANEL = 49


def shifted(shard, axis, by):
    devices = lax.axis_size(axis)
    return lax.ppermute(shard, axis, [(i, (i + by) % devices) for i in range(devices)])


def body(density, density_rows, square_rows, panel_shift):
    row_id = lax.axis_index("row")
    col_id = lax.axis_index("col")
    n_col = lax.axis_size("col")
    levels = lax.axis_size("row").bit_length() - 1
    blk = density.shape[1]
    rh = density_rows.shape[2]
    first = 2 * row_id
    own_shift = lax.dynamic_slice(panel_shift, (first,), (2,))

    def make_turn(left_rows, right_rows, out_rows):
        crow = lax.dynamic_slice(out_rows, (first, col_id, 0), (2, 1, rh)).reshape(2, rh)

        def apply_turn(panel, left_tile, right_slot, total):
            arow = lax.dynamic_slice(left_rows, (first, panel, 0), (2, 1, rh)).reshape(2, rh)
            brow = lax.dynamic_slice(right_rows, (panel, col_id, 0), (1, 1, rh)).reshape(rh)
            far_shift = lax.dynamic_slice(panel_shift, (panel,), (1,))
            match_a = arow[:, None, :] == crow[:, :, None]
            has_a = jnp.any(match_a, axis=-1)
            target = jnp.mod(crow + far_shift[0] - own_shift[:, None], PANEL)
            match_b = jnp.logical_and(brow[None, None, :] == target[:, :, None], has_a[:, :, None])
            left_view = left_tile.reshape(2, blk, rh, blk)
            right_view = right_slot.reshape(blk, rh, blk)
            picked_a = jnp.einsum(
                "hea,hxay->hxey",
                match_a.astype(jnp.bfloat16),
                left_view,
                preferred_element_type=jnp.float32,
            ).astype(jnp.bfloat16)
            picked_b = jnp.einsum(
                "heb,xby->hxey",
                match_b.astype(jnp.bfloat16),
                right_view,
                preferred_element_type=jnp.float32,
            ).astype(jnp.bfloat16)
            return total + jnp.einsum(
                "hxey,hyez->hxez", picked_a, picked_b, preferred_element_type=jnp.float32
            )

        return apply_turn

    start = jnp.zeros((2, blk, rh, blk), jnp.float32)

    def align_left(tile):
        for level in range(levels):
            moved = shifted(tile, "col", -(2 ** (level + 1)))
            tile = jnp.where(row_id >> level & 1 == 1, moved, tile)
        return tile

    def align_right(pair):
        moved = jnp.stack([pair[1], shifted(pair[0], "row", -1)])
        pair = jnp.where(col_id & 1 == 1, moved, pair)
        for level in range(1, levels + 1):
            moved = shifted(pair, "row", -(2 ** (level - 1)))
            pair = jnp.where(col_id >> level & 1 == 1, moved, pair)
        return pair

    def multiply(left, left_rows, right, right_rows, out_rows):
        apply_turn = make_turn(left_rows, right_rows, out_rows)

        def round_body(turn_pair, carry):
            left_tile, right_pair, total = carry
            for inner in range(2):
                step = 2 * turn_pair + inner
                panel = (col_id + first + step) % n_col
                total = apply_turn(panel, left_tile, right_pair[0], total)
                left_tile = shifted(left_tile, "col", -1)
                right_pair = jnp.stack([right_pair[1], shifted(right_pair[0], "row", -1)])
            return (left_tile, right_pair, total)

        left_end, right_end, total = lax.fori_loop(0, n_col // 2, round_body, (left, right, start))
        return (total, right_end)

    aligned_right = align_right(density)
    square_total, returned_right = multiply(
        align_left(density), density_rows, aligned_right, density_rows, square_rows
    )
    square = square_total.astype(jnp.bfloat16).reshape(2, blk, rh * blk)
    second_right = align_right(density)
    cube_total, unused_right = multiply(
        align_left(square), square_rows, second_right, density_rows, square_rows
    )
    purified = 3.0 * square.astype(jnp.float32) - 2.0 * cube_total.reshape(2, blk, rh * blk)
    return purified


def solution(mesh):
    placed = (P("row", None, "col"), P(), P(), P())
    return jax.shard_map(
        body, mesh=mesh, in_specs=placed, out_specs=P("row", None, "col"), check_vma=False
    )
```

profile of v0, /device:TPU:0, one launch (start us, length us, event | category | flops | bytes accessed | tf_op | source)
XLA Modules:
  0.0 354.8 jit_solution(6468517060623158963)
XLA Ops:
  0.0 5.0 %collective-permute-start.8 = (bf16[2,64,2048]{2,1,0:T(8,128)(2,1)}, bf16[2,64,2048]{2,1,0:T(8,128)(2,1)S(1)}, u32[]{:S(2)}, u32[]{:S(2)}) collective-permute-start(bf16[2,64,2048]{2,1,0:T(8,128)(2,1)} %param.8), channel_id=1, source_target_pairs={{0,6},{1,7},{2,0},{3,1},{4,2},{5,3},{6,4},{7,5},{8,14},{9,15},{10,... | collective-permute-start | bytes 1572872 | tf_op jit(solution)/shard_map/ppermute | solution.py:11
  6.1 2.5 collective-permute-start.10
  8.6 5.3 %collective-permute-done.10 = bf16[64,2048]{1,0:T(8,128)(2,1)S(1)} collective-permute-done((bf16[64,2048]{1,0:T(8,128)(2,1)S(1)}, bf16[64,2048]{1,0:T(8,128)(2,1)S(1)}, u32[]{:S(2)}, u32[]{:S(2)}) %collective-permute-start.10) | collective-permute-done | bytes 262176 | tf_op jit(solution)/shard_map/ppermute | solution.py:11
  13.9 2.6 collective-permute-done.8
  17.7 2.5 collective-permute-start.11
  21.7 8.9 %collective-permute-done.11 = bf16[2,64,2048]{2,1,0:T(8,128)(2,1)S(1)} collective-permute-done((bf16[2,64,2048]{2,1,0:T(8,128)(2,1)S(1)}, bf16[2,64,2048]{2,1,0:T(8,128)(2,1)S(1)}, u32[]{:S(2)}, u32[]{:S(2)}) %collective-permute-start.11) | collective-permute-done | bytes 524320 | tf_op jit(solution)/shard_map/ppermute | solution.py:11
  32.3 12.6 %collective-permute-done.9 = bf16[2,64,2048]{2,1,0:T(8,128)(2,1)S(1)} collective-permute-done((bf16[2,64,2048]{2,1,0:T(8,128)(2,1)S(1)}, bf16[2,64,2048]{2,1,0:T(8,128)(2,1)S(1)}, u32[]{:S(2)}, u32[]{:S(2)}) %collective-permute-start.9) | collective-permute-done | bytes 524320 | tf_op jit(solution)/shard_map/ppermute | solution.py:11
  48.6 129.8 %while.42 = (s32[]{:T(128)}, bf16[2,64,2048]{2,1,0:T(8,128)(2,1)}, bf16[2,64,2048]{2,1,0:T(8,128)(2,1)}, f32[2,64,32,64]{1,3,2,0:T(8,128)}, s32[]{:T(128)}, /*in...) while((s32[]{:T(128)}, bf16[2,64,2048]{2,1,0:T(8,128)(2,1)}, ...), condition=%wide.region_3.4_spmd.clone, body=%wide.region_0.3_spmd.clone.sunk | while | flops 135287712 | bytes 32511756 | solution.py:84
  54.3 2.1 reshape.198
  65.2 2.2 fusion.127
  69.4 2.8 reshape.200
  75.1 4.3 %collective-permute-done.1 = bf16[2,64,2048]{2,1,0:T(8,128)(2,1)} collective-permute-done((bf16[2,64,2048]{2,1,0:T(8,128)(2,1)}, bf16[2,64,2048]{2,1,0:T(8,128)(2,1)}, u32[]{:S(2)}, u32[]{:S(2)}) %collective-permute-start.1) | collective-permute-done | bytes 524320 | tf_op jit(solution)/shard_map/while/body/eval_jaxpr/ppermute | solution.py:11
  79.4 3.7 %collective-permute-start = (bf16[2,64,2048]{2,1,0:T(8,128)(2,1)}, bf16[2,64,2048]{2,1,0:T(8,128)(2,1)}, u32[]{:S(2)}, u32[]{:S(2)}) collective-permute-start(bf16[2,64,2048]{2,1,0:T(8,128)(2,1)} %get-tuple-element.1120), channel_id=1, source_target_pairs={{0,7},{1,0},{2,1},{3,2},{4,3},{5,4},{6,5},{7,6},{8,15},{9,8},{10,9... | collective-permute-start | bytes 1572872 | tf_op jit(solution)/shard_map/while/body/eval_jaxpr/ppermute | solution.py:11
  87.7 2.1 reshape.198
  98.7 2.2 fusion.127
  102.8 2.8 reshape.200
  108.3 4.3 %collective-permute-done.1 = bf16[2,64,2048]{2,1,0:T(8,128)(2,1)} collective-permute-done((bf16[2,64,2048]{2,1,0:T(8,128)(2,1)}, bf16[2,64,2048]{2,1,0:T(8,128)(2,1)}, u32[]{:S(2)}, u32[]{:S(2)}) %collective-permute-start.1) | collective-permute-done | bytes 524320 | tf_op jit(solution)/shard_map/while/body/eval_jaxpr/ppermute | solution.py:11
  112.6 3.7 %collective-permute-start = (bf16[2,64,2048]{2,1,0:T(8,128)(2,1)}, bf16[2,64,2048]{2,1,0:T(8,128)(2,1)}, u32[]{:S(2)}, u32[]{:S(2)}) collective-permute-start(bf16[2,64,2048]{2,1,0:T(8,128)(2,1)} %get-tuple-element.1120), channel_id=1, source_target_pairs={{0,7},{1,0},{2,1},{3,2},{4,3},{5,4},{6,5},{7,6},{8,15},{9,8},{10,9... | collective-permute-start | bytes 1572872 | tf_op jit(solution)/shard_map/while/body/eval_jaxpr/ppermute | solution.py:11
  120.4 2.1 reshape.198
  131.3 2.2 fusion.127
  135.5 2.8 reshape.200
  141.0 4.3 %collective-permute-done.1 = bf16[2,64,2048]{2,1,0:T(8,128)(2,1)} collective-permute-done((bf16[2,64,2048]{2,1,0:T(8,128)(2,1)}, bf16[2,64,2048]{2,1,0:T(8,128)(2,1)}, u32[]{:S(2)}, u32[]{:S(2)}) %collective-permute-start.1) | collective-permute-done | bytes 524320 | tf_op jit(solution)/shard_map/while/body/eval_jaxpr/ppermute | solution.py:11
  145.3 3.7 %collective-permute-start = (bf16[2,64,2048]{2,1,0:T(8,128)(2,1)}, bf16[2,64,2048]{2,1,0:T(8,128)(2,1)}, u32[]{:S(2)}, u32[]{:S(2)}) collective-permute-start(bf16[2,64,2048]{2,1,0:T(8,128)(2,1)} %get-tuple-element.1120), channel_id=1, source_target_pairs={{0,7},{1,0},{2,1},{3,2},{4,3},{5,4},{6,5},{7,6},{8,15},{9,8},{10,9... | collective-permute-start | bytes 1572872 | tf_op jit(solution)/shard_map/while/body/eval_jaxpr/ppermute | solution.py:11
  153.5 2.1 reshape.198
  164.5 2.2 fusion.127
  168.6 2.8 reshape.200
  174.2 4.3 %collective-permute-done.1 = bf16[2,64,2048]{2,1,0:T(8,128)(2,1)} collective-permute-done((bf16[2,64,2048]{2,1,0:T(8,128)(2,1)}, bf16[2,64,2048]{2,1,0:T(8,128)(2,1)}, u32[]{:S(2)}, u32[]{:S(2)}) %collective-permute-start.1) | collective-permute-done | bytes 524320 | tf_op jit(solution)/shard_map/while/body/eval_jaxpr/ppermute | solution.py:11
  180.8 12.0 %collective-permute-done.13 = bf16[2,64,2048]{2,1,0:T(8,128)(2,1)S(1)} collective-permute-done((bf16[2,64,2048]{2,1,0:T(8,128)(2,1)S(1)}, bf16[2,64,2048]{2,1,0:T(8,128)(2,1)S(1)}, u32[]{:S(2)}, u32[]{:S(2)}) %collective-permute-start.13) | collective-permute-done | bytes 524320 | tf_op jit(solution)/shard_map/ppermute | solution.py:11
  192.9 25.9 %collective-permute-done.14 = bf16[2,64,2048]{2,1,0:T(8,128)(2,1)S(1)} collective-permute-done((bf16[2,64,2048]{2,1,0:T(8,128)(2,1)S(1)}, bf16[2,64,2048]{2,1,0:T(8,128)(2,1)S(1)}, u32[]{:S(2)}, u32[]{:S(2)}) %collective-permute-start.14) | collective-permute-done | bytes 524320 | tf_op jit(solution)/shard_map/ppermute | solution.py:11
  219.7 129.4 %while.43 = (s32[]{:T(128)}, bf16[2,64,2048]{2,1,0:T(8,128)(2,1)}, bf16[2,64,2048]{2,1,0:T(8,128)(2,1)}, f32[2,64,32,64]{1,3,2,0:T(8,128)}, s32[]{:T(128)}, /*in...) while((s32[]{:T(128)}, bf16[2,64,2048]{2,1,0:T(8,128)(2,1)}, ...), condition=%wide.region_7.8_spmd.clone, body=%wide.region_4.7_spmd.clone.sunk | while | flops 135287712 | bytes 32511764 | solution.py:84
  225.1 2.1 reshape.202
  236.1 2.2 fusion.145
  240.2 2.8 reshape.204
  245.8 4.3 %collective-permute-done.5 = bf16[2,64,2048]{2,1,0:T(8,128)(2,1)} collective-permute-done((bf16[2,64,2048]{2,1,0:T(8,128)(2,1)}, bf16[2,64,2048]{2,1,0:T(8,128)(2,1)}, u32[]{:S(2)}, u32[]{:S(2)}) %collective-permute-start.5) | collective-permute-done | bytes 524320 | tf_op jit(solution)/shard_map/while/body/eval_jaxpr/ppermute | solution.py:11
  250.0 3.7 %collective-permute-start.4 = (bf16[2,64,2048]{2,1,0:T(8,128)(2,1)}, bf16[2,64,2048]{2,1,0:T(8,128)(2,1)}, u32[]{:S(2)}, u32[]{:S(2)}) collective-permute-start(bf16[2,64,2048]{2,1,0:T(8,128)(2,1)} %get-tuple-element.1172), channel_id=1, source_target_pairs={{0,7},{1,0},{2,1},{3,2},{4,3},{5,4},{6,5},{7,6},{8,15},{9,8},{10,9... | collective-permute-start | bytes 1572872 | tf_op jit(solution)/shard_map/while/body/eval_jaxpr/ppermute | solution.py:11
  269.3 2.2 fusion.145
  273.4 2.8 reshape.204
  279.0 4.3 %collective-permute-done.5 = bf16[2,64,2048]{2,1,0:T(8,128)(2,1)} collective-permute-done((bf16[2,64,2048]{2,1,0:T(8,128)(2,1)}, bf16[2,64,2048]{2,1,0:T(8,128)(2,1)}, u32[]{:S(2)}, u32[]{:S(2)}) %collective-permute-start.5) | collective-permute-done | bytes 524320 | tf_op jit(solution)/shard_map/while/body/eval_jaxpr/ppermute | solution.py:11
  283.2 3.7 %collective-permute-start.4 = (bf16[2,64,2048]{2,1,0:T(8,128)(2,1)}, bf16[2,64,2048]{2,1,0:T(8,128)(2,1)}, u32[]{:S(2)}, u32[]{:S(2)}) collective-permute-start(bf16[2,64,2048]{2,1,0:T(8,128)(2,1)} %get-tuple-element.1172), channel_id=1, source_target_pairs={{0,7},{1,0},{2,1},{3,2},{4,3},{5,4},{6,5},{7,6},{8,15},{9,8},{10,9... | collective-permute-start | bytes 1572872 | tf_op jit(solution)/shard_map/while/body/eval_jaxpr/ppermute | solution.py:11
  302.0 2.2 fusion.145
  306.1 2.8 reshape.204
  311.7 4.3 %collective-permute-done.5 = bf16[2,64,2048]{2,1,0:T(8,128)(2,1)} collective-permute-done((bf16[2,64,2048]{2,1,0:T(8,128)(2,1)}, bf16[2,64,2048]{2,1,0:T(8,128)(2,1)}, u32[]{:S(2)}, u32[]{:S(2)}) %collective-permute-start.5) | collective-permute-done | bytes 524320 | tf_op jit(solution)/shard_map/while/body/eval_jaxpr/ppermute | solution.py:11
  315.9 3.7 %collective-permute-start.4 = (bf16[2,64,2048]{2,1,0:T(8,128)(2,1)}, bf16[2,64,2048]{2,1,0:T(8,128)(2,1)}, u32[]{:S(2)}, u32[]{:S(2)}) collective-permute-start(bf16[2,64,2048]{2,1,0:T(8,128)(2,1)} %get-tuple-element.1172), channel_id=1, source_target_pairs={{0,7},{1,0},{2,1},{3,2},{4,3},{5,4},{6,5},{7,6},{8,15},{9,8},{10,9... | collective-permute-start | bytes 1572872 | tf_op jit(solution)/shard_map/while/body/eval_jaxpr/ppermute | solution.py:11
  324.2 2.1 reshape.202
  335.2 2.2 fusion.145
  339.3 2.8 reshape.204
  344.9 4.3 %collective-permute-done.5 = bf16[2,64,2048]{2,1,0:T(8,128)(2,1)} collective-permute-done((bf16[2,64,2048]{2,1,0:T(8,128)(2,1)}, bf16[2,64,2048]{2,1,0:T(8,128)(2,1)}, u32[]{:S(2)}, u32[]{:S(2)}) %collective-permute-start.5) | collective-permute-done | bytes 524320 | tf_op jit(solution)/shard_map/while/body/eval_jaxpr/ppermute | solution.py:11
  352.5 2.3 multiply_subtract_fusion
  (246 shorter events, 165.4 us)
Async XLA Ops:
  0.0 20.2 %copy-start.8 = (s32[8,8,32]{2,1,0:T(8,128)S(1)}, s32[8,8,32]{2,1,0:T(8,128)}, u32[]{:S(2)}) copy-start(s32[8,8,32]{2,1,0:T(8,128)} %param.10) | copy-start | bytes 24580
  0.0 16.5 %collective-permute-start.8 = (bf16[2,64,2048]{2,1,0:T(8,128)(2,1)}, bf16[2,64,2048]{2,1,0:T(8,128)(2,1)S(1)}, u32[]{:S(2)}, u32[]{:S(2)}) collective-permute-start(bf16[2,64,2048]{2,1,0:T(8,128)(2,1)} %param.8), channel_id=1, source_target_pairs={{0,6},{1,7},{2,0},{3,1},{4,2},{5,3},{6,4},{7,5},{8,14},{9,15},{10,... | collective-permute-start | bytes 1572872 | tf_op jit(solution)/shard_map/ppermute | solution.py:11
  6.1 7.8 %collective-permute-start.10 = (bf16[64,2048]{1,0:T(8,128)(2,1)S(1)}, bf16[64,2048]{1,0:T(8,128)(2,1)S(1)}, u32[]{:S(2)}, u32[]{:S(2)}) collective-permute-start(bf16[64,2048]{1,0:T(8,128)(2,1)S(1)} %get-tuple-element.893), channel_id=1, source_target_pairs={{0,24},{8,0},{16,8},{24,16},{1,25},{9,1},{17,9},{25,17},{2,26},{10... | collective-permute-start | bytes 786440 | tf_op jit(solution)/shard_map/ppermute | solution.py:11
  16.6 15.7 %copy-start.6 = (s32[8]{0:T(128)S(1)}, s32[8]{0:T(128)}, u32[]{:S(2)}) copy-start(s32[8]{0:T(128)} %param.11) | copy-start | bytes 100
  16.6 15.7 %copy-start.7 = (s32[8,8,32]{2,1,0:T(8,128)S(1)}, s32[8,8,32]{2,1,0:T(8,128)}, u32[]{:S(2)}) copy-start(s32[8,8,32]{2,1,0:T(8,128)} %param.9) | copy-start | bytes 24580
  17.7 12.8 %collective-permute-start.11 = (bf16[2,64,2048]{2,1,0:T(8,128)(2,1)S(1)}, bf16[2,64,2048]{2,1,0:T(8,128)(2,1)S(1)}, u32[]{:S(2)}, u32[]{:S(2)}) collective-permute-start(bf16[2,64,2048]{2,1,0:T(8,128)(2,1)S(1)} %get-tuple-element.890), channel_id=1, source_target_pairs={{0,24},{8,0},{16,8},{24,16},{1,25},{9,1},{17,9},{25,17},{2,26},{10... | collective-permute-start | bytes 1572872 | tf_op jit(solution)/shard_map/ppermute | solution.py:11
  20.2 24.7 %collective-permute-start.9 = (bf16[2,64,2048]{2,1,0:T(8,128)(2,1)S(1)}, bf16[2,64,2048]{2,1,0:T(8,128)(2,1)S(1)}, u32[]{:S(2)}, u32[]{:S(2)}) collective-permute-start(bf16[2,64,2048]{2,1,0:T(8,128)(2,1)S(1)} %get-tuple-element.891), channel_id=1, source_target_pairs={{0,4},{1,5},{2,6},{3,7},{4,0},{5,1},{6,2},{7,3},{8,12},{9,13},{10,... | collective-permute-start | bytes 1572872 | tf_op jit(solution)/shard_map/ppermute | solution.py:11
  30.6 15.2 %collective-permute-start.12 = (bf16[2,64,2048]{2,1,0:T(8,128)(2,1)S(1)}, bf16[2,64,2048]{2,1,0:T(8,128)(2,1)S(1)}, u32[]{:S(2)}, u32[]{:S(2)}) collective-permute-start(bf16[2,64,2048]{2,1,0:T(8,128)(2,1)S(1)} %broadcast_select_fusion), channel_id=1, source_target_pairs={{0,16},{8,24},{16,0},{24,8},{1,17},{9,25},{17,1},{25,9},{2,18},{10... | collective-permute-start | bytes 1572872 | tf_op jit(solution)/shard_map/ppermute | solution.py:11
  48.6 20.8 %collective-permute-start = (bf16[2,64,2048]{2,1,0:T(8,128)(2,1)}, bf16[2,64,2048]{2,1,0:T(8,128)(2,1)}, u32[]{:S(2)}, u32[]{:S(2)}) collective-permute-start(bf16[2,64,2048]{2,1,0:T(8,128)(2,1)} %get-tuple-element.1120), channel_id=1, source_target_pairs={{0,7},{1,0},{2,1},{3,2},{4,3},{5,4},{6,5},{7,6},{8,15},{9,8},{10,9... | collective-permute-start | bytes 1572872 | tf_op jit(solution)/shard_map/while/body/eval_jaxpr/ppermute | solution.py:11
  52.3 15.1 %collective-permute-start.2 = (bf16[64,2048]{1,0:T(8,128)(2,1)}, bf16[64,2048]{1,0:T(8,128)(2,1)}, u32[]{:S(2)}, u32[]{:S(2)}) collective-permute-start(bf16[64,2048]{1,0:T(8,128)(2,1)} %get-tuple-element.1061), channel_id=1, source_target_pairs={{0,24},{8,0},{16,8},{24,16},{1,25},{9,1},{17,9},{25,17},{2,26},{10... | collective-permute-start | bytes 786440 | tf_op jit(solution)/shard_map/while/body/eval_jaxpr/ppermute | solution.py:11
  52.9 14.6 %collective-permute-start.3 = (bf16[64,2048]{1,0:T(8,128)(2,1)S(1)}, bf16[64,2048]{1,0:T(8,128)(2,1)}, u32[]{:S(2)}, u32[]{:S(2)}) collective-permute-start(bf16[64,2048]{1,0:T(8,128)(2,1)S(1)} %get-tuple-element.1062), channel_id=1, source_target_pairs={{0,24},{8,0},{16,8},{24,16},{1,25},{9,1},{17,9},{25,17},{2,26},{10... | collective-permute-start | bytes 786440 | tf_op jit(solution)/shard_map/while/body/eval_jaxpr/ppermute | solution.py:11
  72.2 7.3 %collective-permute-start.1 = (bf16[2,64,2048]{2,1,0:T(8,128)(2,1)}, bf16[2,64,2048]{2,1,0:T(8,128)(2,1)}, u32[]{:S(2)}, u32[]{:S(2)}) collective-permute-start(bf16[2,64,2048]{2,1,0:T(8,128)(2,1)} %collective-permute-done), channel_id=1, source_target_pairs={{0,7},{1,0},{2,1},{3,2},{4,3},{5,4},{6,5},{7,6},{8,15},{9,8},{10,9... | collective-permute-start | bytes 1572872 | tf_op jit(solution)/shard_map/while/body/eval_jaxpr/ppermute | solution.py:11
  75.1 4.3 %copy-start.1 = (f32[2,64,32,64]{1,3,2,0:T(8,128)}, f32[2,64,32,64]{1,3,2,0:T(8,128)S(1)}, u32[]{:S(2)}) copy-start(f32[2,64,32,64]{1,3,2,0:T(8,128)S(1)} %bitcast_add_fusion.6) | copy-start | bytes 3145732 | tf_op jit(solution)/shard_map/while
  79.4 23.4 %collective-permute-start = (bf16[2,64,2048]{2,1,0:T(8,128)(2,1)}, bf16[2,64,2048]{2,1,0:T(8,128)(2,1)}, u32[]{:S(2)}, u32[]{:S(2)}) collective-permute-start(bf16[2,64,2048]{2,1,0:T(8,128)(2,1)} %get-tuple-element.1120), channel_id=1, source_target_pairs={{0,7},{1,0},{2,1},{3,2},{4,3},{5,4},{6,5},{7,6},{8,15},{9,8},{10,9... | collective-permute-start | bytes 1572872 | tf_op jit(solution)/shard_map/while/body/eval_jaxpr/ppermute | solution.py:11
  85.0 15.9 %collective-permute-start.2 = (bf16[64,2048]{1,0:T(8,128)(2,1)}, bf16[64,2048]{1,0:T(8,128)(2,1)}, u32[]{:S(2)}, u32[]{:S(2)}) collective-permute-start(bf16[64,2048]{1,0:T(8,128)(2,1)} %get-tuple-element.1061), channel_id=1, source_target_pairs={{0,24},{8,0},{16,8},{24,16},{1,25},{9,1},{17,9},{25,17},{2,26},{10... | collective-permute-start | bytes 786440 | tf_op jit(solution)/shard_map/while/body/eval_jaxpr/ppermute | solution.py:11
  86.8 14.1 %collective-permute-start.3 = (bf16[64,2048]{1,0:T(8,128)(2,1)S(1)}, bf16[64,2048]{1,0:T(8,128)(2,1)}, u32[]{:S(2)}, u32[]{:S(2)}) collective-permute-start(bf16[64,2048]{1,0:T(8,128)(2,1)S(1)} %get-tuple-element.1062), channel_id=1, source_target_pairs={{0,24},{8,0},{16,8},{24,16},{1,25},{9,1},{17,9},{25,17},{2,26},{10... | collective-permute-start | bytes 786440 | tf_op jit(solution)/shard_map/while/body/eval_jaxpr/ppermute | solution.py:11
  105.6 7.0 %collective-permute-start.1 = (bf16[2,64,2048]{2,1,0:T(8,128)(2,1)}, bf16[2,64,2048]{2,1,0:T(8,128)(2,1)}, u32[]{:S(2)}, u32[]{:S(2)}) collective-permute-start(bf16[2,64,2048]{2,1,0:T(8,128)(2,1)} %collective-permute-done), channel_id=1, source_target_pairs={{0,7},{1,0},{2,1},{3,2},{4,3},{5,4},{6,5},{7,6},{8,15},{9,8},{10,9... | collective-permute-start | bytes 1572872 | tf_op jit(solution)/shard_map/while/body/eval_jaxpr/ppermute | solution.py:11
  108.3 4.3 %copy-start.1 = (f32[2,64,32,64]{1,3,2,0:T(8,128)}, f32[2,64,32,64]{1,3,2,0:T(8,128)S(1)}, u32[]{:S(2)}) copy-start(f32[2,64,32,64]{1,3,2,0:T(8,128)S(1)} %bitcast_add_fusion.6) | copy-start | bytes 3145732 | tf_op jit(solution)/shard_map/while
  112.6 22.9 %collective-permute-start = (bf16[2,64,2048]{2,1,0:T(8,128)(2,1)}, bf16[2,64,2048]{2,1,0:T(8,128)(2,1)}, u32[]{:S(2)}, u32[]{:S(2)}) collective-permute-start(bf16[2,64,2048]{2,1,0:T(8,128)(2,1)} %get-tuple-element.1120), channel_id=1, source_target_pairs={{0,7},{1,0},{2,1},{3,2},{4,3},{5,4},{6,5},{7,6},{8,15},{9,8},{10,9... | collective-permute-start | bytes 1572872 | tf_op jit(solution)/shard_map/while/body/eval_jaxpr/ppermute | solution.py:11
  118.1 15.4 %collective-permute-start.2 = (bf16[64,2048]{1,0:T(8,128)(2,1)}, bf16[64,2048]{1,0:T(8,128)(2,1)}, u32[]{:S(2)}, u32[]{:S(2)}) collective-permute-start(bf16[64,2048]{1,0:T(8,128)(2,1)} %get-tuple-element.1061), channel_id=1, source_target_pairs={{0,24},{8,0},{16,8},{24,16},{1,25},{9,1},{17,9},{25,17},{2,26},{10... | collective-permute-start | bytes 786440 | tf_op jit(solution)/shard_map/while/body/eval_jaxpr/ppermute | solution.py:11
  120.1 13.5 %collective-permute-start.3 = (bf16[64,2048]{1,0:T(8,128)(2,1)S(1)}, bf16[64,2048]{1,0:T(8,128)(2,1)}, u32[]{:S(2)}, u32[]{:S(2)}) collective-permute-start(bf16[64,2048]{1,0:T(8,128)(2,1)S(1)} %get-tuple-element.1062), channel_id=1, source_target_pairs={{0,24},{8,0},{16,8},{24,16},{1,25},{9,1},{17,9},{25,17},{2,26},{10... | collective-permute-start | bytes 786440 | tf_op jit(solution)/shard_map/while/body/eval_jaxpr/ppermute | solution.py:11
  138.2 7.0 %collective-permute-start.1 = (bf16[2,64,2048]{2,1,0:T(8,128)(2,1)}, bf16[2,64,2048]{2,1,0:T(8,128)(2,1)}, u32[]{:S(2)}, u32[]{:S(2)}) collective-permute-start(bf16[2,64,2048]{2,1,0:T(8,128)(2,1)} %collective-permute-done), channel_id=1, source_target_pairs={{0,7},{1,0},{2,1},{3,2},{4,3},{5,4},{6,5},{7,6},{8,15},{9,8},{10,9... | collective-permute-start | bytes 1572872 | tf_op jit(solution)/shard_map/while/body/eval_jaxpr/ppermute | solution.py:11
  141.0 4.3 %copy-start.1 = (f32[2,64,32,64]{1,3,2,0:T(8,128)}, f32[2,64,32,64]{1,3,2,0:T(8,128)S(1)}, u32[]{:S(2)}) copy-start(f32[2,64,32,64]{1,3,2,0:T(8,128)S(1)} %bitcast_add_fusion.6) | copy-start | bytes 3145732 | tf_op jit(solution)/shard_map/while
  145.3 23.4 %collective-permute-start = (bf16[2,64,2048]{2,1,0:T(8,128)(2,1)}, bf16[2,64,2048]{2,1,0:T(8,128)(2,1)}, u32[]{:S(2)}, u32[]{:S(2)}) collective-permute-start(bf16[2,64,2048]{2,1,0:T(8,128)(2,1)} %get-tuple-element.1120), channel_id=1, source_target_pairs={{0,7},{1,0},{2,1},{3,2},{4,3},{5,4},{6,5},{7,6},{8,15},{9,8},{10,9... | collective-permute-start | bytes 1572872 | tf_op jit(solution)/shard_map/while/body/eval_jaxpr/ppermute | solution.py:11
  150.8 15.9 %collective-permute-start.2 = (bf16[64,2048]{1,0:T(8,128)(2,1)}, bf16[64,2048]{1,0:T(8,128)(2,1)}, u32[]{:S(2)}, u32[]{:S(2)}) collective-permute-start(bf16[64,2048]{1,0:T(8,128)(2,1)} %get-tuple-element.1061), channel_id=1, source_target_pairs={{0,24},{8,0},{16,8},{24,16},{1,25},{9,1},{17,9},{25,17},{2,26},{10... | collective-permute-start | bytes 786440 | tf_op jit(solution)/shard_map/while/body/eval_jaxpr/ppermute | solution.py:11
  152.7 14.1 %collective-permute-start.3 = (bf16[64,2048]{1,0:T(8,128)(2,1)S(1)}, bf16[64,2048]{1,0:T(8,128)(2,1)}, u32[]{:S(2)}, u32[]{:S(2)}) collective-permute-start(bf16[64,2048]{1,0:T(8,128)(2,1)S(1)} %get-tuple-element.1062), channel_id=1, source_target_pairs={{0,24},{8,0},{16,8},{24,16},{1,25},{9,1},{17,9},{25,17},{2,26},{10... | collective-permute-start | bytes 786440 | tf_op jit(solution)/shard_map/while/body/eval_jaxpr/ppermute | solution.py:11
  171.4 7.0 %collective-permute-start.1 = (bf16[2,64,2048]{2,1,0:T(8,128)(2,1)}, bf16[2,64,2048]{2,1,0:T(8,128)(2,1)}, u32[]{:S(2)}, u32[]{:S(2)}) collective-permute-start(bf16[2,64,2048]{2,1,0:T(8,128)(2,1)} %collective-permute-done), channel_id=1, source_target_pairs={{0,7},{1,0},{2,1},{3,2},{4,3},{5,4},{6,5},{7,6},{8,15},{9,8},{10,9... | collective-permute-start | bytes 1572872 | tf_op jit(solution)/shard_map/while/body/eval_jaxpr/ppermute | solution.py:11
  180.6 39.1 %copy-start.4 = (bf16[2,64,2048]{2,1,0:T(8,128)(2,1)}, bf16[2,64,2048]{2,1,0:T(8,128)(2,1)S(1)}, u32[]{:S(2)}) copy-start(bf16[2,64,2048]{2,1,0:T(8,128)(2,1)S(1)} %copy.31) | copy-start | bytes 1572868
  180.6 12.2 %collective-permute-start.13 = (bf16[2,64,2048]{2,1,0:T(8,128)(2,1)S(1)}, bf16[2,64,2048]{2,1,0:T(8,128)(2,1)S(1)}, u32[]{:S(2)}, u32[]{:S(2)}) collective-permute-start(bf16[2,64,2048]{2,1,0:T(8,128)(2,1)S(1)} %copy.31), channel_id=1, source_target_pairs={{0,6},{1,7},{2,0},{3,1},{4,2},{5,3},{6,4},{7,5},{8,14},{9,15},{10,... | collective-permute-start | bytes 1572872 | tf_op jit(solution)/shard_map/ppermute | solution.py:11
  192.9 26.0 %collective-permute-start.14 = (bf16[2,64,2048]{2,1,0:T(8,128)(2,1)S(1)}, bf16[2,64,2048]{2,1,0:T(8,128)(2,1)S(1)}, u32[]{:S(2)}, u32[]{:S(2)}) collective-permute-start(bf16[2,64,2048]{2,1,0:T(8,128)(2,1)S(1)} %broadcast_select_fusion.2), channel_id=1, source_target_pairs={{0,4},{1,5},{2,6},{3,7},{4,0},{5,1},{6,2},{7,3},{8,12},{9,13},{10,... | collective-permute-start | bytes 1572872 | tf_op jit(solution)/shard_map/ppermute | solution.py:11
  219.7 20.5 %collective-permute-start.4 = (bf16[2,64,2048]{2,1,0:T(8,128)(2,1)}, bf16[2,64,2048]{2,1,0:T(8,128)(2,1)}, u32[]{:S(2)}, u32[]{:S(2)}) collective-permute-start(bf16[2,64,2048]{2,1,0:T(8,128)(2,1)} %get-tuple-element.1172), channel_id=1, source_target_pairs={{0,7},{1,0},{2,1},{3,2},{4,3},{5,4},{6,5},{7,6},{8,15},{9,8},{10,9... | collective-permute-start | bytes 1572872 | tf_op jit(solution)/shard_map/while/body/eval_jaxpr/ppermute | solution.py:11
  222.9 15.4 %collective-permute-start.6 = (bf16[64,2048]{1,0:T(8,128)(2,1)}, bf16[64,2048]{1,0:T(8,128)(2,1)}, u32[]{:S(2)}, u32[]{:S(2)}) collective-permute-start(bf16[64,2048]{1,0:T(8,128)(2,1)} %get-tuple-element.1088), channel_id=1, source_target_pairs={{0,24},{8,0},{16,8},{24,16},{1,25},{9,1},{17,9},{25,17},{2,26},{10... | collective-permute-start | bytes 786440 | tf_op jit(solution)/shard_map/while/body/eval_jaxpr/ppermute | solution.py:11
  224.8 13.5 %collective-permute-start.7 = (bf16[64,2048]{1,0:T(8,128)(2,1)S(1)}, bf16[64,2048]{1,0:T(8,128)(2,1)}, u32[]{:S(2)}, u32[]{:S(2)}) collective-permute-start(bf16[64,2048]{1,0:T(8,128)(2,1)S(1)} %get-tuple-element.1089), channel_id=1, source_target_pairs={{0,24},{8,0},{16,8},{24,16},{1,25},{9,1},{17,9},{25,17},{2,26},{10... | collective-permute-start | bytes 786440 | tf_op jit(solution)/shard_map/while/body/eval_jaxpr/ppermute | solution.py:11
  243.0 7.0 %collective-permute-start.5 = (bf16[2,64,2048]{2,1,0:T(8,128)(2,1)}, bf16[2,64,2048]{2,1,0:T(8,128)(2,1)}, u32[]{:S(2)}, u32[]{:S(2)}) collective-permute-start(bf16[2,64,2048]{2,1,0:T(8,128)(2,1)} %collective-permute-done.4), channel_id=1, source_target_pairs={{0,7},{1,0},{2,1},{3,2},{4,3},{5,4},{6,5},{7,6},{8,15},{9,8},{10,9... | collective-permute-start | bytes 1572872 | tf_op jit(solution)/shard_map/while/body/eval_jaxpr/ppermute | solution.py:11
  250.0 23.4 %collective-permute-start.4 = (bf16[2,64,2048]{2,1,0:T(8,128)(2,1)}, bf16[2,64,2048]{2,1,0:T(8,128)(2,1)}, u32[]{:S(2)}, u32[]{:S(2)}) collective-permute-start(bf16[2,64,2048]{2,1,0:T(8,128)(2,1)} %get-tuple-element.1172), channel_id=1, source_target_pairs={{0,7},{1,0},{2,1},{3,2},{4,3},{5,4},{6,5},{7,6},{8,15},{9,8},{10,9... | collective-permute-start | bytes 1572872 | tf_op jit(solution)/shard_map/while/body/eval_jaxpr/ppermute | solution.py:11
  255.6 15.9 %collective-permute-start.6 = (bf16[64,2048]{1,0:T(8,128)(2,1)}, bf16[64,2048]{1,0:T(8,128)(2,1)}, u32[]{:S(2)}, u32[]{:S(2)}) collective-permute-start(bf16[64,2048]{1,0:T(8,128)(2,1)} %get-tuple-element.1088), channel_id=1, source_target_pairs={{0,24},{8,0},{16,8},{24,16},{1,25},{9,1},{17,9},{25,17},{2,26},{10... | collective-permute-start | bytes 786440 | tf_op jit(solution)/shard_map/while/body/eval_jaxpr/ppermute | solution.py:11
  257.4 14.1 %collective-permute-start.7 = (bf16[64,2048]{1,0:T(8,128)(2,1)S(1)}, bf16[64,2048]{1,0:T(8,128)(2,1)}, u32[]{:S(2)}, u32[]{:S(2)}) collective-permute-start(bf16[64,2048]{1,0:T(8,128)(2,1)S(1)} %get-tuple-element.1089), channel_id=1, source_target_pairs={{0,24},{8,0},{16,8},{24,16},{1,25},{9,1},{17,9},{25,17},{2,26},{10... | collective-permute-start | bytes 786440 | tf_op jit(solution)/shard_map/while/body/eval_jaxpr/ppermute | solution.py:11
  276.2 7.0 %collective-permute-start.5 = (bf16[2,64,2048]{2,1,0:T(8,128)(2,1)}, bf16[2,64,2048]{2,1,0:T(8,128)(2,1)}, u32[]{:S(2)}, u32[]{:S(2)}) collective-permute-start(bf16[2,64,2048]{2,1,0:T(8,128)(2,1)} %collective-permute-done.4), channel_id=1, source_target_pairs={{0,7},{1,0},{2,1},{3,2},{4,3},{5,4},{6,5},{7,6},{8,15},{9,8},{10,9... | collective-permute-start | bytes 1572872 | tf_op jit(solution)/shard_map/while/body/eval_jaxpr/ppermute | solution.py:11
  278.9 4.3 %copy-start.3 = (f32[2,64,32,64]{1,3,2,0:T(8,128)}, f32[2,64,32,64]{1,3,2,0:T(8,128)S(1)}, u32[]{:S(2)}) copy-start(f32[2,64,32,64]{1,3,2,0:T(8,128)S(1)} %bitcast_add_fusion.7) | copy-start | bytes 3145732 | tf_op jit(solution)/shard_map/while
  283.2 22.9 %collective-permute-start.4 = (bf16[2,64,2048]{2,1,0:T(8,128)(2,1)}, bf16[2,64,2048]{2,1,0:T(8,128)(2,1)}, u32[]{:S(2)}, u32[]{:S(2)}) collective-permute-start(bf16[2,64,2048]{2,1,0:T(8,128)(2,1)} %get-tuple-element.1172), channel_id=1, source_target_pairs={{0,7},{1,0},{2,1},{3,2},{4,3},{5,4},{6,5},{7,6},{8,15},{9,8},{10,9... | collective-permute-start | bytes 1572872 | tf_op jit(solution)/shard_map/while/body/eval_jaxpr/ppermute | solution.py:11
  288.8 15.4 %collective-permute-start.6 = (bf16[64,2048]{1,0:T(8,128)(2,1)}, bf16[64,2048]{1,0:T(8,128)(2,1)}, u32[]{:S(2)}, u32[]{:S(2)}) collective-permute-start(bf16[64,2048]{1,0:T(8,128)(2,1)} %get-tuple-element.1088), channel_id=1, source_target_pairs={{0,24},{8,0},{16,8},{24,16},{1,25},{9,1},{17,9},{25,17},{2,26},{10... | collective-permute-start | bytes 786440 | tf_op jit(solution)/shard_map/while/body/eval_jaxpr/ppermute | solution.py:11
  290.8 13.5 %collective-permute-start.7 = (bf16[64,2048]{1,0:T(8,128)(2,1)S(1)}, bf16[64,2048]{1,0:T(8,128)(2,1)}, u32[]{:S(2)}, u32[]{:S(2)}) collective-permute-start(bf16[64,2048]{1,0:T(8,128)(2,1)S(1)} %get-tuple-element.1089), channel_id=1, source_target_pairs={{0,24},{8,0},{16,8},{24,16},{1,25},{9,1},{17,9},{25,17},{2,26},{10... | collective-permute-start | bytes 786440 | tf_op jit(solution)/shard_map/while/body/eval_jaxpr/ppermute | solution.py:11
  308.9 7.0 %collective-permute-start.5 = (bf16[2,64,2048]{2,1,0:T(8,128)(2,1)}, bf16[2,64,2048]{2,1,0:T(8,128)(2,1)}, u32[]{:S(2)}, u32[]{:S(2)}) collective-permute-start(bf16[2,64,2048]{2,1,0:T(8,128)(2,1)} %collective-permute-done.4), channel_id=1, source_target_pairs={{0,7},{1,0},{2,1},{3,2},{4,3},{5,4},{6,5},{7,6},{8,15},{9,8},{10,9... | collective-permute-start | bytes 1572872 | tf_op jit(solution)/shard_map/while/body/eval_jaxpr/ppermute | solution.py:11
  311.7 4.3 %copy-start.3 = (f32[2,64,32,64]{1,3,2,0:T(8,128)}, f32[2,64,32,64]{1,3,2,0:T(8,128)S(1)}, u32[]{:S(2)}) copy-start(f32[2,64,32,64]{1,3,2,0:T(8,128)S(1)} %bitcast_add_fusion.7) | copy-start | bytes 3145732 | tf_op jit(solution)/shard_map/while
  315.9 23.4 %collective-permute-start.4 = (bf16[2,64,2048]{2,1,0:T(8,128)(2,1)}, bf16[2,64,2048]{2,1,0:T(8,128)(2,1)}, u32[]{:S(2)}, u32[]{:S(2)}) collective-permute-start(bf16[2,64,2048]{2,1,0:T(8,128)(2,1)} %get-tuple-element.1172), channel_id=1, source_target_pairs={{0,7},{1,0},{2,1},{3,2},{4,3},{5,4},{6,5},{7,6},{8,15},{9,8},{10,9... | collective-permute-start | bytes 1572872 | tf_op jit(solution)/shard_map/while/body/eval_jaxpr/ppermute | solution.py:11
  321.5 15.9 %collective-permute-start.6 = (bf16[64,2048]{1,0:T(8,128)(2,1)}, bf16[64,2048]{1,0:T(8,128)(2,1)}, u32[]{:S(2)}, u32[]{:S(2)}) collective-permute-start(bf16[64,2048]{1,0:T(8,128)(2,1)} %get-tuple-element.1088), channel_id=1, source_target_pairs={{0,24},{8,0},{16,8},{24,16},{1,25},{9,1},{17,9},{25,17},{2,26},{10... | collective-permute-start | bytes 786440 | tf_op jit(solution)/shard_map/while/body/eval_jaxpr/ppermute | solution.py:11
  323.3 14.1 %collective-permute-start.7 = (bf16[64,2048]{1,0:T(8,128)(2,1)S(1)}, bf16[64,2048]{1,0:T(8,128)(2,1)}, u32[]{:S(2)}, u32[]{:S(2)}) collective-permute-start(bf16[64,2048]{1,0:T(8,128)(2,1)S(1)} %get-tuple-element.1089), channel_id=1, source_target_pairs={{0,24},{8,0},{16,8},{24,16},{1,25},{9,1},{17,9},{25,17},{2,26},{10... | collective-permute-start | bytes 786440 | tf_op jit(solution)/shard_map/while/body/eval_jaxpr/ppermute | solution.py:11
  342.1 7.0 %collective-permute-start.5 = (bf16[2,64,2048]{2,1,0:T(8,128)(2,1)}, bf16[2,64,2048]{2,1,0:T(8,128)(2,1)}, u32[]{:S(2)}, u32[]{:S(2)}) collective-permute-start(bf16[2,64,2048]{2,1,0:T(8,128)(2,1)} %collective-permute-done.4), channel_id=1, source_target_pairs={{0,7},{1,0},{2,1},{3,2},{4,3},{5,4},{6,5},{7,6},{8,15},{9,8},{10,9... | collective-permute-start | bytes 1572872 | tf_op jit(solution)/shard_map/while/body/eval_jaxpr/ppermute | solution.py:11
  (12 other events, 29.8 us)
where the time goes:
time: 356 us; the launch traced here: 355 us
  waiting for transfers between devices  102 us (29%)
  local copies, waits for them, and re-layouts  97.7 us (27%)
  starting transfers between devices  58.6 us (16%)
  matrix products  58.5 us (16%)
  other arithmetic  37.4 us (11%)
    ppermute x39, waiting for transfers between devices, shifted(): lax.ppermute(shard, axis, [(i, (i + by) % devices) for i in range(devices)])  102 us
    ppermute x39, starting transfers between devices, shifted(): lax.ppermute(shard, axis, [(i, (i + by) % devices) for i in range(devices)])  58.6 us
    reshape x16, local copies, waits for them, and re-layouts, apply_turn(): left_view = left_tile.reshape(2, blk, rh, blk)  38.7 us
    dot_general x16, matrix products, apply_turn(): jnp.einsum('hea,hxay->hxey', match_a.astype(jnp.bfloat16), left_view, pre...  26.4 us
    dot_general x16, local copies, waits for them, and re-layouts, apply_turn(): jnp.einsum('heb,xby->hxey', match_b.astype(jnp.bfloat16), right_view, pre...  25.7 us
    dot_general x16, matrix products, apply_turn(): jnp.einsum('hxey,hyez->hxez', picked_a, picked_b, preferred_element_type=...  24.4 us
    another operation x8, other arithmetic, round_body(): right_pair = jnp.stack([right_pair[1], shifted(right_pair[0], 'row', -1)])  15.1 us
    slice x8, local copies, waits for them, and re-layouts, round_body(): right_pair = jnp.stack([right_pair[1], shifted(right_pair[0], 'row', -1)])  14.9 us
  transfers between devices with their start and end apart: 39, of which 14 were waited for; matrix products, arithmetic and copies ran while one was open for 45% of the time, Pallas kernels for 0%

commit v1 on v0

v1 whole, which is shorter than its diff:
```python
import functools

import jax
import jax.numpy as jnp
from jax import lax
from jax.experimental import pallas as pl
from jax.experimental.pallas import tpu as pltpu
from jax.sharding import PartitionSpec as P

PANEL = 49
PIECES = 4

SMEM = pl.BlockSpec(memory_space=pltpu.SMEM)
VMEM = pl.BlockSpec(memory_space=pltpu.VMEM)
HBM = pl.BlockSpec(memory_space=pltpu.HBM)
PARAMS = pltpu.CompilerParams(vmem_limit_bytes=40 * 1024 * 1024)


class Plan:
    def __init__(self, n_row, n_col, blk):
        self.n_row, self.n_col, self.blk = n_row, n_col, blk
        self.ndev = n_row * n_col
        chips = self.ndev // 2
        self.full = min(self.ndev, PANEL)
        self.shared = min(chips, PANEL - self.full)
        self.extra = PANEL - self.full - self.shared
        self.half = blk // 2
        self.piece = blk // PIECES
        self.back_rows = blk + (self.half if self.shared else 0)
        self.rows = self.back_rows + self.piece * self.extra

    def starts(self, u, rows):
        first = u * rows
        step = self.half
        if self.shared:
            chip = u - self.full
            is_full, is_shared = u < self.full, u < self.full + self.shared
            tail = self.ndev * rows + (chip - self.shared) * self.blk
            first = jnp.where(is_full, first, jnp.where(is_shared, 2 * chip * rows + self.blk, tail))
            step = jnp.where(jnp.logical_and(is_shared, jnp.logical_not(is_full)), rows, self.half)
        return [pl.multiple_of(first + h * step, self.piece) for h in range(2)]


def residue(row, shift):
    u = row - shift
    return jnp.where(u < 0, u + PANEL, u)


def kept_lanes(rows, u, shift, blk):
    npan = rows.shape[0]
    target = u + shift
    target = jnp.where(target >= PANEL, target - PANEL, target)
    has = jnp.sum((rows == target).astype(jnp.float32), axis=1, keepdims=True)
    lane = lax.broadcasted_iota(jnp.int32, (npan, npan * blk), 1)
    tile = lax.broadcasted_iota(jnp.int32, (npan, npan * blk), 0)
    return jnp.sum(jnp.where(lane // blk == tile, has, 0.0), axis=0, keepdims=True)


def pack_kernel(plan, x_hbm, rows_hbm, kept_hbm, shift_hbm, out_ref, keep_ref, x_ref, rows_ref, kept_ref, shift_ref, stage, sems):
    row_id, col_id = lax.axis_index("row"), lax.axis_index("col")
    blk, half, piece, ndev = plan.blk, plan.half, plan.piece, plan.ndev
    npan = 2 * plan.n_row
    own = pl.ds(2 * row_id, 2)
    copies = [
        pltpu.make_async_copy(shift_hbm, shift_ref, sems.at[0]),
        pltpu.make_async_copy(rows_hbm.at[own], rows_ref, sems.at[1]),
        pltpu.make_async_copy(x_hbm, x_ref, sems.at[2]),
        pltpu.make_async_copy(kept_hbm, kept_ref, sems.at[3]),
    ]
    for copy in copies:
        copy.start()
    stage[...] = jnp.zeros_like(stage)
    for copy in copies:
        copy.wait()
    for p in range(2):
        shift = shift_ref[2 * row_id + p]
        lanes = slice(p * blk, (p + 1) * blk)
        for e in range(rows_ref.shape[2]):
            u = residue(rows_ref[p, col_id, e], shift)
            block = x_ref[p, :, e * blk : (e + 1) * blk]
            for h, start in enumerate(plan.starts(u, plan.rows)):
                stage[pl.ds(start, half), lanes] = block[h * half : (h + 1) * half]
    for d in range(ndev):
        at = slice(d * plan.rows, d * plan.rows + plan.back_rows)
        out_ref[d, : plan.back_rows] = stage[at]
        group = 2 * (d // plan.n_col % 2) + d % 2
        for k in range(plan.extra):
            start = ndev * plan.rows + k * blk + group * piece
            to = plan.back_rows + k * piece
            out_ref[d, to : to + piece] = stage[start : start + piece]
    me = row_id * plan.n_col + col_id
    sets = [jnp.minimum(me, plan.full - 1), plan.full + me // 2]
    for k, u in enumerate(sets[: keep_ref.shape[0]]):
        for panel in range(npan):
            keep_ref[k, panel : panel + 1] = kept_lanes(kept_ref[panel], u, shift_ref[panel], blk)


def split_pair(low, high):
    blk = low.shape[1] // 2
    first = jnp.concatenate([low[:, :blk], high[:, :blk]], axis=1)
    second = jnp.concatenate([low[:, blk:], high[:, blk:]], axis=1)
    return first, second


def dot(a, b):
    return jnp.dot(a, b, preferred_element_type=jnp.float32)


def purify(s, m):
    return 3.0 * s.astype(jnp.float32) - 2.0 * dot(s, m)


def full_kernel(plan, keep_ref, y_ref, out_ref, m_ref, s_ref):
    blk, n_col = plan.blk, plan.n_col
    for r in range(plan.n_row):
        for j in range(n_col // 2):
            src = r * n_col + 2 * j
            first, second = split_pair(y_ref[src, :blk], y_ref[src + 1, :blk])
            lanes = slice(2 * j * blk, (2 * j + 2) * blk)
            m_ref[2 * r * blk : (2 * r + 1) * blk, lanes] = first
            m_ref[(2 * r + 1) * blk : (2 * r + 2) * blk, lanes] = second
    m = m_ref[...]
    for panel in range(2 * plan.n_row):
        at = slice(panel * blk, (panel + 1) * blk)
        s = dot(m_ref[at], m)
        s_ref[at] = jnp.where(keep_ref[0, panel : panel + 1] > 0, s, 0.0).astype(jnp.bfloat16)
    for r in range(plan.n_row):
        res = purify(s_ref[2 * r * blk : (2 * r + 2) * blk], m).astype(jnp.bfloat16)
        for j in range(n_col // 2):
            lanes = slice(2 * j * blk, (2 * j + 2) * blk)
            first, second = split_pair(res[:blk, lanes], res[blk:, lanes])
            out_ref[r * n_col + 2 * j, :blk] = first
            out_ref[r * n_col + 2 * j + 1, :blk] = second


def shared_kernel(plan, keep_ref, own_ref, far_ref, part_ref, out_ref, *refs):
    *extra_refs, m_ref, s_ref, o_ref = refs
    blk, half, piece, n_col = plan.blk, plan.half, plan.piece, plan.n_col
    first_core = lax.axis_index("col") % 2 == 0
    out_ref[:, :blk] = part_ref[:, :blk]
    for r in range(plan.n_row):
        for j in range(n_col // 2):
            src = r * n_col + 2 * j
            lanes = slice(2 * j * blk, (2 * j + 2) * blk)
            own = split_pair(own_ref[src, :half], own_ref[src + 1, :half])
            far = split_pair(far_ref[src, :half], far_ref[src + 1, :half])
            for p in range(2):
                at = (2 * r + p) * blk
                m_ref[at : at + half, lanes] = jnp.where(first_core, own[p], far[p])
                m_ref[at + half : at + blk, lanes] = jnp.where(first_core, far[p], own[p])
                o_ref[(2 * r + p) * half : (2 * r + p + 1) * half, lanes] = own[p]
    for k in range(plan.extra):
        at = slice(half + k * piece, half + (k + 1) * piece)
        own, far = own_ref[:, at], far_ref[:, at]
        extra_refs[0][:, 2 * k * piece : (2 * k + 1) * piece] = jnp.where(first_core, own, far)
        extra_refs[0][:, (2 * k + 1) * piece : (2 * k + 2) * piece] = jnp.where(first_core, far, own)
    m = m_ref[...]
    for panel in range(2 * plan.n_row):
        at = slice(panel * half, (panel + 1) * half)
        s = dot(o_ref[at], m)
        s_ref[at] = jnp.where(keep_ref[1, panel : panel + 1] > 0, s, 0.0).astype(jnp.bfloat16)
    for r in range(plan.n_row):
        res = purify(s_ref[2 * r * half : (2 * r + 2) * half], m).astype(jnp.bfloat16)
        for j in range(n_col // 2):
            lanes = slice(2 * j * blk, (2 * j + 2) * blk)
            first, second = split_pair(res[:half, lanes], res[half:, lanes])
            out_ref[r * n_col + 2 * j, blk:] = first
            out_ref[r * n_col + 2 * j + 1, blk:] = second


def extra_block(plan, k, near_ref, far_ref, kept_ref, shift_ref, m_ref, s_ref):
    row_id, col_id = lax.axis_index("row"), lax.axis_index("col")
    blk, n_col = plan.blk, plan.n_col
    even = row_id % 2 == 0
    at = slice(2 * k * plan.piece, (2 * k + 2) * plan.piece)

    def whole(src):
        near, far = near_ref[src, at], far_ref[src, at]
        return jnp.concatenate([jnp.where(even, near, far), jnp.where(even, far, near)], axis=0)

    for r in range(plan.n_row):
        for j in range(n_col // 2):
            lanes = slice(2 * j * blk, (2 * j + 2) * blk)
            pair = split_pair(whole(r * n_col + 2 * j), whole(r * n_col + 2 * j + 1))
            for p in range(2):
                m_ref[(2 * r + p) * blk : (2 * r + p + 1) * blk, lanes] = pair[p]
    for j in range(n_col // 2):
        lanes = slice(2 * j * blk, (2 * j + 2) * blk)
        src = row_id * n_col + 2 * j
        pair = split_pair(whole(src), whole(src + 1))
        for p in range(2):
            s_ref[p * blk : (p + 1) * blk, lanes] = pair[p]
    m = m_ref[...]
    s = dot(s_ref[...], m)
    kept = []
    for p in range(2):
        panel = 2 * row_id + p
        keep = kept_lanes(kept_ref[panel], plan.full + plan.shared + k, shift_ref[panel], blk)
        kept.append(jnp.where(keep > 0, s[p * blk : (p + 1) * blk], 0.0).astype(jnp.bfloat16))
    res = purify(jnp.concatenate(kept, axis=0), m)
    mine = res[:, : 2 * blk]
    for j in range(1, n_col // 2):
        mine = jnp.where(col_id // 2 == j, res[:, 2 * j * blk : (2 * j + 2) * blk], mine)
    first, second = split_pair(mine[:blk], mine[blk:])
    return jnp.where(col_id % 2 == 0, first, second)


def unpack_kernel(plan, kept_hbm, shift_hbm, ret_ref, *refs):
    *halves, out_ref, kept_ref, rows_ref, shift_ref, stage, m_ref, s_ref, sems = refs
    row_id, col_id = lax.axis_index("row"), lax.axis_index("col")
    blk, half, rows = plan.blk, plan.half, plan.back_rows
    copies = [
        pltpu.make_async_copy(shift_hbm, shift_ref, sems.at[0]),
        pltpu.make_async_copy(kept_hbm.at[pl.ds(2 * row_id, 2)], rows_ref, sems.at[1]),
        pltpu.make_async_copy(kept_hbm, kept_ref, sems.at[2]),
    ]
    for copy in copies:
        copy.start()
    for d in range(plan.ndev):
        stage[d * rows : (d + 1) * rows] = ret_ref[d]
    for copy in copies:
        copy.wait()
    for k in range(plan.extra):
        block = extra_block(plan, k, *halves, kept_ref, shift_ref, m_ref, s_ref)
        start = plan.ndev * rows + k * blk
        stage[start : start + blk] = block.astype(jnp.bfloat16)
    for p in range(2):
        shift = shift_ref[2 * row_id + p]
        lanes = slice(p * blk, (p + 1) * blk)
        for e in range(rows_ref.shape[2]):
            u = residue(rows_ref[p, col_id, e], shift)
            for h, start in enumerate(plan.starts(u, rows)):
                tile = stage[pl.ds(start, half), :]
                out_ref[p, h * half : (h + 1) * half, e * blk : (e + 1) * blk] = tile[:, lanes].astype(jnp.float32)


def body(density, density_rows, square_rows, panel_shift):
    both = ("row", "col")
    n_row, n_col = lax.axis_size("row"), lax.axis_size("col")
    blk, rh = density.shape[1], density_rows.shape[2]
    npan = density_rows.shape[0]
    plan = Plan(n_row, n_col, blk)
    ndev, rows, back = plan.ndev, plan.rows, plan.back_rows
    bf16 = jnp.bfloat16
    size = n_col * blk
    square = pltpu.VMEM((size, size), bf16)
    tables = [pltpu.VMEM(square_rows.shape, jnp.int32), pltpu.SMEM((2, npan, rh), jnp.int32), pltpu.SMEM((npan,), jnp.int32)]

    packed, keep = pl.pallas_call(
        functools.partial(pack_kernel, plan),
        out_shape=[
            jax.ShapeDtypeStruct((ndev, rows, 2 * blk), bf16),
            jax.ShapeDtypeStruct((2 if plan.shared else 1, npan, size), jnp.float32),
        ],
        in_specs=[HBM] * 4,
        out_specs=[VMEM] * 2,
        scratch_shapes=[
            pltpu.VMEM(density.shape, bf16),
            tables[1],
            tables[0],
            tables[2],
            pltpu.VMEM((ndev * rows + plan.extra * blk, 2 * blk), bf16),
            pltpu.SemaphoreType.DMA((4,)),
        ],
        compiler_params=PARAMS,
        name="pack",
    )(density, density_rows, square_rows, panel_shift)
    y = lax.all_to_all(packed, both, 0, 0, tiled=True)
    back_shape = jax.ShapeDtypeStruct((ndev, back, 2 * blk), bf16)
    if plan.shared:
        own = y[:, blk:]
        far = lax.ppermute(own, "col", [(i, i ^ 1) for i in range(n_col)])
    out = pl.pallas_call(
        functools.partial(full_kernel, plan),
        out_shape=back_shape,
        in_specs=[VMEM] * 2,
        out_specs=VMEM,
        scratch_shapes=[square] * 2,
        compiler_params=PARAMS,
        cost_estimate=pl.CostEstimate(flops=4 * size**3, bytes_accessed=4 * ndev * rows * 2 * blk, transcendentals=0),
        name="full",
    )(keep, y)
    halves = []
    if plan.shared:
        shapes = [back_shape]
        if plan.extra:
            shapes.append(jax.ShapeDtypeStruct((ndev, 2 * plan.piece * plan.extra, 2 * blk), bf16))
        out, *halves = pl.pallas_call(
            functools.partial(shared_kernel, plan),
            out_shape=shapes,
            in_specs=[VMEM] * 4,
            out_specs=[VMEM] * len(shapes),
            scratch_shapes=[square] + [pltpu.VMEM((size // 2, size), bf16)] * 2,
            compiler_params=PARAMS,
            name="shared",
        )(keep, own, far, out)
    if halves:
        halves.append(lax.ppermute(halves[0], "row", [(i, i ^ 1) for i in range(n_row)]))
    ret = lax.all_to_all(out, both, 0, 0, tiled=True)
    return pl.pallas_call(
        functools.partial(unpack_kernel, plan),
        out_shape=jax.ShapeDtypeStruct(density.shape, jnp.float32),
        in_specs=[HBM] * 2 + [VMEM] * (1 + len(halves)),
        out_specs=VMEM,
        scratch_shapes=tables
        + [
            pltpu.VMEM((ndev * back + plan.extra * blk, 2 * blk), bf16),
            square,
            pltpu.VMEM((2 * blk, size), bf16),
            pltpu.SemaphoreType.DMA((3,)),
        ],
        compiler_params=PARAMS,
        name="unpack",
    )(square_rows, panel_shift, ret, *halves)


def solution(mesh):
    placed = (P("row", None, "col"), P(), P(), P())
    return jax.shard_map(
        body, mesh=mesh, in_specs=placed, out_specs=P("row", None, "col"), check_vma=False
    )
```

time: 356 us -> 68.6 us (0.19)
  local copies, waits for them, and re-layouts: 97.7 us -> 3.25 us
  waiting for transfers between devices: 102 us -> 20.5 us
  matrix products: 58.5 us -> 0 us
  starting transfers between devices: 58.6 us -> 4.53 us
  other arithmetic: 37.4 us -> 0 us
  blocking collectives: 0 us -> 31.9 us
  Pallas kernels: 0 us -> 7.89 us
    ppermute x39 -> x2, waiting for transfers between devices: 102 us -> 13.2 us  [the longest x1 13 us: body(): lax.ppermute(halves[0], 'row', [(i, i ^ 1) for i in range(n_row)])]
    dot_general x48 -> x0, matrix products: 58.5 us -> none  [the longest x16 26.4 us: apply_turn(): jnp.einsum('hea,hxay->hxey', match_a.astype(jnp.bfloat16), left_view, pre...]
    ppermute x39 -> x2, starting transfers between devices: 58.6 us -> 1.77 us  [the longest x1 1.7 us: body(): lax.ppermute(halves[0], 'row', [(i, i ^ 1) for i in range(n_row)])]
    reshape x18 -> x0, local copies, waits for them, and re-layouts: 39 us -> none  [the longest x16 38.7 us: apply_turn(): left_view = left_tile.reshape(2, blk, rh, blk)]
    all_to_all x0 -> x1, blocking collectives: none -> 31.9 us  [body(): y = lax.all_to_all(packed, both, 0, 0, tiled=True)]
    dot_general x16 -> x0, local copies, waits for them, and re-layouts: 25.7 us -> none  [apply_turn(): jnp.einsum('heb,xby->hxey', match_b.astype(jnp.bfloat16), right_view, pre...]
    slice x9 -> x1, local copies, waits for them, and re-layouts: 16 us -> 0.03 us  [body(): own = y[:, blk:]]
    another operation x8 -> x0, other arithmetic: 15.1 us -> none  [round_body(): right_pair = jnp.stack([right_pair[1], shifted(right_pair[0], 'row', -1)])]
  transfers between devices with their start and end apart: 39 -> 3, of which waited for: 14 -> 3; matrix products, arithmetic and copies ran while one was open for 45% -> 0% of each run, Pallas kernels for 0% -> 2%
where the time goes in v1:
time: 68.6 us; the launch traced here: 68.1 us
  blocking collectives  31.9 us (47%)
  waiting for transfers between devices  20.5 us (30%)
  Pallas kernels  7.89 us (12%)
  starting transfers between devices  4.53 us (7%)
  local copies, waits for them, and re-layouts  3.25 us (5%)
    all_to_all x1, blocking collectives, body(): y = lax.all_to_all(packed, both, 0, 0, tiled=True)  31.9 us
    ppermute x1, waiting for transfers between devices, body(): lax.ppermute(halves[0], 'row', [(i, i ^ 1) for i in range(n_row)])  13 us
    all_to_all x1, waiting for transfers between devices, body(): ret = lax.all_to_all(out, both, 0, 0, tiled=True)  7.3 us
    unnamed x12, local copies, waits for them, and re-layouts  3.22 us
    all_to_all x1, starting transfers between devices, body(): ret = lax.all_to_all(out, both, 0, 0, tiled=True)  2.76 us
    pallas_call x1, Pallas kernels, body(): pl.pallas_call(functools.partial(unpack_kernel, plan), out_shape=jax.Shap...  2.73 us
    pallas_call x1, Pallas kernels, body(): pl.pallas_call(functools.partial(shared_kernel, plan), out_shape=shapes,...  2.3 us
    ppermute x1, starting transfers between devices, body(): lax.ppermute(halves[0], 'row', [(i, i ^ 1) for i in range(n_row)])  1.7 us
  transfers between devices with their start and end apart: 3, of which 3 were waited for; matrix products, arithmetic and copies ran while one was open for 0% of the time, Pallas kernels for 2%

profile of v1, /device:TPU:0, one launch (start us, length us, event | category | flops | bytes accessed | tf_op | source)
XLA Modules:
  0.0 68.1 jit_solution(4265196129958603743)
XLA Ops:
  0.0 0.0 copy-start
  0.0 1.0 %copy-done = bf16[2,64,2048]{2,1,0:T(8,128)(2,1)S(1)} copy-done((bf16[2,64,2048]{2,1,0:T(8,128)(2,1)S(1)}, bf16[2,64,2048]{2,1,0:T(8,128)(2,1)}, u32[]{:S(2)}) %copy-start) | copy-done | bytes 524312
  1.0 0.0 copy-start.1
  1.0 0.8 %copy-done.1 = s32[8,8,32]{2,1,0:T(8,128)S(1)} copy-done((s32[8,8,32]{2,1,0:T(8,128)S(1)}, s32[8,8,32]{2,1,0:T(8,128)}, u32[]{:S(2)}) %copy-start.1) | copy-done | bytes 8216
  1.8 0.0 copy-start.3
  1.8 0.8 %copy-done.3 = s32[8,8,32]{2,1,0:T(8,128)S(1)} copy-done((s32[8,8,32]{2,1,0:T(8,128)S(1)}, s32[8,8,32]{2,1,0:T(8,128)}, u32[]{:S(2)}) %copy-start.3) | copy-done | bytes 8216
  2.6 0.0 copy-start.4
  2.6 0.7 copy-done.4
  3.2 1.4 %pack.1 = (bf16[32,112,128]{2,1,0:T(8,128)(2,1)S(1)}, f32[2,8,512]{2,1,0:T(8,128)S(1)}) custom-call(bf16[2,64,2048]{2,1,0:T(8,128)(2,1)S(1)} %copy-done, s32[8,8,32]{2,1,0:T(8,128)S(1)} %copy-done.3, s32[8,8,32]{2,1,0:T(8,128)S(1)} %copy-done.1, s32[8]{0:T(128)S(1)} %copy-done.4), custom_call_target="tpu_custom_call" | custom-call | tf_op jit(solution)/shard_map/pack/pallas_call | solution.py:249
  4.6 31.9 %all_to_all.10.y_ref = bf16[32,112,128]{2,1,0:T(8,128)(2,1)S(1)} all-to-all(bf16[32,112,128]{2,1,0:T(8,128)(2,1)S(1)} %get-tuple-element.10), channel_id=1, replica_groups=mesh['row'=4,'col'=8] {'row','col'}, dimensions={0} | all-to-all | bytes 1835008 | tf_op jit(solution)/shard_map/all_to_all | solution.py:268
  36.5 0.1 collective-permute-start
  36.6 1.4 %full.1.part_ref = bf16[32,96,128]{2,1,0:T(8,128)(2,1)S(1)} custom-call(f32[2,8,512]{2,1,0:T(8,128)S(1)} %get-tuple-element.9.keep_ref, bf16[32,112,128]{2,1,0:T(8,128)(2,1)S(1)} %all_to_all.10.y_ref), custom_call_target="tpu_custom_call" | custom-call | flops 536870912 | bytes 1835008 | tf_op jit(solution)/shard_map/full/pallas_call | solution.py:273
  38.1 0.3 collective-permute-done.far_ref
  38.3 2.3 %shared.1 = (bf16[32,96,128]{2,1,0:T(8,128)(2,1)}, bf16[32,32,128]{2,1,0:T(8,128)(2,1)S(1)}) custom-call(f32[2,8,512]{2,1,0:T(8,128)S(1)} %get-tuple-element.9.keep_ref, bf16[32,48,128]{2,1,0:T(8,128)(2,1)S(1)} %slice.4.own_ref, bf16[32,48,128]{2,1,0:T(8,128)(2,1)S(1)} %collective-permute-done.far_ref, bf16[32,96,128]{2,1,0:T(8,128)(2,1)S(1)} %full.1.part_ref), custom_call_target="tpu_custom_call" | custom-call | tf_op jit(solution)/shard_map/shared/pallas_call | solution.py:288
  40.6 0.0 copy-start.2
  40.6 2.8 %all-to-all-start.1 = ((bf16[32,96,128]{2,1,0:T(8,128)(2,1)}), bf16[32,96,128]{2,1,0:T(8,128)(2,1)S(1)}, u32[]{:S(2)}, u32[]{:S(2)}) async-start(bf16[32,96,128]{2,1,0:T(8,128)(2,1)} %get-tuple-element.11), calls=%async_computation.1 | async-start | bytes 1572864 | tf_op jit(solution)/shard_map/all_to_all | solution.py:299
  43.4 0.0 copy-start.5
  43.4 1.7 %collective-permute-start.1 = (bf16[32,32,128]{2,1,0:T(8,128)(2,1)S(1)}, bf16[32,32,128]{2,1,0:T(8,128)(2,1)S(1)}, u32[]{:S(2)}, u32[]{:S(2)}) collective-permute-start(bf16[32,32,128]{2,1,0:T(8,128)(2,1)S(1)} %get-tuple-element.12.refs_0_), channel_id=1, source_target_pairs={{0,8},{8,0},{16,24},{24,16},{1,9},{9,1},{17,25},{25,17},{2,10},{10... | collective-permute-start | bytes 786440 | tf_op jit(solution)/shard_map/ppermute | solution.py:298
  45.1 13.0 %collective-permute-done.1.refs_1_ = bf16[32,32,128]{2,1,0:T(8,128)(2,1)S(1)} collective-permute-done((bf16[32,32,128]{2,1,0:T(8,128)(2,1)S(1)}, bf16[32,32,128]{2,1,0:T(8,128)(2,1)S(1)}, u32[]{:S(2)}, u32[]{:S(2)}) %collective-permute-start.1) | collective-permute-done | bytes 262176 | tf_op jit(solution)/shard_map/ppermute | solution.py:298
  58.1 7.3 %all-to-all-done.1.ret_ref = bf16[32,96,128]{2,1,0:T(8,128)(2,1)S(1)} async-done(((bf16[32,96,128]{2,1,0:T(8,128)(2,1)}), bf16[32,96,128]{2,1,0:T(8,128)(2,1)S(1)}, u32[]{:S(2)}, u32[]{:S(2)}) %all-to-all-start.1) | async-done | bytes 786464 | tf_op jit(solution)/shard_map/all_to_all | solution.py:299
  65.4 0.0 copy-done.2
  65.4 0.0 copy-done.5
  65.4 2.7 %unpack.1 = f32[2,64,2048]{2,1,0:T(8,128)} custom-call(s32[8,8,32]{2,1,0:T(8,128)S(1)} %copy-done.2, s32[8]{0:T(128)S(1)} %copy-done.5, bf16[32,96,128]{2,1,0:T(8,128)(2,1)S(1)} %all-to-all-done.1.ret_ref, bf16[32,32,128]{2,1,0:T(8,128)(2,1)S(1)} %get-tuple-element.12.refs_0_, bf16[32,32,128]{2,1,0:T(8,128)(2,1)S(1)} %collective-permute-done.1.refs_1_), custom_call_target="tpu_custom_call" | custom-call | tf_op jit(solution)/shard_map/unpack/pallas_call | solution.py:300
  (1 shorter events, 0.0 us)
Async XLA Ops:
  0.0 1.0 %copy-start = (bf16[2,64,2048]{2,1,0:T(8,128)(2,1)S(1)}, bf16[2,64,2048]{2,1,0:T(8,128)(2,1)}, u32[]{:S(2)}) copy-start(bf16[2,64,2048]{2,1,0:T(8,128)(2,1)} %x_hbm.1) | copy-start | bytes 1572868
  1.0 0.8 %copy-start.1 = (s32[8,8,32]{2,1,0:T(8,128)S(1)}, s32[8,8,32]{2,1,0:T(8,128)}, u32[]{:S(2)}) copy-start(s32[8,8,32]{2,1,0:T(8,128)} %kept_hbm.3) | copy-start | bytes 24580
  1.8 0.8 %copy-start.3 = (s32[8,8,32]{2,1,0:T(8,128)S(1)}, s32[8,8,32]{2,1,0:T(8,128)}, u32[]{:S(2)}) copy-start(s32[8,8,32]{2,1,0:T(8,128)} %rows_hbm.1) | copy-start | bytes 24580
  2.6 0.7 copy-start.4
  36.5 1.8 %collective-permute-start = (bf16[32,48,128]{2,1,0:T(8,128)(2,1)S(1)}, bf16[32,48,128]{2,1,0:T(8,128)(2,1)S(1)}, u32[]{:S(2)}, u32[]{:S(2)}) collective-permute-start(bf16[32,48,128]{2,1,0:T(8,128)(2,1)S(1)} %slice.4.own_ref), channel_id=1, source_target_pairs={{0,1},{1,0},{2,3},{3,2},{4,5},{5,4},{6,7},{7,6},{8,9},{9,8},{10,11... | collective-permute-start | bytes 1179656 | tf_op jit(solution)/shard_map/ppermute | solution.py:272
  40.6 24.7 %copy-start.2 = (s32[8,8,32]{2,1,0:T(8,128)S(1)}, s32[8,8,32]{2,1,0:T(8,128)}, u32[]{:S(2)}) copy-start(s32[8,8,32]{2,1,0:T(8,128)} %kept_hbm.3) | copy-start | bytes 24580
  40.6 24.7 %all-to-all-start.1 = ((bf16[32,96,128]{2,1,0:T(8,128)(2,1)}), bf16[32,96,128]{2,1,0:T(8,128)(2,1)S(1)}, u32[]{:S(2)}, u32[]{:S(2)}) async-start(bf16[32,96,128]{2,1,0:T(8,128)(2,1)} %get-tuple-element.11), calls=%async_computation.1 | async-start | bytes 1572864 | tf_op jit(solution)/shard_map/all_to_all | solution.py:299
  43.4 22.0 %copy-start.5 = (s32[8]{0:T(128)S(1)}, s32[8]{0:T(128)}, u32[]{:S(2)}) copy-start(s32[8]{0:T(128)} %shift_hbm.3) | copy-start | bytes 100
  43.4 14.7 %collective-permute-start.1 = (bf16[32,32,128]{2,1,0:T(8,128)(2,1)S(1)}, bf16[32,32,128]{2,1,0:T(8,128)(2,1)S(1)}, u32[]{:S(2)}, u32[]{:S(2)}) collective-permute-start(bf16[32,32,128]{2,1,0:T(8,128)(2,1)S(1)} %get-tuple-element.12.refs_0_), channel_id=1, source_target_pairs={{0,8},{8,0},{16,24},{24,16},{1,9},{9,1},{17,25},{25,17},{2,10},{10... | collective-permute-start | bytes 786440 | tf_op jit(solution)/shard_map/ppermute | solution.py:298

commit v2 on v1

v2 whole, which is shorter than its diff:
```python
import functools

import jax
import jax.numpy as jnp
from jax import lax
from jax.experimental import pallas as pl
from jax.experimental.pallas import tpu as pltpu
from jax.sharding import PartitionSpec as P

PANEL = 49

SMEM = pl.BlockSpec(memory_space=pltpu.SMEM)
VMEM = pl.BlockSpec(memory_space=pltpu.VMEM)
HBM = pl.BlockSpec(memory_space=pltpu.HBM)
PARAMS = pltpu.CompilerParams(vmem_limit_bytes=40 * 1024 * 1024)
PACK_PARAMS = pltpu.CompilerParams(vmem_limit_bytes=63 * 1024 * 1024)


class Plan:
    def __init__(self, n_row, n_col, blk):
        self.n_row, self.n_col, self.blk = n_row, n_col, blk
        self.ndev = n_row * n_col
        chips = self.ndev // 2
        self.full = min(self.ndev, PANEL)
        self.shared = min(chips, PANEL - self.full)
        self.extra = PANEL - self.full - self.shared
        self.half = blk // 2
        self.rows = blk + (self.half if self.shared else 0)

    def starts(self, u):
        rows = self.rows
        first = u * rows
        step = self.half
        if self.shared:
            chip = u - self.full
            is_full, is_shared = u < self.full, u < self.full + self.shared
            tail = self.ndev * rows + (chip - self.shared) * self.blk
            first = jnp.where(is_full, first, jnp.where(is_shared, 2 * chip * rows + self.blk, tail))
            step = jnp.where(jnp.logical_and(is_shared, jnp.logical_not(is_full)), rows, self.half)
        return [pl.multiple_of(first + h * step, self.half) for h in range(2)]

    def slot(self, apart):
        return apart % 2 * (self.n_col // 2) + apart // 2


def residue(row, shift):
    u = row - shift
    return jnp.where(u < 0, u + PANEL, u)


def kept_lanes(rows, u, shift, blk):
    npan = rows.shape[0]
    target = u + shift
    target = jnp.where(target >= PANEL, target - PANEL, target)
    has = jnp.sum((rows == target).astype(jnp.float32), axis=1, keepdims=True)
    lane = lax.broadcasted_iota(jnp.int32, (npan, npan * blk), 1)
    tile = lax.broadcasted_iota(jnp.int32, (npan, npan * blk), 0)
    return jnp.sum(jnp.where(lane // blk == tile, has, 0.0), axis=0, keepdims=True)


def pack_kernel(plan, x_hbm, rows_hbm, shift_hbm, out_ref, *refs):
    *extra_refs, x_ref, rows_ref, shift_ref, stage, sems = refs
    row_id, col_id = lax.axis_index("row"), lax.axis_index("col")
    blk, half, total = plan.blk, plan.half, plan.ndev * plan.rows
    copies = [
        pltpu.make_async_copy(shift_hbm, shift_ref, sems.at[0]),
        pltpu.make_async_copy(rows_hbm.at[pl.ds(2 * row_id, 2)], rows_ref, sems.at[1]),
        pltpu.make_async_copy(x_hbm.at[0], x_ref.at[0], sems.at[2]),
        pltpu.make_async_copy(x_hbm.at[1], x_ref.at[1], sems.at[3]),
    ]
    for copy in copies:
        copy.start()
    stage[...] = jnp.zeros_like(stage)
    for copy in copies[:2]:
        copy.wait()
    for p in range(2):
        copies[2 + p].wait()
        shift = shift_ref[2 * row_id + p]
        lanes = slice(p * blk, (p + 1) * blk)
        for e in range(rows_ref.shape[2]):
            u = residue(rows_ref[p, col_id, e], shift)
            block = x_ref[p, :, e * blk : (e + 1) * blk]
            for h, start in enumerate(plan.starts(u)):
                stage[pl.ds(start, half), lanes] = block[h * half : (h + 1) * half]
    copies = [pltpu.make_async_copy(stage.at[pl.ds(0, total)], out_ref, sems.at[0])]
    for ref in extra_refs:
        copies.append(pltpu.make_async_copy(stage.at[pl.ds(total, plan.extra * blk)], ref, sems.at[1]))
    for copy in copies:
        copy.start()
    for copy in copies:
        copy.wait()


def mask_kernel(plan, shift_ref, kept_ref, keep_ref):
    me = lax.axis_index("row") * plan.n_col + lax.axis_index("col")
    sets = [jnp.minimum(me, plan.full - 1), plan.full + me // 2]
    sets += [plan.full + plan.shared + k for k in range(plan.extra)]
    for k, u in enumerate(sets[: keep_ref.shape[0]]):
        for panel in range(2 * plan.n_row):
            keep_ref[k, panel : panel + 1] = kept_lanes(kept_ref[panel], u, shift_ref[panel], plan.blk)


def split_pair(low, high):
    blk = low.shape[1] // 2
    first = jnp.concatenate([low[:, :blk], high[:, :blk]], axis=1)
    second = jnp.concatenate([low[:, blk:], high[:, blk:]], axis=1)
    return first, second


def dot(a, b):
    return jnp.dot(a, b, preferred_element_type=jnp.float32)


def purify(s, m):
    return 3.0 * s.astype(jnp.float32) - 2.0 * dot(s, m)


def full_kernel(plan, keep_ref, y_ref, out_ref, m_ref, s_ref):
    blk, n_col = plan.blk, plan.n_col
    for r in range(plan.n_row):
        for j in range(n_col // 2):
            src = r * n_col + 2 * j
            first, second = split_pair(y_ref[src, :blk], y_ref[src + 1, :blk])
            lanes = slice(2 * j * blk, (2 * j + 2) * blk)
            m_ref[2 * r * blk : (2 * r + 1) * blk, lanes] = first
            m_ref[(2 * r + 1) * blk : (2 * r + 2) * blk, lanes] = second
    m = m_ref[...]
    for panel in range(2 * plan.n_row):
        at = slice(panel * blk, (panel + 1) * blk)
        s = dot(m_ref[at], m)
        s_ref[at] = jnp.where(keep_ref[0, panel : panel + 1] > 0, s, 0.0).astype(jnp.bfloat16)
    for r in range(plan.n_row):
        res = purify(s_ref[2 * r * blk : (2 * r + 2) * blk], m).astype(jnp.bfloat16)
        for j in range(n_col // 2):
            lanes = slice(2 * j * blk, (2 * j + 2) * blk)
            first, second = split_pair(res[:blk, lanes], res[blk:, lanes])
            out_ref[r * n_col + 2 * j, :blk] = first
            out_ref[r * n_col + 2 * j + 1, :blk] = second


def shared_kernel(plan, keep_ref, own_ref, far_ref, part_ref, out_ref, m_ref, s_ref, o_ref):
    blk, half, n_col = plan.blk, plan.half, plan.n_col
    first_core = lax.axis_index("col") % 2 == 0
    out_ref[:, :blk] = part_ref[:, :blk]
    for r in range(plan.n_row):
        for j in range(n_col // 2):
            src = r * n_col + 2 * j
            lanes = slice(2 * j * blk, (2 * j + 2) * blk)
            own = split_pair(own_ref[src], own_ref[src + 1])
            far = split_pair(far_ref[src], far_ref[src + 1])
            for p in range(2):
                at = (2 * r + p) * blk
                m_ref[at : at + half, lanes] = jnp.where(first_core, own[p], far[p])
                m_ref[at + half : at + blk, lanes] = jnp.where(first_core, far[p], own[p])
                o_ref[(2 * r + p) * half : (2 * r + p + 1) * half, lanes] = own[p]
    m = m_ref[...]
    for panel in range(2 * plan.n_row):
        at = slice(panel * half, (panel + 1) * half)
        s = dot(o_ref[at], m)
        s_ref[at] = jnp.where(keep_ref[1, panel : panel + 1] > 0, s, 0.0).astype(jnp.bfloat16)
    for r in range(plan.n_row):
        res = purify(s_ref[2 * r * half : (2 * r + 2) * half], m).astype(jnp.bfloat16)
        for j in range(n_col // 2):
            lanes = slice(2 * j * blk, (2 * j + 2) * blk)
            first, second = split_pair(res[:half, lanes], res[half:, lanes])
            out_ref[r * n_col + 2 * j, blk:] = first
            out_ref[r * n_col + 2 * j + 1, blk:] = second


def extra_kernel(plan, keep_ref, *refs):
    row_refs, (out_ref, m_ref, o_ref) = refs[: plan.n_row], refs[plan.n_row :]
    row_id, col_id = lax.axis_index("row"), lax.axis_index("col")
    blk, n_col = plan.blk, plan.n_col
    for k in range(plan.extra):
        at = slice(k * blk, (k + 1) * blk)
        for apart, ref in enumerate(row_refs):
            start = pl.multiple_of(jnp.bitwise_xor(row_id, apart) * 2 * blk, 2 * blk)
            for j in range(n_col // 2):
                lanes = slice(2 * j * blk, (2 * j + 2) * blk)
                low, high = (ref[plan.slot(jnp.bitwise_xor(col_id, 2 * j + c)), at] for c in range(2))
                tile = jnp.concatenate(split_pair(low, high), axis=0)
                m_ref[pl.ds(start, 2 * blk), lanes] = tile
                if apart == 0:
                    o_ref[:, lanes] = tile
        m = m_ref[...]
        s = dot(o_ref[...], m)
        kept = []
        for p in range(2):
            keep = keep_ref[2 + k, pl.ds(2 * row_id + p, 1)]
            kept.append(jnp.where(keep > 0, s[p * blk : (p + 1) * blk], 0.0).astype(jnp.bfloat16))
        res = purify(jnp.concatenate(kept, axis=0), m)
        mine = res[:, : 2 * blk]
        for j in range(1, n_col // 2):
            mine = jnp.where(col_id // 2 == j, res[:, 2 * j * blk : (2 * j + 2) * blk], mine)
        first, second = split_pair(mine[:blk], mine[blk:])
        out_ref[at] = jnp.where(col_id % 2 == 0, first, second).astype(jnp.bfloat16)


def unpack_kernel(plan, kept_hbm, shift_hbm, ret_ref, *refs):
    *extra_refs, out_ref, rows_ref, shift_ref, stage, sems = refs
    row_id, col_id = lax.axis_index("row"), lax.axis_index("col")
    blk, half, rows, ndev = plan.blk, plan.half, plan.rows, plan.ndev
    copies = [
        pltpu.make_async_copy(shift_hbm, shift_ref, sems.at[0]),
        pltpu.make_async_copy(kept_hbm.at[pl.ds(2 * row_id, 2)], rows_ref, sems.at[1]),
    ]
    for copy in copies:
        copy.start()
    for d in range(ndev):
        stage[d * rows : (d + 1) * rows] = ret_ref[d]
    for ref in extra_refs:
        stage[ndev * rows :] = ref[...]
    for copy in copies:
        copy.wait()
    for p in range(2):
        shift = shift_ref[2 * row_id + p]
        lanes = slice(p * blk, (p + 1) * blk)
        for e in range(rows_ref.shape[2]):
            u = residue(rows_ref[p, col_id, e], shift)
            for h, start in enumerate(plan.starts(u)):
                tile = stage[pl.ds(start, half), :]
                out_ref[p, h * half : (h + 1) * half, e * blk : (e + 1) * blk] = tile[:, lanes].astype(jnp.float32)


def swapped(shard, axis, by):
    return lax.ppermute(shard, axis, [(i, i ^ by) for i in range(lax.axis_size(axis))])


def body(density, density_rows, square_rows, panel_shift):
    both = ("row", "col")
    n_row, n_col = lax.axis_size("row"), lax.axis_size("col")
    blk, rh = density.shape[1], density_rows.shape[2]
    npan = density_rows.shape[0]
    plan = Plan(n_row, n_col, blk)
    ndev, rows = plan.ndev, plan.rows
    bf16 = jnp.bfloat16
    size = n_col * blk
    square = pltpu.VMEM((size, size), bf16)
    tables = [pltpu.SMEM((2, npan, rh), jnp.int32), pltpu.SMEM((npan,), jnp.int32)]
    stage = pltpu.VMEM((ndev * rows + plan.extra * blk, 2 * blk), bf16)
    moved = jax.ShapeDtypeStruct((ndev, rows, 2 * blk), bf16)

    flat = jax.ShapeDtypeStruct((ndev * rows, 2 * blk), bf16)
    extra_shapes = [jax.ShapeDtypeStruct((plan.extra * blk, 2 * blk), bf16)] if plan.extra else []
    packed, *extra = pl.pallas_call(
        functools.partial(pack_kernel, plan),
        out_shape=[flat] + extra_shapes,
        in_specs=[HBM] * 3,
        out_specs=[HBM] * (1 + len(extra_shapes)),
        scratch_shapes=[pltpu.VMEM(density.shape, bf16)] + tables + [stage, pltpu.SemaphoreType.DMA((4,))],
        compiler_params=PACK_PARAMS,
        name="pack",
    )(density, density_rows, panel_shift)
    y = lax.all_to_all(packed.reshape(moved.shape), both, 0, 0, tiled=True)
    sets = 1 + (1 if plan.shared else 0) + plan.extra
    keep = pl.pallas_call(
        functools.partial(mask_kernel, plan),
        out_shape=jax.ShapeDtypeStruct((sets, npan, size), jnp.float32),
        in_specs=[SMEM, VMEM],
        out_specs=VMEM,
        compiler_params=PARAMS,
        name="masks",
    )(panel_shift, square_rows)
    if plan.extra:
        extra = extra[0][None]
        line = [extra] + [swapped(extra, "col", by) for by in range(2, n_col, 2)]
        y, keep, *line = lax.optimization_barrier((y, keep, *line))
        line = jnp.concatenate(line, axis=0)
        line = jnp.concatenate([line, swapped(line, "col", 1)], axis=0)
        plane = [line] + [swapped(line, "row", by) for by in range(1, n_row)]
        extra = [
            pl.pallas_call(
                functools.partial(extra_kernel, plan),
                out_shape=extra_shapes[0],
                in_specs=[VMEM] * (1 + n_row),
                out_specs=VMEM,
                scratch_shapes=[square, pltpu.VMEM((2 * blk, size), bf16)],
                compiler_params=PARAMS,
                name="extra",
            )(keep, *plane)
        ]
    if plan.shared:
        own = y[:, blk:]
        far = swapped(own, "col", 1)
    out = pl.pallas_call(
        functools.partial(full_kernel, plan),
        out_shape=moved,
        in_specs=[VMEM] * 2,
        out_specs=VMEM,
        scratch_shapes=[square] * 2,
        compiler_params=PARAMS,
        cost_estimate=pl.CostEstimate(flops=4 * size**3, bytes_accessed=4 * ndev * rows * 2 * blk, transcendentals=0),
        name="full",
    )(keep, y)
    if plan.shared:
        out = pl.pallas_call(
            functools.partial(shared_kernel, plan),
            out_shape=moved,
            in_specs=[VMEM] * 4,
            out_specs=VMEM,
            scratch_shapes=[square] + [pltpu.VMEM((size // 2, size), bf16)] * 2,
            compiler_params=PARAMS,
            name="shared",
        )(keep, own, far, out)
    ret = lax.all_to_all(out, both, 0, 0, tiled=True)
    return pl.pallas_call(
        functools.partial(unpack_kernel, plan),
        out_shape=jax.ShapeDtypeStruct(density.shape, jnp.float32),
        in_specs=[HBM] * 2 + [VMEM] * (1 + len(extra)),
        out_specs=VMEM,
        scratch_shapes=tables + [stage, pltpu.SemaphoreType.DMA((2,))],
        compiler_params=PARAMS,
        name="unpack",
    )(square_rows, panel_shift, ret, *extra)


def solution(mesh):
    placed = (P("row", None, "col"), P(), P(), P())
    return jax.shard_map(
        body, mesh=mesh, in_specs=placed, out_specs=P("row", None, "col"), check_vma=False
    )
```

time: 68.6 us -> 63.9 us (0.931)
  blocking collectives: 31.9 us -> 0 us
  waiting for transfers between devices: 20.5 us -> 34.8 us
  starting transfers between devices: 4.53 us -> 18.7 us
  local copies, waits for them, and re-layouts: 3.25 us -> 0.07 us
  Pallas kernels: 7.89 us -> 9.77 us
    all_to_all x1 -> x0, blocking collectives: 31.9 us -> none  [body(): y = lax.all_to_all(packed, both, 0, 0, tiled=True)]
    ppermute x2 -> x8, waiting for transfers between devices: 13.2 us -> 29.1 us  [swapped(): lax.ppermute(shard, axis, [(i, i ^ by) for i in range(lax.axis_size(axis))])]
    all_to_all x0 -> x1, starting transfers between devices: none -> 7.3 us  [body(): y = lax.all_to_all(packed.reshape(moved.shape), both, 0, 0, tiled=True)]
    ppermute x2 -> x8, starting transfers between devices: 1.77 us -> 8.4 us  [swapped(): lax.ppermute(shard, axis, [(i, i ^ by) for i in range(lax.axis_size(axis))])]
    unnamed x12 -> x10, local copies, waits for them, and re-layouts: 3.22 us -> 0.04 us
    pallas_call x3 -> x5, Pallas kernels: 5.16 us -> 7.63 us  [the longest x1 2.45 us: body(): pl.pallas_call(functools.partial(pack_kernel, plan), out_shape=[flat] + e...]
    all_to_all x1, waiting for transfers between devices: 7.3 us -> 5.12 us  [body(): ret = lax.all_to_all(out, both, 0, 0, tiled=True)]
  transfers between devices with their start and end apart: 3 -> 10, of which waited for: 3 -> 8; matrix products, arithmetic and copies ran while one was open for 0% -> 0% of each run, Pallas kernels for 2% -> 5%
where the time goes in v2:
time: 63.9 us; the launch traced here: 63.5 us
  waiting for transfers between devices  34.8 us (54%)
  starting transfers between devices  18.7 us (29%)
  Pallas kernels  9.77 us (15%)
    ppermute x8, waiting for transfers between devices, swapped(): lax.ppermute(shard, axis, [(i, i ^ by) for i in range(lax.axis_size(axis))])  29.1 us
    ppermute x8, starting transfers between devices, swapped(): lax.ppermute(shard, axis, [(i, i ^ by) for i in range(lax.axis_size(axis))])  8.4 us
    all_to_all x1, starting transfers between devices, body(): y = lax.all_to_all(packed.reshape(moved.shape), both, 0, 0, tiled=True)  7.3 us
    all_to_all x1, waiting for transfers between devices, body(): ret = lax.all_to_all(out, both, 0, 0, tiled=True)  5.12 us
    all_to_all x1, starting transfers between devices, body(): ret = lax.all_to_all(out, both, 0, 0, tiled=True)  3.03 us
    pallas_call x1, Pallas kernels, body(): pl.pallas_call(functools.partial(pack_kernel, plan), out_shape=[flat] + e...  2.45 us
    pallas_call x1, Pallas kernels, body(): pl.pallas_call(functools.partial(shared_kernel, plan), out_shape=moved, i...  2.29 us
    pallas_call x1, Pallas kernels, body(): pl.pallas_call(functools.partial(unpack_kernel, plan), out_shape=jax.Shap...  2.14 us
  transfers between devices with their start and end apart: 10, of which 8 were waited for; matrix products, arithmetic and copies ran while one was open for 0% of the time, Pallas kernels for 5%

profile of v2, /device:TPU:0, one launch (start us, length us, event | category | flops | bytes accessed | tf_op | source)
XLA Modules:
  0.0 63.5 jit_solution(1017365578628675809)
XLA Ops:
  0.0 2.5 %pack.1 = (bf16[3072,128]{1,0:T(8,128)(2,1)}, bf16[64,128]{1,0:T(8,128)(2,1)}) custom-call(bf16[2,64,2048]{2,1,0:T(8,128)(2,1)} %x_hbm.1, s32[8,8,32]{2,1,0:T(8,128)} %rows_hbm.1, s32[8]{0:T(128)} %shift_hbm.3), custom_call_target="tpu_custom_call" | custom-call | tf_op jit(solution)/shard_map/pack/pallas_call | solution.py:245
  2.5 0.0 copy-start.2
  2.5 0.0 copy-start
  2.5 7.3 %all-to-all-start = ((bf16[32,96,128]{2,1,0:T(8,128)(2,1)}), bf16[32,96,128]{2,1,0:T(8,128)(2,1)S(1)}, u32[]{:S(2)}, u32[]{:S(2)}) async-start(bf16[32,96,128]{2,1,0:T(8,128)(2,1)} %bitcast.2), calls=%async_computation | async-start | bytes 1572864 | tf_op jit(solution)/shard_map/all_to_all | solution.py:254
  9.8 0.0 copy-start.1
  9.8 0.0 copy-done.2
  9.8 3.7 %collective-permute-start.2 = (bf16[1,64,128]{2,1,0:T(8,128)(2,1)S(1)}, bf16[1,64,128]{2,1,0:T(8,128)(2,1)S(1)}, u32[]{:S(2)}, u32[]{:S(2)}) collective-permute-start(bf16[1,64,128]{2,1,0:T(8,128)(2,1)S(1)} %bitcast.3), channel_id=1, source_target_pairs={{0,6},{1,7},{2,4},{3,5},{4,2},{5,3},{6,0},{7,1},{8,14},{9,15},{10,... | collective-permute-start | bytes 49160 | tf_op jit(solution)/shard_map/ppermute | solution.py:226
  13.5 0.0 collective-permute-start.1
  13.5 0.8 %collective-permute-start = (bf16[1,64,128]{2,1,0:T(8,128)(2,1)S(1)}, bf16[1,64,128]{2,1,0:T(8,128)(2,1)S(1)}, u32[]{:S(2)}, u32[]{:S(2)}) collective-permute-start(bf16[1,64,128]{2,1,0:T(8,128)(2,1)S(1)} %bitcast.5), channel_id=1, source_target_pairs={{0,2},{1,3},{2,0},{3,1},{4,6},{5,7},{6,4},{7,5},{8,10},{9,11},{10,... | collective-permute-start | bytes 49160 | tf_op jit(solution)/shard_map/ppermute | solution.py:226
  14.3 0.0 copy-done
  14.3 0.0 copy-done.1
  14.3 0.7 %masks.1.keep_ref = f32[3,8,512]{2,1,0:T(8,128)S(1)} custom-call(s32[8]{0:T(128)S(1)} %copy-done.1, s32[8,8,32]{2,1,0:T(8,128)S(1)} %copy-done), custom_call_target="tpu_custom_call" | custom-call | tf_op jit(solution)/shard_map/masks/pallas_call | solution.py:256
  15.0 12.8 %collective-permute-done.2 = bf16[1,64,128]{2,1,0:T(8,128)(2,1)S(1)} collective-permute-done((bf16[1,64,128]{2,1,0:T(8,128)(2,1)S(1)}, bf16[1,64,128]{2,1,0:T(8,128)(2,1)S(1)}, u32[]{:S(2)}, u32[]{:S(2)}) %collective-permute-start.2) | collective-permute-done | bytes 16416 | tf_op jit(solution)/shard_map/ppermute | solution.py:226
  27.9 4.0 %collective-permute-done.1 = bf16[1,64,128]{2,1,0:T(8,128)(2,1)S(1)} collective-permute-done((bf16[1,64,128]{2,1,0:T(8,128)(2,1)S(1)}, bf16[1,64,128]{2,1,0:T(8,128)(2,1)S(1)}, u32[]{:S(2)}, u32[]{:S(2)}) %collective-permute-start.1) | collective-permute-done | bytes 16416 | tf_op jit(solution)/shard_map/ppermute | solution.py:226
  31.8 0.0 collective-permute-done
  31.8 0.6 %all-to-all-done.y_ref = bf16[32,96,128]{2,1,0:T(8,128)(2,1)S(1)} async-done(((bf16[32,96,128]{2,1,0:T(8,128)(2,1)}), bf16[32,96,128]{2,1,0:T(8,128)(2,1)S(1)}, u32[]{:S(2)}, u32[]{:S(2)}) %all-to-all-start) | async-done | bytes 786464 | tf_op jit(solution)/shard_map/all_to_all | solution.py:254
  32.5 0.1 collective-permute-start.3
  32.6 1.5 %full.1.part_ref = bf16[32,96,128]{2,1,0:T(8,128)(2,1)S(1)} custom-call(f32[3,8,512]{2,1,0:T(8,128)S(1)} %masks.1.keep_ref, bf16[32,96,128]{2,1,0:T(8,128)(2,1)S(1)} %all-to-all-done.y_ref), custom_call_target="tpu_custom_call" | custom-call | flops 536870912 | bytes 1572864 | tf_op jit(solution)/shard_map/full/pallas_call | solution.py:285
  34.0 0.1 collective-permute-done.3.far_ref
  34.1 2.3 %shared.1 = bf16[32,96,128]{2,1,0:T(8,128)(2,1)} custom-call(f32[3,8,512]{2,1,0:T(8,128)S(1)} %masks.1.keep_ref, bf16[32,32,128]{2,1,0:T(8,128)(2,1)S(1)} %slice.3.own_ref, bf16[32,32,128]{2,1,0:T(8,128)(2,1)S(1)} %collective-permute-done.3.far_ref, bf16[32,96,128]{2,1,0:T(8,128)(2,1)S(1)} %full.1.part_ref), custom_call_target="tpu_custom_call" | custom-call | tf_op jit(solution)/shard_map/shared/pallas_call | solution.py:296
  36.4 3.0 %all-to-all-start.1 = ((bf16[32,96,128]{2,1,0:T(8,128)(2,1)}), bf16[32,96,128]{2,1,0:T(8,128)(2,1)S(1)}, u32[]{:S(2)}, u32[]{:S(2)}) async-start(bf16[32,96,128]{2,1,0:T(8,128)(2,1)} %shared.1), calls=%async_computation.1 | async-start | bytes 1572864 | tf_op jit(solution)/shard_map/all_to_all | solution.py:305
  39.4 0.3 collective-permute-start.4
  39.8 1.0 %collective-permute-done.4 = bf16[4,64,128]{2,1,0:T(8,128)(2,1)S(1)} collective-permute-done((bf16[4,64,128]{2,1,0:T(8,128)(2,1)S(1)}, bf16[4,64,128]{2,1,0:T(8,128)(2,1)S(1)}, u32[]{:S(2)}, u32[]{:S(2)}) %collective-permute-start.4) | collective-permute-done | bytes 65568 | tf_op jit(solution)/shard_map/ppermute | solution.py:226
  40.8 2.7 %collective-permute-start.7 = (bf16[8,64,128]{2,1,0:T(8,128)(2,1)S(1)}, bf16[8,64,128]{2,1,0:T(8,128)(2,1)S(1)}, u32[]{:S(2)}, u32[]{:S(2)}) collective-permute-start(bf16[8,64,128]{2,1,0:T(8,128)(2,1)S(1)} %constant_dynamic-update-slice_fusion.refs_0_), channel_id=1, source_target_pairs={{0,24},{8,16},{16,8},{24,0},{1,25},{9,17},{17,9},{25,1},{2,26},{10... | collective-permute-start | bytes 393224 | tf_op jit(solution)/shard_map/ppermute | solution.py:226
  43.5 0.6 collective-permute-start.6
  44.1 0.3 collective-permute-start.5
  44.3 8.0 %collective-permute-done.7.refs_3_ = bf16[8,64,128]{2,1,0:T(8,128)(2,1)S(1)} collective-permute-done((bf16[8,64,128]{2,1,0:T(8,128)(2,1)S(1)}, bf16[8,64,128]{2,1,0:T(8,128)(2,1)S(1)}, u32[]{:S(2)}, u32[]{:S(2)}) %collective-permute-start.7) | collective-permute-done | bytes 131104 | tf_op jit(solution)/shard_map/ppermute | solution.py:226
  52.3 3.2 %collective-permute-done.6.refs_2_ = bf16[8,64,128]{2,1,0:T(8,128)(2,1)S(1)} collective-permute-done((bf16[8,64,128]{2,1,0:T(8,128)(2,1)S(1)}, bf16[8,64,128]{2,1,0:T(8,128)(2,1)S(1)}, u32[]{:S(2)}, u32[]{:S(2)}) %collective-permute-start.6) | collective-permute-done | bytes 131104 | tf_op jit(solution)/shard_map/ppermute | solution.py:226
  55.6 0.0 collective-permute-done.5.refs_1_
  55.6 0.7 %extra.1.refs_0_ = bf16[64,128]{1,0:T(8,128)(2,1)S(1)} custom-call(f32[3,8,512]{2,1,0:T(8,128)S(1)} %masks.1.keep_ref, bf16[8,64,128]{2,1,0:T(8,128)(2,1)S(1)} %constant_dynamic-update-slice_fusion.refs_0_, bf16[8,64,128]{2,1,0:T(8,128)(2,1)S(1)} %collective-permute-done.5.refs_1_, bf16[8,64,128]{2,1,0:T(8,128)(2,1)S(1)} %collective-permute-done.6.refs_2_, ...), custom_call_target="tpu_custom_call" | custom-call | tf_op jit(solution)/shard_map/extra/pallas_call | solution.py:272
  56.3 5.1 %all-to-all-done.1.ret_ref = bf16[32,96,128]{2,1,0:T(8,128)(2,1)S(1)} async-done(((bf16[32,96,128]{2,1,0:T(8,128)(2,1)}), bf16[32,96,128]{2,1,0:T(8,128)(2,1)S(1)}, u32[]{:S(2)}, u32[]{:S(2)}) %all-to-all-start.1) | async-done | bytes 786464 | tf_op jit(solution)/shard_map/all_to_all | solution.py:305
  61.4 2.1 %unpack.1 = f32[2,64,2048]{2,1,0:T(8,128)} custom-call(s32[8,8,32]{2,1,0:T(8,128)S(1)} %copy-done, s32[8]{0:T(128)S(1)} %copy-done.1, bf16[32,96,128]{2,1,0:T(8,128)(2,1)S(1)} %all-to-all-done.1.ret_ref, bf16[64,128]{1,0:T(8,128)(2,1)S(1)} %extra.1.refs_0_), custom_call_target="tpu_custom_call" | custom-call | tf_op jit(solution)/shard_map/unpack/pallas_call | solution.py:306
  (7 shorter events, 0.1 us)
Async XLA Ops:
  2.5 7.3 %copy-start.2 = (bf16[64,128]{1,0:T(8,128)(2,1)S(1)}, bf16[64,128]{1,0:T(8,128)(2,1)}, u32[]{:S(2)}) copy-start(bf16[64,128]{1,0:T(8,128)(2,1)} %get-tuple-element.14) | copy-start | bytes 49156
  2.5 11.8 %copy-start = (s32[8,8,32]{2,1,0:T(8,128)S(1)}, s32[8,8,32]{2,1,0:T(8,128)}, u32[]{:S(2)}) copy-start(s32[8,8,32]{2,1,0:T(8,128)} %kept_hbm.1) | copy-start | bytes 24580
  2.5 30.0 %all-to-all-start = ((bf16[32,96,128]{2,1,0:T(8,128)(2,1)}), bf16[32,96,128]{2,1,0:T(8,128)(2,1)S(1)}, u32[]{:S(2)}, u32[]{:S(2)}) async-start(bf16[32,96,128]{2,1,0:T(8,128)(2,1)} %bitcast.2), calls=%async_computation | async-start | bytes 1572864 | tf_op jit(solution)/shard_map/all_to_all | solution.py:254
  9.8 4.5 %copy-start.1 = (s32[8]{0:T(128)S(1)}, s32[8]{0:T(128)}, u32[]{:S(2)}) copy-start(s32[8]{0:T(128)} %shift_hbm.3) | copy-start | bytes 100
  9.8 18.0 %collective-permute-start.2 = (bf16[1,64,128]{2,1,0:T(8,128)(2,1)S(1)}, bf16[1,64,128]{2,1,0:T(8,128)(2,1)S(1)}, u32[]{:S(2)}, u32[]{:S(2)}) collective-permute-start(bf16[1,64,128]{2,1,0:T(8,128)(2,1)S(1)} %bitcast.3), channel_id=1, source_target_pairs={{0,6},{1,7},{2,4},{3,5},{4,2},{5,3},{6,0},{7,1},{8,14},{9,15},{10,... | collective-permute-start | bytes 49160 | tf_op jit(solution)/shard_map/ppermute | solution.py:226
  13.5 18.3 %collective-permute-start.1 = (bf16[1,64,128]{2,1,0:T(8,128)(2,1)S(1)}, bf16[1,64,128]{2,1,0:T(8,128)(2,1)S(1)}, u32[]{:S(2)}, u32[]{:S(2)}) collective-permute-start(bf16[1,64,128]{2,1,0:T(8,128)(2,1)S(1)} %bitcast.4), channel_id=1, source_target_pairs={{0,4},{1,5},{2,6},{3,7},{4,0},{5,1},{6,2},{7,3},{8,12},{9,13},{10,... | collective-permute-start | bytes 49160 | tf_op jit(solution)/shard_map/ppermute | solution.py:226
  13.5 18.3 %collective-permute-start = (bf16[1,64,128]{2,1,0:T(8,128)(2,1)S(1)}, bf16[1,64,128]{2,1,0:T(8,128)(2,1)S(1)}, u32[]{:S(2)}, u32[]{:S(2)}) collective-permute-start(bf16[1,64,128]{2,1,0:T(8,128)(2,1)S(1)} %bitcast.5), channel_id=1, source_target_pairs={{0,2},{1,3},{2,0},{3,1},{4,6},{5,7},{6,4},{7,5},{8,10},{9,11},{10,... | collective-permute-start | bytes 49160 | tf_op jit(solution)/shard_map/ppermute | solution.py:226
  32.5 1.6 %collective-permute-start.3 = (bf16[32,32,128]{2,1,0:T(8,128)(2,1)S(1)}, bf16[32,32,128]{2,1,0:T(8,128)(2,1)S(1)}, u32[]{:S(2)}, u32[]{:S(2)}) collective-permute-start(bf16[32,32,128]{2,1,0:T(8,128)(2,1)S(1)} %slice.3.own_ref), channel_id=1, source_target_pairs={{0,1},{1,0},{2,3},{3,2},{4,5},{5,4},{6,7},{7,6},{8,9},{9,8},{10,11... | collective-permute-start | bytes 786440 | tf_op jit(solution)/shard_map/ppermute | solution.py:226
  36.4 25.0 %all-to-all-start.1 = ((bf16[32,96,128]{2,1,0:T(8,128)(2,1)}), bf16[32,96,128]{2,1,0:T(8,128)(2,1)S(1)}, u32[]{:S(2)}, u32[]{:S(2)}) async-start(bf16[32,96,128]{2,1,0:T(8,128)(2,1)} %shared.1), calls=%async_computation.1 | async-start | bytes 1572864 | tf_op jit(solution)/shard_map/all_to_all | solution.py:305
  39.4 1.3 %collective-permute-start.4 = (bf16[4,64,128]{2,1,0:T(8,128)(2,1)S(1)}, bf16[4,64,128]{2,1,0:T(8,128)(2,1)S(1)}, u32[]{:S(2)}, u32[]{:S(2)}) collective-permute-start(bf16[4,64,128]{2,1,0:T(8,128)(2,1)S(1)} %pad_maximum_fusion), channel_id=1, source_target_pairs={{0,1},{1,0},{2,3},{3,2},{4,5},{5,4},{6,7},{7,6},{8,9},{9,8},{10,11... | collective-permute-start | bytes 196616 | tf_op jit(solution)/shard_map/ppermute | solution.py:226
  40.8 11.6 %collective-permute-start.7 = (bf16[8,64,128]{2,1,0:T(8,128)(2,1)S(1)}, bf16[8,64,128]{2,1,0:T(8,128)(2,1)S(1)}, u32[]{:S(2)}, u32[]{:S(2)}) collective-permute-start(bf16[8,64,128]{2,1,0:T(8,128)(2,1)S(1)} %constant_dynamic-update-slice_fusion.refs_0_), channel_id=1, source_target_pairs={{0,24},{8,16},{16,8},{24,0},{1,25},{9,17},{17,9},{25,1},{2,26},{10... | collective-permute-start | bytes 393224 | tf_op jit(solution)/shard_map/ppermute | solution.py:226
  43.5 12.0 %collective-permute-start.6 = (bf16[8,64,128]{2,1,0:T(8,128)(2,1)S(1)}, bf16[8,64,128]{2,1,0:T(8,128)(2,1)S(1)}, u32[]{:S(2)}, u32[]{:S(2)}) collective-permute-start(bf16[8,64,128]{2,1,0:T(8,128)(2,1)S(1)} %constant_dynamic-update-slice_fusion.refs_0_), channel_id=1, source_target_pairs={{0,16},{8,24},{16,0},{24,8},{1,17},{9,25},{17,1},{25,9},{2,18},{10... | collective-permute-start | bytes 393224 | tf_op jit(solution)/shard_map/ppermute | solution.py:226
  44.1 11.5 %collective-permute-start.5 = (bf16[8,64,128]{2,1,0:T(8,128)(2,1)S(1)}, bf16[8,64,128]{2,1,0:T(8,128)(2,1)S(1)}, u32[]{:S(2)}, u32[]{:S(2)}) collective-permute-start(bf16[8,64,128]{2,1,0:T(8,128)(2,1)S(1)} %constant_dynamic-update-slice_fusion.refs_0_), channel_id=1, source_target_pairs={{0,8},{8,0},{16,24},{24,16},{1,9},{9,1},{17,25},{25,17},{2,10},{10... | collective-permute-start | bytes 393224 | tf_op jit(solution)/shard_map/ppermute | solution.py:226

commit v3 on v2

--- a/solution.py
+++ b/solution.py
@@ -2,6 +2,7 @@
 
 import jax
 import jax.numpy as jnp
+import numpy as np
 from jax import lax
 from jax.experimental import pallas as pl
 from jax.experimental.pallas import tpu as pltpu
@@ -27,25 +28,22 @@
         self.half = blk // 2
         self.rows = blk + (self.half if self.shared else 0)
 
-    def starts(self, u):
-        rows = self.rows
-        first = u * rows
-        step = self.half
-        if self.shared:
+    def starts(self):
+        table = np.zeros((2, 2 * PANEL - 1), np.int32)
+        for i in range(2 * PANEL - 1):
+            u = (i + 1) % PANEL
             chip = u - self.full
-            is_full, is_shared = u < self.full, u < self.full + self.shared
-            tail = self.ndev * rows + (chip - self.shared) * self.blk
-            first = jnp.where(is_full, first, jnp.where(is_shared, 2 * chip * rows + self.blk, tail))
-            step = jnp.where(jnp.logical_and(is_shared, jnp.logical_not(is_full)), rows, self.half)
-        return [pl.multiple_of(first + h * step, self.half) for h in range(2)]
+            if u < self.full:
+                first, step = u * self.rows, self.half
+            elif chip < self.shared:
+                first, step = 2 * chip * self.rows + self.blk, self.rows
+            else:
+                first, step = self.ndev * self.rows + (chip - self.shared) * self.blk, self.half
+            table[:, i] = first, first + step
+        return table
 
     def slot(self, apart):
         return apart % 2 * (self.n_col // 2) + apart // 2
-
-
-def residue(row, shift):
-    u = row - shift
-    return jnp.where(u < 0, u + PANEL, u)
 
 
 def kept_lanes(rows, u, shift, blk):
@@ -58,29 +56,31 @@
     return jnp.sum(jnp.where(lane // blk == tile, has, 0.0), axis=0, keepdims=True)
 
 
-def pack_kernel(plan, x_hbm, rows_hbm, shift_hbm, out_ref, *refs):
-    *extra_refs, x_ref, rows_ref, shift_ref, stage, sems = refs
+def pack_kernel(plan, x_hbm, rows_hbm, shift_hbm, starts_hbm, out_ref, *refs):
+    *extra_refs, x_ref, rows_ref, shift_ref, starts_ref, stage, sems = refs
     row_id, col_id = lax.axis_index("row"), lax.axis_index("col")
     blk, half, total = plan.blk, plan.half, plan.ndev * plan.rows
     copies = [
         pltpu.make_async_copy(shift_hbm, shift_ref, sems.at[0]),
         pltpu.make_async_copy(rows_hbm.at[pl.ds(2 * row_id, 2)], rows_ref, sems.at[1]),
-        pltpu.make_async_copy(x_hbm.at[0], x_ref.at[0], sems.at[2]),
-        pltpu.make_async_copy(x_hbm.at[1], x_ref.at[1], sems.at[3]),
+        pltpu.make_async_copy(starts_hbm, starts_ref, sems.at[2]),
+        pltpu.make_async_copy(x_hbm.at[0], x_ref.at[0], sems.at[3]),
+        pltpu.make_async_copy(x_hbm.at[1], x_ref.at[1], sems.at[4]),
     ]
     for copy in copies:
         copy.start()
     stage[...] = jnp.zeros_like(stage)
-    for copy in copies[:2]:
+    for copy in copies[:3]:
         copy.wait()
     for p in range(2):
-        copies[2 + p].wait()
-        shift = shift_ref[2 * row_id + p]
+        copies[3 + p].wait()
+        base = PANEL - 1 - shift_ref[2 * row_id + p]
         lanes = slice(p * blk, (p + 1) * blk)
         for e in range(rows_ref.shape[2]):
-            u = residue(rows_ref[p, col_id, e], shift)
+            at = rows_ref[p, col_id, e] + base
             block = x_ref[p, :, e * blk : (e + 1) * blk]
-            for h, start in enumerate(plan.starts(u)):
+            for h in range(2):
+                start = pl.multiple_of(starts_ref[h, at], half)
                 stage[pl.ds(start, half), lanes] = block[h * half : (h + 1) * half]
     copies = [pltpu.make_async_copy(stage.at[pl.ds(0, total)], out_ref, sems.at[0])]
     for ref in extra_refs:
@@ -113,6 +113,16 @@
 
 def purify(s, m):
     return 3.0 * s.astype(jnp.float32) - 2.0 * dot(s, m)
+
+
+def put_blocks(plan, res, height, out_ref):
+    for r in range(plan.n_row):
+        for j in range(plan.n_col // 2):
+            lanes = slice(2 * j * plan.blk, (2 * j + 2) * plan.blk)
+            upper = res[2 * r * height : (2 * r + 1) * height, lanes]
+            lower = res[(2 * r + 1) * height : (2 * r + 2) * height, lanes]
+            to = r * plan.n_col + 2 * j
+            out_ref[to], out_ref[to + 1] = split_pair(upper, lower)
 
 
 def full_kernel(plan, keep_ref, y_ref, out_ref, m_ref, s_ref):
@@ -125,23 +135,19 @@
             m_ref[2 * r * blk : (2 * r + 1) * blk, lanes] = first
             m_ref[(2 * r + 1) * blk : (2 * r + 2) * blk, lanes] = second
     m = m_ref[...]
+    s = dot(m, m)
     for panel in range(2 * plan.n_row):
         at = slice(panel * blk, (panel + 1) * blk)
-        s = dot(m_ref[at], m)
-        s_ref[at] = jnp.where(keep_ref[0, panel : panel + 1] > 0, s, 0.0).astype(jnp.bfloat16)
-    for r in range(plan.n_row):
-        res = purify(s_ref[2 * r * blk : (2 * r + 2) * blk], m).astype(jnp.bfloat16)
-        for j in range(n_col // 2):
-            lanes = slice(2 * j * blk, (2 * j + 2) * blk)
-            first, second = split_pair(res[:blk, lanes], res[blk:, lanes])
-            out_ref[r * n_col + 2 * j, :blk] = first
-            out_ref[r * n_col + 2 * j + 1, :blk] = second
-
-
-def shared_kernel(plan, keep_ref, own_ref, far_ref, part_ref, out_ref, m_ref, s_ref, o_ref):
+        s_ref[at] = jnp.where(keep_ref[0, panel : panel + 1] > 0, s[at], 0.0).astype(jnp.bfloat16)
+    res = purify(s_ref[...], m).astype(jnp.bfloat16)
+    put_blocks(plan, res, blk, out_ref)
+
+
+def shared_kernel(plan, keep_ref, own_ref, far_ref, part_ref, out_hbm, m_ref, s_ref, o_ref, res_ref, sems):
     blk, half, n_col = plan.blk, plan.half, plan.n_col
     first_core = lax.axis_index("col") % 2 == 0
-    out_ref[:, :blk] = part_ref[:, :blk]
+    part_copy = pltpu.make_async_copy(part_ref, out_hbm.at[:, pl.ds(0, blk)], sems.at[0])
+    part_copy.start()
     for r in range(plan.n_row):
         for j in range(n_col // 2):
             src = r * n_col + 2 * j
@@ -154,17 +160,15 @@
                 m_ref[at + half : at + blk, lanes] = jnp.where(first_core, far[p], own[p])
                 o_ref[(2 * r + p) * half : (2 * r + p + 1) * half, lanes] = own[p]
     m = m_ref[...]
+    s = dot(o_ref[...], m)
     for panel in range(2 * plan.n_row):
         at = slice(panel * half, (panel + 1) * half)
-        s = dot(o_ref[at], m)
-        s_ref[at] = jnp.where(keep_ref[1, panel : panel + 1] > 0, s, 0.0).astype(jnp.bfloat16)
-    for r in range(plan.n_row):
-        res = purify(s_ref[2 * r * half : (2 * r + 2) * half], m).astype(jnp.bfloat16)
-        for j in range(n_col // 2):
-            lanes = slice(2 * j * blk, (2 * j + 2) * blk)
-            first, second = split_pair(res[:half, lanes], res[half:, lanes])
-            out_ref[r * n_col + 2 * j, blk:] = first
-            out_ref[r * n_col + 2 * j + 1, blk:] = second
+        s_ref[at] = jnp.where(keep_ref[1, panel : panel + 1] > 0, s[at], 0.0).astype(jnp.bfloat16)
+    put_blocks(plan, purify(s_ref[...], m).astype(jnp.bfloat16), half, res_ref)
+    res_copy = pltpu.make_async_copy(res_ref, out_hbm.at[:, pl.ds(blk, half)], sems.at[1])
+    res_copy.start()
+    part_copy.wait()
+    res_copy.wait()
 
 
 def extra_kernel(plan, keep_ref, *refs):
@@ -196,30 +200,34 @@
         out_ref[at] = jnp.where(col_id % 2 == 0, first, second).astype(jnp.bfloat16)
 
 
-def unpack_kernel(plan, kept_hbm, shift_hbm, ret_ref, *refs):
-    *extra_refs, out_ref, rows_ref, shift_ref, stage, sems = refs
+def unpack_kernel(plan, kept_hbm, shift_hbm, starts_hbm, ret_ref, *refs):
+    *extra_refs, out_hbm, rows_ref, shift_ref, starts_ref, stage, out_ref, sems = refs
     row_id, col_id = lax.axis_index("row"), lax.axis_index("col")
-    blk, half, rows, ndev = plan.blk, plan.half, plan.rows, plan.ndev
+    blk, half, total = plan.blk, plan.half, plan.ndev * plan.rows
     copies = [
         pltpu.make_async_copy(shift_hbm, shift_ref, sems.at[0]),
         pltpu.make_async_copy(kept_hbm.at[pl.ds(2 * row_id, 2)], rows_ref, sems.at[1]),
+        pltpu.make_async_copy(starts_hbm, starts_ref, sems.at[2]),
     ]
     for copy in copies:
         copy.start()
-    for d in range(ndev):
-        stage[d * rows : (d + 1) * rows] = ret_ref[d]
+    stage[:total] = ret_ref[...]
     for ref in extra_refs:
-        stage[ndev * rows :] = ref[...]
+        stage[total:] = ref[...]
     for copy in copies:
         copy.wait()
+    copies = [pltpu.make_async_copy(out_ref.at[p], out_hbm.at[p], sems.at[3 + p]) for p in range(2)]
     for p in range(2):
-        shift = shift_ref[2 * row_id + p]
+        base = PANEL - 1 - shift_ref[2 * row_id + p]
         lanes = slice(p * blk, (p + 1) * blk)
         for e in range(rows_ref.shape[2]):
-            u = residue(rows_ref[p, col_id, e], shift)
-            for h, start in enumerate(plan.starts(u)):
-                tile = stage[pl.ds(start, half), :]
+            at = rows_ref[p, col_id, e] + base
+            for h in range(2):
+                tile = stage[pl.ds(pl.multiple_of(starts_ref[h, at], half), half), :]
                 out_ref[p, h * half : (h + 1) * half, e * blk : (e + 1) * blk] = tile[:, lanes].astype(jnp.float32)
+        copies[p].start()
+    for copy in copies:
+        copy.wait()
 
 
 def swapped(shard, axis, by):
@@ -237,6 +245,8 @@
     size = n_col * blk
     square = pltpu.VMEM((size, size), bf16)
     tables = [pltpu.SMEM((2, npan, rh), jnp.int32), pltpu.SMEM((npan,), jnp.int32)]
+    starts = jnp.asarray(plan.starts())
+    tables.append(pltpu.SMEM(starts.shape, jnp.int32))
     stage = pltpu.VMEM((ndev * rows + plan.extra * blk, 2 * blk), bf16)
     moved = jax.ShapeDtypeStruct((ndev, rows, 2 * blk), bf16)
 
@@ -245,12 +255,12 @@
     packed, *extra = pl.pallas_call(
         functools.partial(pack_kernel, plan),
         out_shape=[flat] + extra_shapes,
-        in_specs=[HBM] * 3,
+        in_specs=[HBM] * 4,
         out_specs=[HBM] * (1 + len(extra_shapes)),
-        scratch_shapes=[pltpu.VMEM(density.shape, bf16)] + tables + [stage, pltpu.SemaphoreType.DMA((4,))],
+        scratch_shapes=[pltpu.VMEM(density.shape, bf16)] + tables + [stage, pltpu.SemaphoreType.DMA((5,))],
         compiler_params=PACK_PARAMS,
         name="pack",
-    )(density, density_rows, panel_shift)
+    )(density, density_rows, panel_shift, starts)
     y = lax.all_to_all(packed.reshape(moved.shape), both, 0, 0, tiled=True)
     sets = 1 + (1 if plan.shared else 0) + plan.extra
     keep = pl.pallas_call(
@@ -284,7 +294,7 @@
         far = swapped(own, "col", 1)
     out = pl.pallas_call(
         functools.partial(full_kernel, plan),
-        out_shape=moved,
+        out_shape=jax.ShapeDtypeStruct((ndev, blk, 2 * blk), bf16),
         in_specs=[VMEM] * 2,
         out_specs=VMEM,
         scratch_shapes=[square] * 2,
@@ -297,8 +307,10 @@
             functools.partial(shared_kernel, plan),
             out_shape=moved,
             in_specs=[VMEM] * 4,
-            out_specs=VMEM,
-            scratch_shapes=[square] + [pltpu.VMEM((size // 2, size), bf16)] * 2,
+            out_specs=HBM,
+            scratch_shapes=[square]
+            + [pltpu.VMEM((size // 2, size), bf16)] * 2
+            + [pltpu.VMEM((ndev, plan.half, 2 * blk), bf16), pltpu.SemaphoreType.DMA((2,))],
             compiler_params=PARAMS,
             name="shared",
         )(keep, own, far, out)
@@ -306,12 +318,12 @@
     return pl.pallas_call(
         functools.partial(unpack_kernel, plan),
         out_shape=jax.ShapeDtypeStruct(density.shape, jnp.float32),
-        in_specs=[HBM] * 2 + [VMEM] * (1 + len(extra)),
-        out_specs=VMEM,
-        scratch_shapes=tables + [stage, pltpu.SemaphoreType.DMA((2,))],
+        in_specs=[HBM] * 3 + [VMEM] * (1 + len(extra)),
+        out_specs=HBM,
+        scratch_shapes=tables + [stage, pltpu.VMEM(density.shape, jnp.float32), pltpu.SemaphoreType.DMA((5,))],
         compiler_params=PARAMS,
         name="unpack",
-    )(square_rows, panel_shift, ret, *extra)
+    )(square_rows, panel_shift, starts, ret.reshape(flat.shape), *extra)
 
 
 def solution(mesh):

time: 63.9 us -> 62.7 us (0.981)
  Pallas kernels: 9.77 us -> 8.14 us
    pallas_call x1, Pallas kernels: 2.29 us -> 1.51 us  [body(): pl.pallas_call(functools.partial(shared_kernel, plan), out_shape=moved, i...]
  transfers between devices with their start and end apart: 10 -> 10, of which waited for: 8 -> 8; matrix products, arithmetic and copies ran while one was open for 0% -> 0% of each run, Pallas kernels for 5% -> 4%
where the time goes in v3:
time: 62.7 us; the launch traced here: 62.4 us
  waiting for transfers between devices  35.3 us (56%)
  starting transfers between devices  18.7 us (30%)
  Pallas kernels  8.14 us (13%)
    ppermute x8, waiting for transfers between devices, swapped(): lax.ppermute(shard, axis, [(i, i ^ by) for i in range(lax.axis_size(axis))])  29.6 us
    ppermute x8, starting transfers between devices, swapped(): lax.ppermute(shard, axis, [(i, i ^ by) for i in range(lax.axis_size(axis))])  8.4 us
    all_to_all x1, starting transfers between devices, body(): y = lax.all_to_all(packed.reshape(moved.shape), both, 0, 0, tiled=True)  7.3 us
    all_to_all x1, waiting for transfers between devices, body(): ret = lax.all_to_all(out, both, 0, 0, tiled=True)  5.11 us
    all_to_all x1, starting transfers between devices, body(): ret = lax.all_to_all(out, both, 0, 0, tiled=True)  2.99 us
    pallas_call x1, Pallas kernels, body(): pl.pallas_call(functools.partial(pack_kernel, plan), out_shape=[flat] + e...  2.32 us
    pallas_call x1, Pallas kernels, body(): pl.pallas_call(functools.partial(unpack_kernel, plan), out_shape=jax.Shap...  1.92 us
    pallas_call x1, Pallas kernels, body(): pl.pallas_call(functools.partial(shared_kernel, plan), out_shape=moved, i...  1.51 us
  transfers between devices with their start and end apart: 10, of which 8 were waited for; matrix products, arithmetic and copies ran while one was open for 0% of the time, Pallas kernels for 4%

profile of v3, /device:TPU:0, one launch (start us, length us, event | category | flops | bytes accessed | tf_op | source)
XLA Modules:
  0.0 62.4 jit_solution(2934345417885328274)
XLA Ops:
  0.0 2.3 %pack.1 = (bf16[3072,128]{1,0:T(8,128)(2,1)}, bf16[64,128]{1,0:T(8,128)(2,1)}) custom-call(bf16[2,64,2048]{2,1,0:T(8,128)(2,1)} %x_hbm.1, s32[8,8,32]{2,1,0:T(8,128)} %rows_hbm.1, s32[8]{0:T(128)} %shift_hbm.3, s32[2,97]{1,0:T(2,128)} %constant.2.clone.starts_hbm), custom_call_target="tpu_custom_call" | custom-call | tf_op jit(solution)/shard_map/pack/pallas_call | solution.py:255
  2.3 0.0 copy-start.3
  2.3 0.0 copy-start
  2.3 7.3 %all-to-all-start = ((bf16[32,96,128]{2,1,0:T(8,128)(2,1)}), bf16[32,96,128]{2,1,0:T(8,128)(2,1)S(1)}, u32[]{:S(2)}, u32[]{:S(2)}) async-start(bf16[32,96,128]{2,1,0:T(8,128)(2,1)} %bitcast.4), calls=%async_computation | async-start | bytes 1572864 | tf_op jit(solution)/shard_map/all_to_all | solution.py:264
  9.7 0.0 copy-start.1
  9.7 0.0 copy-done.3
  9.7 3.7 %collective-permute-start.2 = (bf16[1,64,128]{2,1,0:T(8,128)(2,1)S(1)}, bf16[1,64,128]{2,1,0:T(8,128)(2,1)S(1)}, u32[]{:S(2)}, u32[]{:S(2)}) collective-permute-start(bf16[1,64,128]{2,1,0:T(8,128)(2,1)S(1)} %bitcast.5), channel_id=1, source_target_pairs={{0,6},{1,7},{2,4},{3,5},{4,2},{5,3},{6,0},{7,1},{8,14},{9,15},{10,... | collective-permute-start | bytes 49160 | tf_op jit(solution)/shard_map/ppermute | solution.py:234
  13.4 0.0 collective-permute-start.1
  13.4 0.8 %collective-permute-start = (bf16[1,64,128]{2,1,0:T(8,128)(2,1)S(1)}, bf16[1,64,128]{2,1,0:T(8,128)(2,1)S(1)}, u32[]{:S(2)}, u32[]{:S(2)}) collective-permute-start(bf16[1,64,128]{2,1,0:T(8,128)(2,1)S(1)} %bitcast.7), channel_id=1, source_target_pairs={{0,2},{1,3},{2,0},{3,1},{4,6},{5,7},{6,4},{7,5},{8,10},{9,11},{10,... | collective-permute-start | bytes 49160 | tf_op jit(solution)/shard_map/ppermute | solution.py:234
  14.1 0.0 copy-done
  14.1 0.0 copy-done.1
  14.1 0.7 %masks.1.keep_ref = f32[3,8,512]{2,1,0:T(8,128)S(1)} custom-call(s32[8]{0:T(128)S(1)} %copy-done.1, s32[8,8,32]{2,1,0:T(8,128)S(1)} %copy-done), custom_call_target="tpu_custom_call" | custom-call | tf_op jit(solution)/shard_map/masks/pallas_call | solution.py:266
  14.9 12.8 %collective-permute-done.2 = bf16[1,64,128]{2,1,0:T(8,128)(2,1)S(1)} collective-permute-done((bf16[1,64,128]{2,1,0:T(8,128)(2,1)S(1)}, bf16[1,64,128]{2,1,0:T(8,128)(2,1)S(1)}, u32[]{:S(2)}, u32[]{:S(2)}) %collective-permute-start.2) | collective-permute-done | bytes 16416 | tf_op jit(solution)/shard_map/ppermute | solution.py:234
  27.7 4.0 %collective-permute-done.1 = bf16[1,64,128]{2,1,0:T(8,128)(2,1)S(1)} collective-permute-done((bf16[1,64,128]{2,1,0:T(8,128)(2,1)S(1)}, bf16[1,64,128]{2,1,0:T(8,128)(2,1)S(1)}, u32[]{:S(2)}, u32[]{:S(2)}) %collective-permute-start.1) | collective-permute-done | bytes 16416 | tf_op jit(solution)/shard_map/ppermute | solution.py:234
  31.7 0.0 collective-permute-done
  31.7 0.6 %all-to-all-done.y_ref = bf16[32,96,128]{2,1,0:T(8,128)(2,1)S(1)} async-done(((bf16[32,96,128]{2,1,0:T(8,128)(2,1)}), bf16[32,96,128]{2,1,0:T(8,128)(2,1)S(1)}, u32[]{:S(2)}, u32[]{:S(2)}) %all-to-all-start) | async-done | bytes 786464 | tf_op jit(solution)/shard_map/all_to_all | solution.py:264
  32.4 0.1 collective-permute-start.3
  32.4 1.0 %full.1.part_ref = bf16[32,64,128]{2,1,0:T(8,128)(2,1)S(1)} custom-call(f32[3,8,512]{2,1,0:T(8,128)S(1)} %masks.1.keep_ref, bf16[32,96,128]{2,1,0:T(8,128)(2,1)S(1)} %all-to-all-done.y_ref), custom_call_target="tpu_custom_call" | custom-call | flops 536870912 | bytes 1572864 | tf_op jit(solution)/shard_map/full/pallas_call | solution.py:295
  33.4 0.6 collective-permute-done.3.far_ref
  34.0 1.5 %shared.1 = bf16[32,96,128]{2,1,0:T(8,128)(2,1)} custom-call(f32[3,8,512]{2,1,0:T(8,128)S(1)} %masks.1.keep_ref, bf16[32,32,128]{2,1,0:T(8,128)(2,1)S(1)} %slice.3.own_ref, bf16[32,32,128]{2,1,0:T(8,128)(2,1)S(1)} %collective-permute-done.3.far_ref, bf16[32,64,128]{2,1,0:T(8,128)(2,1)S(1)} %full.1.part_ref), custom_call_target="tpu_custom_call" | custom-call | tf_op jit(solution)/shard_map/shared/pallas_call | solution.py:306
  35.5 3.0 %all-to-all-start.1 = ((bf16[32,96,128]{2,1,0:T(8,128)(2,1)}), bf16[32,96,128]{2,1,0:T(8,128)(2,1)S(1)}, u32[]{:S(2)}, u32[]{:S(2)}) async-start(bf16[32,96,128]{2,1,0:T(8,128)(2,1)} %shared.1), calls=%async_computation.1 | async-start | bytes 1572864 | tf_op jit(solution)/shard_map/all_to_all | solution.py:317
  38.5 0.3 collective-permute-start.4
  38.8 1.0 %collective-permute-done.4 = bf16[4,64,128]{2,1,0:T(8,128)(2,1)S(1)} collective-permute-done((bf16[4,64,128]{2,1,0:T(8,128)(2,1)S(1)}, bf16[4,64,128]{2,1,0:T(8,128)(2,1)S(1)}, u32[]{:S(2)}, u32[]{:S(2)}) %collective-permute-start.4) | collective-permute-done | bytes 65568 | tf_op jit(solution)/shard_map/ppermute | solution.py:234
  39.8 2.7 %collective-permute-start.7 = (bf16[8,64,128]{2,1,0:T(8,128)(2,1)S(1)}, bf16[8,64,128]{2,1,0:T(8,128)(2,1)S(1)}, u32[]{:S(2)}, u32[]{:S(2)}) collective-permute-start(bf16[8,64,128]{2,1,0:T(8,128)(2,1)S(1)} %constant_dynamic-update-slice_fusion.refs_0_), channel_id=1, source_target_pairs={{0,24},{8,16},{16,8},{24,0},{1,25},{9,17},{17,9},{25,1},{2,26},{10... | collective-permute-start | bytes 393224 | tf_op jit(solution)/shard_map/ppermute | solution.py:234
  42.6 0.6 collective-permute-start.6
  43.1 0.3 collective-permute-start.5
  43.4 8.0 %collective-permute-done.7.refs_3_ = bf16[8,64,128]{2,1,0:T(8,128)(2,1)S(1)} collective-permute-done((bf16[8,64,128]{2,1,0:T(8,128)(2,1)S(1)}, bf16[8,64,128]{2,1,0:T(8,128)(2,1)S(1)}, u32[]{:S(2)}, u32[]{:S(2)}) %collective-permute-start.7) | collective-permute-done | bytes 131104 | tf_op jit(solution)/shard_map/ppermute | solution.py:234
  51.4 3.2 %collective-permute-done.6.refs_2_ = bf16[8,64,128]{2,1,0:T(8,128)(2,1)S(1)} collective-permute-done((bf16[8,64,128]{2,1,0:T(8,128)(2,1)S(1)}, bf16[8,64,128]{2,1,0:T(8,128)(2,1)S(1)}, u32[]{:S(2)}, u32[]{:S(2)}) %collective-permute-start.6) | collective-permute-done | bytes 131104 | tf_op jit(solution)/shard_map/ppermute | solution.py:234
  54.6 0.0 collective-permute-done.5.refs_1_
  54.6 0.7 %extra.1.refs_0_ = bf16[64,128]{1,0:T(8,128)(2,1)S(1)} custom-call(f32[3,8,512]{2,1,0:T(8,128)S(1)} %masks.1.keep_ref, bf16[8,64,128]{2,1,0:T(8,128)(2,1)S(1)} %constant_dynamic-update-slice_fusion.refs_0_, bf16[8,64,128]{2,1,0:T(8,128)(2,1)S(1)} %collective-permute-done.5.refs_1_, bf16[8,64,128]{2,1,0:T(8,128)(2,1)S(1)} %collective-permute-done.6.refs_2_, ...), custom_call_target="tpu_custom_call" | custom-call | tf_op jit(solution)/shard_map/extra/pallas_call | solution.py:282
  55.3 0.0 copy-start.2
  55.3 5.1 %all-to-all-done.1 = bf16[32,96,128]{2,1,0:T(8,128)(2,1)S(1)} async-done(((bf16[32,96,128]{2,1,0:T(8,128)(2,1)}), bf16[32,96,128]{2,1,0:T(8,128)(2,1)S(1)}, u32[]{:S(2)}, u32[]{:S(2)}) %all-to-all-start.1) | async-done | bytes 786464 | tf_op jit(solution)/shard_map/all_to_all | solution.py:317
  60.4 0.0 copy-done.2
  60.4 1.9 %unpack.1 = f32[2,64,2048]{2,1,0:T(8,128)} custom-call(s32[8,8,32]{2,1,0:T(8,128)S(1)} %copy-done, s32[8]{0:T(128)S(1)} %copy-done.1, s32[2,97]{1,0:T(2,128)S(1)} %copy-done.2, bf16[3072,128]{1,0:T(8,128)(2,1)S(1)} %bitcast.3, bf16[64,128]{1,0:T(8,128)(2,1)S(1)} %extra.1.refs_0_), custom_call_target="tpu_custom_call" | custom-call | tf_op jit(solution)/shard_map/unpack/pallas_call | solution.py:318
  (7 shorter events, 0.1 us)
Async XLA Ops:
  2.3 7.3 %copy-start.3 = (bf16[64,128]{1,0:T(8,128)(2,1)S(1)}, bf16[64,128]{1,0:T(8,128)(2,1)}, u32[]{:S(2)}) copy-start(bf16[64,128]{1,0:T(8,128)(2,1)} %get-tuple-element.14) | copy-start | bytes 49156
  2.3 11.8 %copy-start = (s32[8,8,32]{2,1,0:T(8,128)S(1)}, s32[8,8,32]{2,1,0:T(8,128)}, u32[]{:S(2)}) copy-start(s32[8,8,32]{2,1,0:T(8,128)} %kept_hbm.1) | copy-start | bytes 24580
  2.3 30.0 %all-to-all-start = ((bf16[32,96,128]{2,1,0:T(8,128)(2,1)}), bf16[32,96,128]{2,1,0:T(8,128)(2,1)S(1)}, u32[]{:S(2)}, u32[]{:S(2)}) async-start(bf16[32,96,128]{2,1,0:T(8,128)(2,1)} %bitcast.4), calls=%async_computation | async-start | bytes 1572864 | tf_op jit(solution)/shard_map/all_to_all | solution.py:264
  9.7 4.5 %copy-start.1 = (s32[8]{0:T(128)S(1)}, s32[8]{0:T(128)}, u32[]{:S(2)}) copy-start(s32[8]{0:T(128)} %shift_hbm.3) | copy-start | bytes 100
  9.7 18.0 %collective-permute-start.2 = (bf16[1,64,128]{2,1,0:T(8,128)(2,1)S(1)}, bf16[1,64,128]{2,1,0:T(8,128)(2,1)S(1)}, u32[]{:S(2)}, u32[]{:S(2)}) collective-permute-start(bf16[1,64,128]{2,1,0:T(8,128)(2,1)S(1)} %bitcast.5), channel_id=1, source_target_pairs={{0,6},{1,7},{2,4},{3,5},{4,2},{5,3},{6,0},{7,1},{8,14},{9,15},{10,... | collective-permute-start | bytes 49160 | tf_op jit(solution)/shard_map/ppermute | solution.py:234
  13.4 18.3 %collective-permute-start.1 = (bf16[1,64,128]{2,1,0:T(8,128)(2,1)S(1)}, bf16[1,64,128]{2,1,0:T(8,128)(2,1)S(1)}, u32[]{:S(2)}, u32[]{:S(2)}) collective-permute-start(bf16[1,64,128]{2,1,0:T(8,128)(2,1)S(1)} %bitcast.6), channel_id=1, source_target_pairs={{0,4},{1,5},{2,6},{3,7},{4,0},{5,1},{6,2},{7,3},{8,12},{9,13},{10,... | collective-permute-start | bytes 49160 | tf_op jit(solution)/shard_map/ppermute | solution.py:234
  13.4 18.3 %collective-permute-start = (bf16[1,64,128]{2,1,0:T(8,128)(2,1)S(1)}, bf16[1,64,128]{2,1,0:T(8,128)(2,1)S(1)}, u32[]{:S(2)}, u32[]{:S(2)}) collective-permute-start(bf16[1,64,128]{2,1,0:T(8,128)(2,1)S(1)} %bitcast.7), channel_id=1, source_target_pairs={{0,2},{1,3},{2,0},{3,1},{4,6},{5,7},{6,4},{7,5},{8,10},{9,11},{10,... | collective-permute-start | bytes 49160 | tf_op jit(solution)/shard_map/ppermute | solution.py:234
  32.4 1.6 %collective-permute-start.3 = (bf16[32,32,128]{2,1,0:T(8,128)(2,1)S(1)}, bf16[32,32,128]{2,1,0:T(8,128)(2,1)S(1)}, u32[]{:S(2)}, u32[]{:S(2)}) collective-permute-start(bf16[32,32,128]{2,1,0:T(8,128)(2,1)S(1)} %slice.3.own_ref), channel_id=1, source_target_pairs={{0,1},{1,0},{2,3},{3,2},{4,5},{5,4},{6,7},{7,6},{8,9},{9,8},{10,11... | collective-permute-start | bytes 786440 | tf_op jit(solution)/shard_map/ppermute | solution.py:234
  35.5 25.0 %all-to-all-start.1 = ((bf16[32,96,128]{2,1,0:T(8,128)(2,1)}), bf16[32,96,128]{2,1,0:T(8,128)(2,1)S(1)}, u32[]{:S(2)}, u32[]{:S(2)}) async-start(bf16[32,96,128]{2,1,0:T(8,128)(2,1)} %shared.1), calls=%async_computation.1 | async-start | bytes 1572864 | tf_op jit(solution)/shard_map/all_to_all | solution.py:317
  38.5 1.3 %collective-permute-start.4 = (bf16[4,64,128]{2,1,0:T(8,128)(2,1)S(1)}, bf16[4,64,128]{2,1,0:T(8,128)(2,1)S(1)}, u32[]{:S(2)}, u32[]{:S(2)}) collective-permute-start(bf16[4,64,128]{2,1,0:T(8,128)(2,1)S(1)} %pad_maximum_fusion), channel_id=1, source_target_pairs={{0,1},{1,0},{2,3},{3,2},{4,5},{5,4},{6,7},{7,6},{8,9},{9,8},{10,11... | collective-permute-start | bytes 196616 | tf_op jit(solution)/shard_map/ppermute | solution.py:234
  39.8 11.6 %collective-permute-start.7 = (bf16[8,64,128]{2,1,0:T(8,128)(2,1)S(1)}, bf16[8,64,128]{2,1,0:T(8,128)(2,1)S(1)}, u32[]{:S(2)}, u32[]{:S(2)}) collective-permute-start(bf16[8,64,128]{2,1,0:T(8,128)(2,1)S(1)} %constant_dynamic-update-slice_fusion.refs_0_), channel_id=1, source_target_pairs={{0,24},{8,16},{16,8},{24,0},{1,25},{9,17},{17,9},{25,1},{2,26},{10... | collective-permute-start | bytes 393224 | tf_op jit(solution)/shard_map/ppermute | solution.py:234
  42.6 12.0 %collective-permute-start.6 = (bf16[8,64,128]{2,1,0:T(8,128)(2,1)S(1)}, bf16[8,64,128]{2,1,0:T(8,128)(2,1)S(1)}, u32[]{:S(2)}, u32[]{:S(2)}) collective-permute-start(bf16[8,64,128]{2,1,0:T(8,128)(2,1)S(1)} %constant_dynamic-update-slice_fusion.refs_0_), channel_id=1, source_target_pairs={{0,16},{8,24},{16,0},{24,8},{1,17},{9,25},{17,1},{25,9},{2,18},{10... | collective-permute-start | bytes 393224 | tf_op jit(solution)/shard_map/ppermute | solution.py:234
  43.1 11.5 %collective-permute-start.5 = (bf16[8,64,128]{2,1,0:T(8,128)(2,1)S(1)}, bf16[8,64,128]{2,1,0:T(8,128)(2,1)S(1)}, u32[]{:S(2)}, u32[]{:S(2)}) collective-permute-start(bf16[8,64,128]{2,1,0:T(8,128)(2,1)S(1)} %constant_dynamic-update-slice_fusion.refs_0_), channel_id=1, source_target_pairs={{0,8},{8,0},{16,24},{24,16},{1,9},{9,1},{17,25},{25,17},{2,10},{10... | collective-permute-start | bytes 393224 | tf_op jit(solution)/shard_map/ppermute | solution.py:234
  55.3 5.1 %copy-start.2 = (s32[2,97]{1,0:T(2,128)S(1)}, s32[2,97]{1,0:T(2,128)}, u32[]{:S(2)}) copy-start(s32[2,97]{1,0:T(2,128)} %constant.2.clone.starts_hbm) | copy-start | bytes 2332

commit v4 on v3

--- a/solution.py
+++ b/solution.py
@@ -21,12 +21,25 @@
     def __init__(self, n_row, n_col, blk):
         self.n_row, self.n_col, self.blk = n_row, n_col, blk
         self.ndev = n_row * n_col
+        self.line = n_col // 2
         chips = self.ndev // 2
         self.full = min(self.ndev, PANEL)
         self.shared = min(chips, PANEL - self.full)
         self.extra = PANEL - self.full - self.shared
         self.half = blk // 2
         self.rows = blk + (self.half if self.shared else 0)
+        self.slots = self.n_row + self.extra if self.shared else 0
+
+    def send_slot(self, at, chip):
+        u = jnp.where(at < PANEL - 1, at + 1, at + 1 - PANEL)
+        if not self.shared:
+            return u
+        apart = jnp.bitwise_xor(u - self.full, chip)
+        shift = self.line.bit_length() - 1
+        plane, line = jnp.right_shift(apart, shift), jnp.bitwise_and(apart, self.line - 1)
+        beyond = u - self.full - self.shared
+        slot = jnp.where(beyond < 0, line * self.slots + plane, self.n_row + beyond)
+        return jnp.where(u < self.full, u, self.ndev + slot)
 
     def starts(self):
         table = np.zeros((2, 2 * PANEL - 1), np.int32)
@@ -43,7 +56,7 @@
         return table
 
     def slot(self, apart):
-        return apart % 2 * (self.n_col // 2) + apart // 2
+        return apart % 2 * self.line + apart // 2
 
 
 def kept_lanes(rows, u, shift, blk):
@@ -56,35 +69,38 @@
     return jnp.sum(jnp.where(lane // blk == tile, has, 0.0), axis=0, keepdims=True)
 
 
-def pack_kernel(plan, x_hbm, rows_hbm, shift_hbm, starts_hbm, out_ref, *refs):
-    *extra_refs, x_ref, rows_ref, shift_ref, starts_ref, stage, sems = refs
+def pack_kernel(plan, x_hbm, rows_hbm, shift_hbm, *refs):
+    *out_refs, x_ref, rows_ref, shift_ref, stage, sems = refs
     row_id, col_id = lax.axis_index("row"), lax.axis_index("col")
-    blk, half, total = plan.blk, plan.half, plan.ndev * plan.rows
+    blk, ndev, slots = plan.blk, plan.ndev, plan.slots
+    chip = row_id * plan.line + col_id // 2
     copies = [
         pltpu.make_async_copy(shift_hbm, shift_ref, sems.at[0]),
         pltpu.make_async_copy(rows_hbm.at[pl.ds(2 * row_id, 2)], rows_ref, sems.at[1]),
-        pltpu.make_async_copy(starts_hbm, starts_ref, sems.at[2]),
-        pltpu.make_async_copy(x_hbm.at[0], x_ref.at[0], sems.at[3]),
-        pltpu.make_async_copy(x_hbm.at[1], x_ref.at[1], sems.at[4]),
+        pltpu.make_async_copy(x_hbm.at[0], x_ref.at[0], sems.at[2]),
+        pltpu.make_async_copy(x_hbm.at[1], x_ref.at[1], sems.at[3]),
     ]
     for copy in copies:
         copy.start()
     stage[...] = jnp.zeros_like(stage)
-    for copy in copies[:3]:
+    for copy in copies[:2]:
         copy.wait()
     for p in range(2):
-        copies[3 + p].wait()
+        copies[2 + p].wait()
         base = PANEL - 1 - shift_ref[2 * row_id + p]
         lanes = slice(p * blk, (p + 1) * blk)
         for e in range(rows_ref.shape[2]):
-            at = rows_ref[p, col_id, e] + base
-            block = x_ref[p, :, e * blk : (e + 1) * blk]
-            for h in range(2):
-                start = pl.multiple_of(starts_ref[h, at], half)
-                stage[pl.ds(start, half), lanes] = block[h * half : (h + 1) * half]
-    copies = [pltpu.make_async_copy(stage.at[pl.ds(0, total)], out_ref, sems.at[0])]
-    for ref in extra_refs:
-        copies.append(pltpu.make_async_copy(stage.at[pl.ds(total, plan.extra * blk)], ref, sems.at[1]))
+            slot = plan.send_slot(rows_ref[p, col_id, e] + base, chip)
+            stage[slot, :, lanes] = x_ref[p, :, e * blk : (e + 1) * blk]
+    for k in range(plan.extra):
+        block = stage[ndev + plan.n_row + k]
+        for i in range(1, plan.line):
+            stage[ndev + i * slots + plan.n_row + k] = block
+    spans = [(0, ndev)] + [(ndev + i * slots, slots) for i in range(len(out_refs) - 1)]
+    copies = [
+        pltpu.make_async_copy(stage.at[pl.ds(first, size)], ref, sems.at[i])
+        for i, ((first, size), ref) in enumerate(zip(spans, out_refs))
+    ]
     for copy in copies:
         copy.start()
     for copy in copies:
@@ -125,12 +141,18 @@
             out_ref[to], out_ref[to + 1] = split_pair(upper, lower)
 
 
-def full_kernel(plan, keep_ref, y_ref, out_ref, m_ref, s_ref):
+def full_kernel(plan, keep_ref, y_ref, *refs):
+    *shared_refs, out_hbm, m_ref, s_ref, res_ref, sems = refs
     blk, n_col = plan.blk, plan.n_col
+    copies = [
+        pltpu.make_async_copy(ref, out_hbm.at[:, pl.ds(blk, plan.half)], sems.at[1]) for ref in shared_refs
+    ]
+    for copy in copies:
+        copy.start()
     for r in range(plan.n_row):
         for j in range(n_col // 2):
             src = r * n_col + 2 * j
-            first, second = split_pair(y_ref[src, :blk], y_ref[src + 1, :blk])
+            first, second = split_pair(y_ref[src], y_ref[src + 1])
             lanes = slice(2 * j * blk, (2 * j + 2) * blk)
             m_ref[2 * r * blk : (2 * r + 1) * blk, lanes] = first
             m_ref[(2 * r + 1) * blk : (2 * r + 2) * blk, lanes] = second
@@ -139,36 +161,55 @@
     for panel in range(2 * plan.n_row):
         at = slice(panel * blk, (panel + 1) * blk)
         s_ref[at] = jnp.where(keep_ref[0, panel : panel + 1] > 0, s[at], 0.0).astype(jnp.bfloat16)
-    res = purify(s_ref[...], m).astype(jnp.bfloat16)
-    put_blocks(plan, res, blk, out_ref)
-
-
-def shared_kernel(plan, keep_ref, own_ref, far_ref, part_ref, out_hbm, m_ref, s_ref, o_ref, res_ref, sems):
-    blk, half, n_col = plan.blk, plan.half, plan.n_col
-    first_core = lax.axis_index("col") % 2 == 0
-    part_copy = pltpu.make_async_copy(part_ref, out_hbm.at[:, pl.ds(0, blk)], sems.at[0])
-    part_copy.start()
-    for r in range(plan.n_row):
+    put_blocks(plan, purify(s_ref[...], m).astype(jnp.bfloat16), blk, res_ref)
+    copies.append(pltpu.make_async_copy(res_ref, out_hbm.at[:, pl.ds(0, blk)], sems.at[0]))
+    copies[-1].start()
+    for copy in copies:
+        copy.wait()
+
+
+def regroup_kernel(plan, *refs):
+    line, plane, extra = refs[: plan.line], refs[plan.line : plan.line + plan.n_row], refs[plan.line + plan.n_row :]
+    for i, sent in enumerate(line):
+        for r, ref in enumerate(plane):
+            ref[i] = sent[r]
+        for ref in extra:
+            for k in range(plan.extra):
+                ref[k * plan.line + i] = sent[plan.n_row + k]
+
+
+def shared_kernel(plan, keep_ref, own_ref, far_ref, out_ref, m_ref, s_ref, o_ref):
+    n_row, n_col, blk, half = plan.n_row, plan.n_col, plan.blk, plan.half
+    row_id, col_id = lax.axis_index("row"), lax.axis_index("col")
+    first_core = col_id % 2 == 0
+    for r in range(n_row):
+        panel = 2 * jnp.bitwise_xor(row_id, r)
+        start = pl.multiple_of(panel * blk, 2 * blk)
         for j in range(n_col // 2):
-            src = r * n_col + 2 * j
             lanes = slice(2 * j * blk, (2 * j + 2) * blk)
-            own = split_pair(own_ref[src], own_ref[src + 1])
-            far = split_pair(far_ref[src], far_ref[src + 1])
+            at = r * plan.line + jnp.bitwise_xor(col_id // 2, j)
+            own, far = own_ref[at], far_ref[at]
+            pair = split_pair(jnp.where(first_core, own, far), jnp.where(first_core, far, own))
+            m_ref[pl.ds(start, 2 * blk), lanes] = jnp.concatenate(pair, axis=0)
             for p in range(2):
-                at = (2 * r + p) * blk
-                m_ref[at : at + half, lanes] = jnp.where(first_core, own[p], far[p])
-                m_ref[at + half : at + blk, lanes] = jnp.where(first_core, far[p], own[p])
-                o_ref[(2 * r + p) * half : (2 * r + p + 1) * half, lanes] = own[p]
+                at = slice((2 * r + p) * half, (2 * r + p + 1) * half)
+                o_ref[at, lanes] = jnp.where(first_core, pair[p][:half], pair[p][half:])
     m = m_ref[...]
     s = dot(o_ref[...], m)
-    for panel in range(2 * plan.n_row):
-        at = slice(panel * half, (panel + 1) * half)
-        s_ref[at] = jnp.where(keep_ref[1, panel : panel + 1] > 0, s[at], 0.0).astype(jnp.bfloat16)
-    put_blocks(plan, purify(s_ref[...], m).astype(jnp.bfloat16), half, res_ref)
-    res_copy = pltpu.make_async_copy(res_ref, out_hbm.at[:, pl.ds(blk, half)], sems.at[1])
-    res_copy.start()
-    part_copy.wait()
-    res_copy.wait()
+    for r in range(n_row):
+        panel = 2 * jnp.bitwise_xor(row_id, r)
+        for p in range(2):
+            at = slice((2 * r + p) * half, (2 * r + p + 1) * half)
+            keep = keep_ref[1, pl.ds(panel + p, 1)]
+            s_ref[at] = jnp.where(keep > 0, s[at], 0.0).astype(jnp.bfloat16)
+    res = purify(s_ref[...], m).astype(jnp.bfloat16)
+    for r in range(n_row):
+        for j in range(n_col // 2):
+            lanes = slice(2 * j * blk, (2 * j + 2) * blk)
+            upper = res[2 * r * half : (2 * r + 1) * half, lanes]
+            lower = res[(2 * r + 1) * half : (2 * r + 2) * half, lanes]
+            to = jnp.bitwise_xor(row_id, r) * n_col + 2 * j
+            out_ref[to], out_ref[to + 1] = split_pair(upper, lower)
 
 
 def extra_kernel(plan, keep_ref, *refs):
@@ -246,22 +287,26 @@
     square = pltpu.VMEM((size, size), bf16)
     tables = [pltpu.SMEM((2, npan, rh), jnp.int32), pltpu.SMEM((npan,), jnp.int32)]
     starts = jnp.asarray(plan.starts())
-    tables.append(pltpu.SMEM(starts.shape, jnp.int32))
-    stage = pltpu.VMEM((ndev * rows + plan.extra * blk, 2 * blk), bf16)
-    moved = jax.ShapeDtypeStruct((ndev, rows, 2 * blk), bf16)
-
-    flat = jax.ShapeDtypeStruct((ndev * rows, 2 * blk), bf16)
-    extra_shapes = [jax.ShapeDtypeStruct((plan.extra * blk, 2 * blk), bf16)] if plan.extra else []
-    packed, *extra = pl.pallas_call(
+
+    def blocks(*shape):
+        return jax.ShapeDtypeStruct((*shape, 2 * blk), bf16)
+
+    shapes = [blocks(ndev, blk)] + ([blocks(plan.slots, blk)] * plan.line if plan.shared else [])
+    packed, *line = pl.pallas_call(
         functools.partial(pack_kernel, plan),
-        out_shape=[flat] + extra_shapes,
-        in_specs=[HBM] * 4,
-        out_specs=[HBM] * (1 + len(extra_shapes)),
-        scratch_shapes=[pltpu.VMEM(density.shape, bf16)] + tables + [stage, pltpu.SemaphoreType.DMA((5,))],
+        out_shape=shapes,
+        in_specs=[HBM] * 3,
+        out_specs=[HBM] * len(shapes),
+        scratch_shapes=[pltpu.VMEM(density.shape, bf16)]
+        + tables
+        + [
+            pltpu.VMEM((ndev + plan.line * plan.slots, blk, 2 * blk), bf16),
+            pltpu.SemaphoreType.DMA((max(4, len(shapes)),)),
+        ],
         compiler_params=PACK_PARAMS,
         name="pack",
-    )(density, density_rows, panel_shift, starts)
-    y = lax.all_to_all(packed.reshape(moved.shape), both, 0, 0, tiled=True)
+    )(density, density_rows, panel_shift)
+    y = lax.all_to_all(packed, both, 0, 0, tiled=True)
     sets = 1 + (1 if plan.shared else 0) + plan.extra
     keep = pl.pallas_call(
         functools.partial(mask_kernel, plan),
@@ -271,17 +316,39 @@
         compiler_params=PARAMS,
         name="masks",
     )(panel_shift, square_rows)
+    shared, extra = [], []
+    if plan.shared:
+        line = line[:1] + [swapped(sent, "col", 2 * i) for i, sent in enumerate(line) if i]
+        plane = pl.pallas_call(
+            functools.partial(regroup_kernel, plan),
+            out_shape=[blocks(plan.line, blk)] * n_row + [blocks(plan.line * plan.extra, blk)] * min(1, plan.extra),
+            in_specs=[VMEM] * plan.line,
+            out_specs=[VMEM] * (n_row + min(1, plan.extra)),
+            compiler_params=PARAMS,
+            cost_estimate=pl.CostEstimate(flops=20_000_000_000, bytes_accessed=0, transcendentals=0),
+            name="regroup",
+        )(*line)
+        plane, line = plane[:n_row], plane[n_row:]
+        own = jnp.concatenate([plane[0]] + [swapped(sent, "row", r) for r, sent in enumerate(plane) if r])
+        far = swapped(own, "col", 1)
+        shared = pl.pallas_call(
+            functools.partial(shared_kernel, plan),
+            out_shape=blocks(ndev, plan.half),
+            in_specs=[VMEM] * 3,
+            out_specs=VMEM,
+            scratch_shapes=[square] + [pltpu.VMEM((size // 2, size), bf16)] * 2,
+            compiler_params=PARAMS,
+            name="shared",
+        )(keep, own, far)
+        y, keep, shared, *line = lax.optimization_barrier((y, keep, shared, *line))
+        shared = [shared]
     if plan.extra:
-        extra = extra[0][None]
-        line = [extra] + [swapped(extra, "col", by) for by in range(2, n_col, 2)]
-        y, keep, *line = lax.optimization_barrier((y, keep, *line))
-        line = jnp.concatenate(line, axis=0)
-        line = jnp.concatenate([line, swapped(line, "col", 1)], axis=0)
-        plane = [line] + [swapped(line, "row", by) for by in range(1, n_row)]
+        line = jnp.concatenate([line[0], swapped(line[0], "col", 1)])
+        plane = [line] + [swapped(line, "row", r) for r in range(1, n_row)]
         extra = [
             pl.pallas_call(
                 functools.partial(extra_kernel, plan),
-                out_shape=extra_shapes[0],
+                out_shape=blocks(plan.extra * blk),
                 in_specs=[VMEM] * (1 + n_row),
                 out_specs=VMEM,
                 scratch_shapes=[square, pltpu.VMEM((2 * blk, size), bf16)],
@@ -289,41 +356,33 @@
                 name="extra",
             )(keep, *plane)
         ]
-    if plan.shared:
-        own = y[:, blk:]
-        far = swapped(own, "col", 1)
     out = pl.pallas_call(
         functools.partial(full_kernel, plan),
-        out_shape=jax.ShapeDtypeStruct((ndev, blk, 2 * blk), bf16),
-        in_specs=[VMEM] * 2,
-        out_specs=VMEM,
-        scratch_shapes=[square] * 2,
+        out_shape=blocks(ndev, rows),
+        in_specs=[VMEM] * (2 + len(shared)),
+        out_specs=HBM,
+        scratch_shapes=[square] * 2 + [pltpu.VMEM((ndev, blk, 2 * blk), bf16), pltpu.SemaphoreType.DMA((2,))],
         compiler_params=PARAMS,
         cost_estimate=pl.CostEstimate(flops=4 * size**3, bytes_accessed=4 * ndev * rows * 2 * blk, transcendentals=0),
         name="full",
-    )(keep, y)
-    if plan.shared:
-        out = pl.pallas_call(
-            functools.partial(shared_kernel, plan),
-            out_shape=moved,
-            in_specs=[VMEM] * 4,
-            out_specs=HBM,
-            scratch_shapes=[square]
-            + [pltpu.VMEM((size // 2, size), bf16)] * 2
-            + [pltpu.VMEM((ndev, plan.half, 2 * blk), bf16), pltpu.SemaphoreType.DMA((2,))],
-            compiler_params=PARAMS,
-            name="shared",
-        )(keep, own, far, out)
+    )(keep, y, *shared)
     ret = lax.all_to_all(out, both, 0, 0, tiled=True)
+    stage = pltpu.VMEM((ndev * rows + plan.extra * blk, 2 * blk), bf16)
     return pl.pallas_call(
         functools.partial(unpack_kernel, plan),
         out_shape=jax.ShapeDtypeStruct(density.shape, jnp.float32),
         in_specs=[HBM] * 3 + [VMEM] * (1 + len(extra)),
         out_specs=HBM,
-        scratch_shapes=tables + [stage, pltpu.VMEM(density.shape, jnp.float32), pltpu.SemaphoreType.DMA((5,))],
+        scratch_shapes=tables
+        + [
+            pltpu.SMEM(starts.shape, jnp.int32),
+            stage,
+            pltpu.VMEM(density.shape, jnp.float32),
+            pltpu.SemaphoreType.DMA((5,)),
+        ],
         compiler_params=PARAMS,
         name="unpack",
-    )(square_rows, panel_shift, starts, ret.reshape(flat.shape), *extra)
+    )(square_rows, panel_shift, starts, ret.reshape(ndev * rows, 2 * blk), *extra)
 
 
 def solution(mesh):

time: 62.7 us -> 59.2 us (0.944)
  waiting for transfers between devices: 35.3 us -> 28.5 us
  starting transfers between devices: 18.7 us -> 21.8 us
    ppermute x8 -> x11, waiting for transfers between devices: 29.6 us -> 19.8 us  [swapped(): lax.ppermute(shard, axis, [(i, i ^ by) for i in range(lax.axis_size(axis))])]
    ppermute x8 -> x11, starting transfers between devices: 8.4 us -> 13 us  [swapped(): lax.ppermute(shard, axis, [(i, i ^ by) for i in range(lax.axis_size(axis))])]
    all_to_all x1, waiting for transfers between devices: 0.64 us -> 3.48 us  [body(): y = lax.all_to_all(packed, both, 0, 0, tiled=True)]
    all_to_all x1, starting transfers between devices: 7.3 us -> 6.07 us  [body(): y = lax.all_to_all(packed, both, 0, 0, tiled=True)]
    pallas_call x4 -> x5, Pallas kernels: 5.49 us -> 5.7 us  [the longest x1 2.39 us: body(): pl.pallas_call(functools.partial(pack_kernel, plan), out_shape=shapes, in...]
  transfers between devices with their start and end apart: 10 -> 13, of which waited for: 8 -> 10; matrix products, arithmetic and copies ran while one was open for 0% -> 0% of each run, Pallas kernels for 4% -> 4%
where the time goes in v4:
time: 59.2 us; the launch traced here: 58.8 us
  waiting for transfers between devices  28.5 us (48%)
  starting transfers between devices  21.8 us (37%)
  Pallas kernels  8.36 us (14%)
    ppermute x11, waiting for transfers between devices, swapped(): lax.ppermute(shard, axis, [(i, i ^ by) for i in range(lax.axis_size(axis))])  19.8 us
    ppermute x11, starting transfers between devices, swapped(): lax.ppermute(shard, axis, [(i, i ^ by) for i in range(lax.axis_size(axis))])  13 us
    all_to_all x1, starting transfers between devices, body(): y = lax.all_to_all(packed, both, 0, 0, tiled=True)  6.07 us
    all_to_all x1, waiting for transfers between devices, body(): ret = lax.all_to_all(out, both, 0, 0, tiled=True)  5.21 us
    all_to_all x1, waiting for transfers between devices, body(): y = lax.all_to_all(packed, both, 0, 0, tiled=True)  3.48 us
    all_to_all x1, starting transfers between devices, body(): ret = lax.all_to_all(out, both, 0, 0, tiled=True)  2.64 us
    pallas_call x1, Pallas kernels, body(): pl.pallas_call(functools.partial(pack_kernel, plan), out_shape=shapes, in...  2.39 us
    pallas_call x1, Pallas kernels, body(): pl.pallas_call(functools.partial(unpack_kernel, plan), out_shape=jax.Shap...  1.92 us
  transfers between devices with their start and end apart: 13, of which 10 were waited for; matrix products, arithmetic and copies ran while one was open for 0% of the time, Pallas kernels for 4%

profile of v4, /device:TPU:0, one launch (start us, length us, event | category | flops | bytes accessed | tf_op | source)
XLA Modules:
  0.0 58.8 jit_solution(6601131368917748645)
XLA Ops:
  0.0 2.4 %pack.1 = (bf16[32,64,128]{2,1,0:T(8,128)(2,1)}, bf16[5,64,128]{2,1,0:T(8,128)(2,1)}, bf16[5,64,128]{2,1,0:T(8,128)(2,1)}, bf16[5,64,128]{2,1,0:T(8,128)(2,1)}, bf16[5,64,128]{2,1,0:T(8,128)(2,1)}) custom-call(bf16[2,64,2048]{2,1,0:T(8,128)(2,1)} %x_hbm.1, s32[8,8,32]{2,1,0:T(8,128)} %rows_hbm.1, s32[8]{0:T(128)} %shift_hbm.3), custom_call_target="tpu_custom_call" | custom-call | tf_op jit(solution)/shard_map/pack/pallas_call | solution.py:295
  2.4 3.1 %collective-permute-start = (bf16[5,64,128]{2,1,0:T(8,128)(2,1)}, bf16[5,64,128]{2,1,0:T(8,128)(2,1)S(1)}, u32[]{:S(2)}, u32[]{:S(2)}) collective-permute-start(bf16[5,64,128]{2,1,0:T(8,128)(2,1)} %get-tuple-element.21), channel_id=1, source_target_pairs={{0,2},{1,3},{2,0},{3,1},{4,6},{5,7},{6,4},{7,5},{8,10},{9,11},{10,... | collective-permute-start | bytes 245768 | tf_op jit(solution)/shard_map/ppermute | solution.py:275
  5.5 2.6 %collective-permute-start.1 = (bf16[5,64,128]{2,1,0:T(8,128)(2,1)}, bf16[5,64,128]{2,1,0:T(8,128)(2,1)S(1)}, u32[]{:S(2)}, u32[]{:S(2)}) collective-permute-start(bf16[5,64,128]{2,1,0:T(8,128)(2,1)} %get-tuple-element.22), channel_id=1, source_target_pairs={{0,4},{1,5},{2,6},{3,7},{4,0},{5,1},{6,2},{7,3},{8,12},{9,13},{10,... | collective-permute-start | bytes 245768 | tf_op jit(solution)/shard_map/ppermute | solution.py:275
  8.1 0.0 collective-permute-start.2
  8.1 0.0 copy-start.3
  8.1 6.1 %all-to-all-start = ((bf16[32,64,128]{2,1,0:T(8,128)(2,1)}), bf16[32,64,128]{2,1,0:T(8,128)(2,1)S(1)}, u32[]{:S(2)}, u32[]{:S(2)}) async-start(bf16[32,64,128]{2,1,0:T(8,128)(2,1)} %get-tuple-element.19), calls=%async_computation | async-start | bytes 1048576 | tf_op jit(solution)/shard_map/all_to_all | solution.py:309
  14.2 0.0 collective-permute-done.refs_1_
  14.2 0.7 %collective-permute-done.1.refs_2_ = bf16[5,64,128]{2,1,0:T(8,128)(2,1)S(1)} collective-permute-done((bf16[5,64,128]{2,1,0:T(8,128)(2,1)}, bf16[5,64,128]{2,1,0:T(8,128)(2,1)S(1)}, u32[]{:S(2)}, u32[]{:S(2)}) %collective-permute-start.1) | collective-permute-done | bytes 81952 | tf_op jit(solution)/shard_map/ppermute | solution.py:275
  14.9 0.0 collective-permute-done.2.refs_3_
  14.9 0.0 copy-done.3
  14.9 1.6 %collective-permute-start.3 = (bf16[4,64,128]{2,1,0:T(8,128)(2,1)S(1)}, bf16[4,64,128]{2,1,0:T(8,128)(2,1)S(1)}, u32[]{:S(2)}, u32[]{:S(2)}) collective-permute-start(bf16[4,64,128]{2,1,0:T(8,128)(2,1)S(1)} %get-tuple-element.25), channel_id=1, source_target_pairs={{0,8},{8,0},{16,24},{24,16},{1,9},{9,1},{17,25},{25,17},{2,10},{10... | collective-permute-start | bytes 196616 | tf_op jit(solution)/shard_map/ppermute | solution.py:275
  16.5 1.5 %collective-permute-start.4 = (bf16[4,64,128]{2,1,0:T(8,128)(2,1)S(1)}, bf16[4,64,128]{2,1,0:T(8,128)(2,1)S(1)}, u32[]{:S(2)}, u32[]{:S(2)}) collective-permute-start(bf16[4,64,128]{2,1,0:T(8,128)(2,1)S(1)} %get-tuple-element.26), channel_id=1, source_target_pairs={{0,16},{8,24},{16,0},{24,8},{1,17},{9,25},{17,1},{25,9},{2,18},{10... | collective-permute-start | bytes 196616 | tf_op jit(solution)/shard_map/ppermute | solution.py:275
  18.0 0.5 collective-permute-start.5
  18.5 3.8 %collective-permute-done.3 = bf16[4,64,128]{2,1,0:T(8,128)(2,1)S(1)} collective-permute-done((bf16[4,64,128]{2,1,0:T(8,128)(2,1)S(1)}, bf16[4,64,128]{2,1,0:T(8,128)(2,1)S(1)}, u32[]{:S(2)}, u32[]{:S(2)}) %collective-permute-start.3) | collective-permute-done | bytes 65568 | tf_op jit(solution)/shard_map/ppermute | solution.py:275
  22.3 0.4 collective-permute-done.4
  22.6 0.0 copy-start
  22.7 0.0 copy-start.1
  22.7 1.9 %collective-permute-done.5 = bf16[4,64,128]{2,1,0:T(8,128)(2,1)S(1)} collective-permute-done((bf16[4,64,128]{2,1,0:T(8,128)(2,1)S(1)}, bf16[4,64,128]{2,1,0:T(8,128)(2,1)S(1)}, u32[]{:S(2)}, u32[]{:S(2)}) %collective-permute-start.5) | collective-permute-done | bytes 65568 | tf_op jit(solution)/shard_map/ppermute | solution.py:275
  24.6 0.1 collective-permute-start.6
  24.7 0.0 copy-done
  24.7 0.0 copy-done.1
  24.7 0.7 %masks.1.keep_ref = f32[3,8,512]{2,1,0:T(8,128)S(1)} custom-call(s32[8]{0:T(128)S(1)} %copy-done.1, s32[8,8,32]{2,1,0:T(8,128)S(1)} %copy-done), custom_call_target="tpu_custom_call" | custom-call | tf_op jit(solution)/shard_map/masks/pallas_call | solution.py:311
  25.5 0.8 %collective-permute-done.6.far_ref = bf16[16,64,128]{2,1,0:T(8,128)(2,1)S(1)} collective-permute-done((bf16[16,64,128]{2,1,0:T(8,128)(2,1)S(1)}, bf16[16,64,128]{2,1,0:T(8,128)(2,1)S(1)}, u32[]{:S(2)}, u32[]{:S(2)}) %collective-permute-start.6) | collective-permute-done | bytes 262176 | tf_op jit(solution)/shard_map/ppermute | solution.py:275
  26.2 0.8 %shared.1.refs_0_ = bf16[32,32,128]{2,1,0:T(8,128)(2,1)S(1)} custom-call(f32[3,8,512]{2,1,0:T(8,128)S(1)} %masks.1.keep_ref, bf16[16,64,128]{2,1,0:T(8,128)(2,1)S(1)} %constant_dynamic-update-slice_fusion.own_ref, bf16[16,64,128]{2,1,0:T(8,128)(2,1)S(1)} %collective-permute-done.6.far_ref), custom_call_target="tpu_custom_call" | custom-call | tf_op jit(solution)/shard_map/shared/pallas_call | solution.py:334
  27.0 3.5 %all-to-all-done.y_ref = bf16[32,64,128]{2,1,0:T(8,128)(2,1)S(1)} async-done(((bf16[32,64,128]{2,1,0:T(8,128)(2,1)}), bf16[32,64,128]{2,1,0:T(8,128)(2,1)S(1)}, u32[]{:S(2)}, u32[]{:S(2)}) %all-to-all-start) | async-done | bytes 524320 | tf_op jit(solution)/shard_map/all_to_all | solution.py:309
  30.5 1.8 %full.1 = bf16[32,96,128]{2,1,0:T(8,128)(2,1)} custom-call(f32[3,8,512]{2,1,0:T(8,128)S(1)} %masks.1.keep_ref, bf16[32,64,128]{2,1,0:T(8,128)(2,1)S(1)} %all-to-all-done.y_ref, bf16[32,32,128]{2,1,0:T(8,128)(2,1)S(1)} %shared.1.refs_0_), custom_call_target="tpu_custom_call" | custom-call | flops 536870912 | bytes 1572864 | tf_op jit(solution)/shard_map/full/pallas_call | solution.py:359
  32.3 2.6 %all-to-all-start.1 = ((bf16[32,96,128]{2,1,0:T(8,128)(2,1)}), bf16[32,96,128]{2,1,0:T(8,128)(2,1)S(1)}, u32[]{:S(2)}, u32[]{:S(2)}) async-start(bf16[32,96,128]{2,1,0:T(8,128)(2,1)} %full.1), calls=%async_computation.1 | async-start | bytes 1572864 | tf_op jit(solution)/shard_map/all_to_all | solution.py:369
  35.0 0.2 collective-permute-start.7
  35.1 1.1 %collective-permute-done.7 = bf16[4,64,128]{2,1,0:T(8,128)(2,1)S(1)} collective-permute-done((bf16[4,64,128]{2,1,0:T(8,128)(2,1)S(1)}, bf16[4,64,128]{2,1,0:T(8,128)(2,1)S(1)}, u32[]{:S(2)}, u32[]{:S(2)}) %collective-permute-start.7) | collective-permute-done | bytes 65568 | tf_op jit(solution)/shard_map/ppermute | solution.py:275
  36.3 2.6 %collective-permute-start.10 = (bf16[8,64,128]{2,1,0:T(8,128)(2,1)S(1)}, bf16[8,64,128]{2,1,0:T(8,128)(2,1)S(1)}, u32[]{:S(2)}, u32[]{:S(2)}) collective-permute-start(bf16[8,64,128]{2,1,0:T(8,128)(2,1)S(1)} %constant_dynamic-update-slice_fusion.4.refs_0_), channel_id=1, source_target_pairs={{0,24},{8,16},{16,8},{24,0},{1,25},{9,17},{17,9},{25,1},{2,26},{10... | collective-permute-start | bytes 393224 | tf_op jit(solution)/shard_map/ppermute | solution.py:275
  38.9 0.5 collective-permute-start.9
  39.5 0.4 collective-permute-start.8
  39.8 7.9 %collective-permute-done.10.refs_3_ = bf16[8,64,128]{2,1,0:T(8,128)(2,1)S(1)} collective-permute-done((bf16[8,64,128]{2,1,0:T(8,128)(2,1)S(1)}, bf16[8,64,128]{2,1,0:T(8,128)(2,1)S(1)}, u32[]{:S(2)}, u32[]{:S(2)}) %collective-permute-start.10) | collective-permute-done | bytes 131104 | tf_op jit(solution)/shard_map/ppermute | solution.py:275
  47.8 3.2 %collective-permute-done.9.refs_2_ = bf16[8,64,128]{2,1,0:T(8,128)(2,1)S(1)} collective-permute-done((bf16[8,64,128]{2,1,0:T(8,128)(2,1)S(1)}, bf16[8,64,128]{2,1,0:T(8,128)(2,1)S(1)}, u32[]{:S(2)}, u32[]{:S(2)}) %collective-permute-start.9) | collective-permute-done | bytes 131104 | tf_op jit(solution)/shard_map/ppermute | solution.py:275
  51.0 0.0 collective-permute-done.8.refs_1_
  51.0 0.7 %extra.1.refs_0_ = bf16[64,128]{1,0:T(8,128)(2,1)S(1)} custom-call(f32[3,8,512]{2,1,0:T(8,128)S(1)} %masks.1.keep_ref, bf16[8,64,128]{2,1,0:T(8,128)(2,1)S(1)} %constant_dynamic-update-slice_fusion.4.refs_0_, bf16[8,64,128]{2,1,0:T(8,128)(2,1)S(1)} %collective-permute-done.8.refs_1_, bf16[8,64,128]{2,1,0:T(8,128)(2,1)S(1)} %collective-permute-done.9.refs_2_, ...), custom_call_target="tpu_custom_call" | custom-call | tf_op jit(solution)/shard_map/extra/pallas_call | solution.py:349
  51.7 0.0 copy-start.2
  51.7 5.2 %all-to-all-done.1 = bf16[32,96,128]{2,1,0:T(8,128)(2,1)S(1)} async-done(((bf16[32,96,128]{2,1,0:T(8,128)(2,1)}), bf16[32,96,128]{2,1,0:T(8,128)(2,1)S(1)}, u32[]{:S(2)}, u32[]{:S(2)}) %all-to-all-start.1) | async-done | bytes 786464 | tf_op jit(solution)/shard_map/all_to_all | solution.py:369
  56.9 0.0 copy-done.2
  56.9 1.9 %unpack.1 = f32[2,64,2048]{2,1,0:T(8,128)} custom-call(s32[8,8,32]{2,1,0:T(8,128)S(1)} %copy-done, s32[8]{0:T(128)S(1)} %copy-done.1, s32[2,97]{1,0:T(2,128)S(1)} %copy-done.2, bf16[3072,128]{1,0:T(8,128)(2,1)S(1)} %bitcast.1, bf16[64,128]{1,0:T(8,128)(2,1)S(1)} %extra.1.refs_0_), custom_call_target="tpu_custom_call" | custom-call | tf_op jit(solution)/shard_map/unpack/pallas_call | solution.py:371
  (7 shorter events, 0.1 us)
Async XLA Ops:
  2.4 11.8 %collective-permute-start = (bf16[5,64,128]{2,1,0:T(8,128)(2,1)}, bf16[5,64,128]{2,1,0:T(8,128)(2,1)S(1)}, u32[]{:S(2)}, u32[]{:S(2)}) collective-permute-start(bf16[5,64,128]{2,1,0:T(8,128)(2,1)} %get-tuple-element.21), channel_id=1, source_target_pairs={{0,2},{1,3},{2,0},{3,1},{4,6},{5,7},{6,4},{7,5},{8,10},{9,11},{10,... | collective-permute-start | bytes 245768 | tf_op jit(solution)/shard_map/ppermute | solution.py:275
  5.5 9.4 %collective-permute-start.1 = (bf16[5,64,128]{2,1,0:T(8,128)(2,1)}, bf16[5,64,128]{2,1,0:T(8,128)(2,1)S(1)}, u32[]{:S(2)}, u32[]{:S(2)}) collective-permute-start(bf16[5,64,128]{2,1,0:T(8,128)(2,1)} %get-tuple-element.22), channel_id=1, source_target_pairs={{0,4},{1,5},{2,6},{3,7},{4,0},{5,1},{6,2},{7,3},{8,12},{9,13},{10,... | collective-permute-start | bytes 245768 | tf_op jit(solution)/shard_map/ppermute | solution.py:275
  8.1 6.8 %collective-permute-start.2 = (bf16[5,64,128]{2,1,0:T(8,128)(2,1)}, bf16[5,64,128]{2,1,0:T(8,128)(2,1)S(1)}, u32[]{:S(2)}, u32[]{:S(2)}) collective-permute-start(bf16[5,64,128]{2,1,0:T(8,128)(2,1)} %get-tuple-element.23), channel_id=1, source_target_pairs={{0,6},{1,7},{2,4},{3,5},{4,2},{5,3},{6,0},{7,1},{8,14},{9,15},{10,... | collective-permute-start | bytes 245768 | tf_op jit(solution)/shard_map/ppermute | solution.py:275
  8.1 6.8 %copy-start.3 = (bf16[5,64,128]{2,1,0:T(8,128)(2,1)S(1)}, bf16[5,64,128]{2,1,0:T(8,128)(2,1)}, u32[]{:S(2)}) copy-start(bf16[5,64,128]{2,1,0:T(8,128)(2,1)} %get-tuple-element.20.refs_0_) | copy-start | bytes 245764
  8.1 22.4 %all-to-all-start = ((bf16[32,64,128]{2,1,0:T(8,128)(2,1)}), bf16[32,64,128]{2,1,0:T(8,128)(2,1)S(1)}, u32[]{:S(2)}, u32[]{:S(2)}) async-start(bf16[32,64,128]{2,1,0:T(8,128)(2,1)} %get-tuple-element.19), calls=%async_computation | async-start | bytes 1048576 | tf_op jit(solution)/shard_map/all_to_all | solution.py:309
  14.9 7.3 %collective-permute-start.3 = (bf16[4,64,128]{2,1,0:T(8,128)(2,1)S(1)}, bf16[4,64,128]{2,1,0:T(8,128)(2,1)S(1)}, u32[]{:S(2)}, u32[]{:S(2)}) collective-permute-start(bf16[4,64,128]{2,1,0:T(8,128)(2,1)S(1)} %get-tuple-element.25), channel_id=1, source_target_pairs={{0,8},{8,0},{16,24},{24,16},{1,9},{9,1},{17,25},{25,17},{2,10},{10... | collective-permute-start | bytes 196616 | tf_op jit(solution)/shard_map/ppermute | solution.py:275
  16.5 6.1 %collective-permute-start.4 = (bf16[4,64,128]{2,1,0:T(8,128)(2,1)S(1)}, bf16[4,64,128]{2,1,0:T(8,128)(2,1)S(1)}, u32[]{:S(2)}, u32[]{:S(2)}) collective-permute-start(bf16[4,64,128]{2,1,0:T(8,128)(2,1)S(1)} %get-tuple-element.26), channel_id=1, source_target_pairs={{0,16},{8,24},{16,0},{24,8},{1,17},{9,25},{17,1},{25,9},{2,18},{10... | collective-permute-start | bytes 196616 | tf_op jit(solution)/shard_map/ppermute | solution.py:275
  18.0 6.6 %collective-permute-start.5 = (bf16[4,64,128]{2,1,0:T(8,128)(2,1)S(1)}, bf16[4,64,128]{2,1,0:T(8,128)(2,1)S(1)}, u32[]{:S(2)}, u32[]{:S(2)}) collective-permute-start(bf16[4,64,128]{2,1,0:T(8,128)(2,1)S(1)} %get-tuple-element.27), channel_id=1, source_target_pairs={{0,24},{8,16},{16,8},{24,0},{1,25},{9,17},{17,9},{25,1},{2,26},{10... | collective-permute-start | bytes 196616 | tf_op jit(solution)/shard_map/ppermute | solution.py:275
  22.6 2.1 %copy-start = (s32[8,8,32]{2,1,0:T(8,128)S(1)}, s32[8,8,32]{2,1,0:T(8,128)}, u32[]{:S(2)}) copy-start(s32[8,8,32]{2,1,0:T(8,128)} %kept_hbm.1) | copy-start | bytes 24580
  22.7 2.1 %copy-start.1 = (s32[8]{0:T(128)S(1)}, s32[8]{0:T(128)}, u32[]{:S(2)}) copy-start(s32[8]{0:T(128)} %shift_hbm.3) | copy-start | bytes 100
  24.6 1.6 %collective-permute-start.6 = (bf16[16,64,128]{2,1,0:T(8,128)(2,1)S(1)}, bf16[16,64,128]{2,1,0:T(8,128)(2,1)S(1)}, u32[]{:S(2)}, u32[]{:S(2)}) collective-permute-start(bf16[16,64,128]{2,1,0:T(8,128)(2,1)S(1)} %constant_dynamic-update-slice_fusion.own_ref), channel_id=1, source_target_pairs={{0,1},{1,0},{2,3},{3,2},{4,5},{5,4},{6,7},{7,6},{8,9},{9,8},{10,11... | collective-permute-start | bytes 786440 | tf_op jit(solution)/shard_map/ppermute | solution.py:275
  32.3 24.6 %all-to-all-start.1 = ((bf16[32,96,128]{2,1,0:T(8,128)(2,1)}), bf16[32,96,128]{2,1,0:T(8,128)(2,1)S(1)}, u32[]{:S(2)}, u32[]{:S(2)}) async-start(bf16[32,96,128]{2,1,0:T(8,128)(2,1)} %full.1), calls=%async_computation.1 | async-start | bytes 1572864 | tf_op jit(solution)/shard_map/all_to_all | solution.py:369
  35.0 1.3 %collective-permute-start.7 = (bf16[4,64,128]{2,1,0:T(8,128)(2,1)S(1)}, bf16[4,64,128]{2,1,0:T(8,128)(2,1)S(1)}, u32[]{:S(2)}, u32[]{:S(2)}) collective-permute-start(bf16[4,64,128]{2,1,0:T(8,128)(2,1)S(1)} %get-tuple-element.32), channel_id=1, source_target_pairs={{0,1},{1,0},{2,3},{3,2},{4,5},{5,4},{6,7},{7,6},{8,9},{9,8},{10,11... | collective-permute-start | bytes 196616 | tf_op jit(solution)/shard_map/ppermute | solution.py:275
  36.3 11.5 %collective-permute-start.10 = (bf16[8,64,128]{2,1,0:T(8,128)(2,1)S(1)}, bf16[8,64,128]{2,1,0:T(8,128)(2,1)S(1)}, u32[]{:S(2)}, u32[]{:S(2)}) collective-permute-start(bf16[8,64,128]{2,1,0:T(8,128)(2,1)S(1)} %constant_dynamic-update-slice_fusion.4.refs_0_), channel_id=1, source_target_pairs={{0,24},{8,16},{16,8},{24,0},{1,25},{9,17},{17,9},{25,1},{2,26},{10... | collective-permute-start | bytes 393224 | tf_op jit(solution)/shard_map/ppermute | solution.py:275
  38.9 12.1 %collective-permute-start.9 = (bf16[8,64,128]{2,1,0:T(8,128)(2,1)S(1)}, bf16[8,64,128]{2,1,0:T(8,128)(2,1)S(1)}, u32[]{:S(2)}, u32[]{:S(2)}) collective-permute-start(bf16[8,64,128]{2,1,0:T(8,128)(2,1)S(1)} %constant_dynamic-update-slice_fusion.4.refs_0_), channel_id=1, source_target_pairs={{0,16},{8,24},{16,0},{24,8},{1,17},{9,25},{17,1},{25,9},{2,18},{10... | collective-permute-start | bytes 393224 | tf_op jit(solution)/shard_map/ppermute | solution.py:275
  39.5 11.5 %collective-permute-start.8 = (bf16[8,64,128]{2,1,0:T(8,128)(2,1)S(1)}, bf16[8,64,128]{2,1,0:T(8,128)(2,1)S(1)}, u32[]{:S(2)}, u32[]{:S(2)}) collective-permute-start(bf16[8,64,128]{2,1,0:T(8,128)(2,1)S(1)} %constant_dynamic-update-slice_fusion.4.refs_0_), channel_id=1, source_target_pairs={{0,8},{8,0},{16,24},{24,16},{1,9},{9,1},{17,25},{25,17},{2,10},{10... | collective-permute-start | bytes 393224 | tf_op jit(solution)/shard_map/ppermute | solution.py:275
  51.7 5.2 %copy-start.2 = (s32[2,97]{1,0:T(2,128)S(1)}, s32[2,97]{1,0:T(2,128)}, u32[]{:S(2)}) copy-start(s32[2,97]{1,0:T(2,128)} %constant.2.clone.starts_hbm) | copy-start | bytes 2332

commit v5 on v4

v5 whole, which is shorter than its diff:
```python
import functools

import jax
import jax.numpy as jnp
from jax import lax
from jax.experimental import pallas as pl
from jax.experimental.pallas import tpu as pltpu
from jax.sharding import PartitionSpec as P

PANEL = 49

SMEM = pl.BlockSpec(memory_space=pltpu.SMEM)
VMEM = pl.BlockSpec(memory_space=pltpu.VMEM)
HBM = pl.BlockSpec(memory_space=pltpu.HBM)
PARAMS = pltpu.CompilerParams(vmem_limit_bytes=40 * 1024 * 1024)
HINT = 20_000_000_000
PACK_PARAMS = pltpu.CompilerParams(vmem_limit_bytes=63 * 1024 * 1024)


class Plan:
    def __init__(self, n_row, n_col, blk):
        self.n_row, self.n_col, self.blk = n_row, n_col, blk
        self.ndev = n_row * n_col
        self.line = n_col // 2
        chips = self.ndev // 2
        self.full = min(self.ndev, PANEL)
        self.shared = min(chips, PANEL - self.full)
        self.extra = PANEL - self.full - self.shared
        self.slots = self.n_row + self.extra if self.shared else 0

    def residue(self, at):
        return jnp.where(at < PANEL - 1, at + 1, at + 1 - PANEL)

    def send_slot(self, at, chip):
        u = self.residue(at)
        if not self.shared:
            return u
        apart = jnp.bitwise_xor(u - self.full, chip)
        shift = self.line.bit_length() - 1
        plane, line = jnp.right_shift(apart, shift), jnp.bitwise_and(apart, self.line - 1)
        beyond = u - self.full - self.shared
        slot = jnp.where(beyond < 0, line * self.slots + plane, self.n_row + beyond)
        return jnp.where(u < self.full, u, self.ndev + slot)

    def back_slot(self, at, chip):
        u = self.residue(at)
        if not self.shared:
            return u
        apart = jnp.bitwise_xor(u - self.full, chip)
        return self.ndev - self.full + jnp.where(
            jnp.logical_and(u >= self.full, u < self.full + self.shared), self.full + apart, u
        )


def kept_lanes(rows, u, shift, blk):
    npan = rows.shape[0]
    target = u + shift
    target = jnp.where(target >= PANEL, target - PANEL, target)
    has = jnp.sum((rows == target).astype(jnp.float32), axis=1, keepdims=True)
    lane = lax.broadcasted_iota(jnp.int32, (npan, npan * blk), 1)
    tile = lax.broadcasted_iota(jnp.int32, (npan, npan * blk), 0)
    return jnp.sum(jnp.where(lane // blk == tile, has, 0.0), axis=0, keepdims=True)


def pack_kernel(plan, x_hbm, rows_hbm, shift_hbm, *refs):
    *out_refs, x_ref, rows_ref, shift_ref, stage, sems = refs
    row_id, col_id = lax.axis_index("row"), lax.axis_index("col")
    blk, ndev, slots = plan.blk, plan.ndev, plan.slots
    chip = row_id * plan.line + col_id // 2
    copies = [
        pltpu.make_async_copy(shift_hbm, shift_ref, sems.at[0]),
        pltpu.make_async_copy(rows_hbm.at[pl.ds(2 * row_id, 2)], rows_ref, sems.at[1]),
        pltpu.make_async_copy(x_hbm.at[0], x_ref.at[0], sems.at[2]),
        pltpu.make_async_copy(x_hbm.at[1], x_ref.at[1], sems.at[3]),
    ]
    for copy in copies:
        copy.start()
    stage[...] = jnp.zeros_like(stage)
    for copy in copies[:2]:
        copy.wait()
    for p in range(2):
        copies[2 + p].wait()
        base = PANEL - 1 - shift_ref[2 * row_id + p]
        lanes = slice(p * blk, (p + 1) * blk)
        for e in range(rows_ref.shape[2]):
            slot = plan.send_slot(rows_ref[p, col_id, e] + base, chip)
            stage[slot, :, lanes] = x_ref[p, :, e * blk : (e + 1) * blk]
    for k in range(plan.extra):
        block = stage[ndev + plan.n_row + k]
        for i in range(1, plan.line):
            stage[ndev + i * slots + plan.n_row + k] = block
    spans = [(0, ndev)] + [(ndev + i * slots, slots) for i in range(len(out_refs) - 1)]
    copies = [
        pltpu.make_async_copy(stage.at[pl.ds(first, size)], ref, sems.at[i])
        for i, ((first, size), ref) in enumerate(zip(spans, out_refs))
    ]
    for copy in copies:
        copy.start()
    for copy in copies:
        copy.wait()


def mask_kernel(plan, shift_ref, kept_ref, keep_ref):
    me = lax.axis_index("row") * plan.n_col + lax.axis_index("col")
    sets = [jnp.minimum(me, plan.full - 1), plan.full + me // 2]
    sets += [plan.full + plan.shared + k for k in range(plan.extra)]
    for k, u in enumerate(sets[: keep_ref.shape[0]]):
        for panel in range(2 * plan.n_row):
            keep_ref[k, panel : panel + 1] = kept_lanes(kept_ref[panel], u, shift_ref[panel], plan.blk)


def split_pair(low, high):
    blk = low.shape[1] // 2
    first = jnp.concatenate([low[:, :blk], high[:, :blk]], axis=1)
    second = jnp.concatenate([low[:, blk:], high[:, blk:]], axis=1)
    return first, second


def dot(a, b):
    return jnp.dot(a, b, preferred_element_type=jnp.float32)


def purify(s, m):
    return 3.0 * s.astype(jnp.float32) - 2.0 * dot(s, m)


def mask_square(plan, s, keep_ref, k, s_ref):
    for panel in range(2 * plan.n_row):
        at = slice(panel * plan.blk, (panel + 1) * plan.blk)
        s_ref[at] = jnp.where(keep_ref[k, panel : panel + 1] > 0, s[at], 0.0).astype(jnp.bfloat16)


def full_kernel(plan, keep_ref, y_ref, out_hbm, m_ref, s_ref, res_ref, sems):
    blk, n_col = plan.blk, plan.n_col
    for r in range(plan.n_row):
        for j in range(n_col // 2):
            src = r * n_col + 2 * j
            first, second = split_pair(y_ref[src], y_ref[src + 1])
            lanes = slice(2 * j * blk, (2 * j + 2) * blk)
            m_ref[2 * r * blk : (2 * r + 1) * blk, lanes] = first
            m_ref[(2 * r + 1) * blk : (2 * r + 2) * blk, lanes] = second
    m = m_ref[...]
    mask_square(plan, dot(m, m), keep_ref, 0, s_ref)
    copies = []
    for r in range(plan.n_row):
        res = purify(s_ref[2 * r * blk : (2 * r + 2) * blk], m).astype(jnp.bfloat16)
        for j in range(n_col // 2):
            lanes = slice(2 * j * blk, (2 * j + 2) * blk)
            to = r * n_col + 2 * j
            res_ref[to], res_ref[to + 1] = split_pair(res[:blk, lanes], res[blk:, lanes])
        at = pl.ds(r * n_col, n_col)
        copies.append(pltpu.make_async_copy(res_ref.at[at], out_hbm.at[at], sems.at[r]))
        copies[-1].start()
    for copy in copies:
        copy.wait()


def regroup_kernel(plan, *refs):
    line, plane, extra = refs[: plan.line], refs[plan.line : plan.line + plan.n_row], refs[plan.line + plan.n_row :]
    for i, sent in enumerate(line):
        for r, ref in enumerate(plane):
            ref[i] = sent[r]
        for ref in extra:
            for k in range(plan.extra):
                ref[k * plan.line + i] = sent[plan.n_row + k]


def return_kernel(plan, *refs):
    ins, outs = refs[: len(refs) // 2], refs[len(refs) // 2 :]
    for i in range(plan.line):
        for r in range(plan.n_row):
            outs[r][i] = ins[i][r]
    for ref, to in zip(ins[plan.line :], outs[plan.n_row :]):
        to[...] = ref[...]


def shared_kernel(plan, keep_ref, own_ref, far_ref, *refs):
    *out_refs, m_ref, s_ref, res_ref = refs
    n_row, n_col, blk = plan.n_row, plan.n_col, plan.blk
    row_id, col_id = lax.axis_index("row"), lax.axis_index("col")
    first_core = col_id % 2 == 0
    for r in range(n_row):
        start = pl.multiple_of(jnp.bitwise_xor(row_id, r) * 2 * blk, 2 * blk)
        for j in range(plan.line):
            lanes = slice(2 * j * blk, (2 * j + 2) * blk)
            at = r * plan.line + jnp.bitwise_xor(col_id // 2, j)
            own, far = own_ref[at], far_ref[at]
            pair = split_pair(jnp.where(first_core, own, far), jnp.where(first_core, far, own))
            m_ref[pl.ds(start, 2 * blk), lanes] = jnp.concatenate(pair, axis=0)
    m = m_ref[...]
    mask_square(plan, dot(m, m), keep_ref, 1, s_ref)
    res = purify(s_ref[...], m).astype(jnp.bfloat16)
    for row in range(n_row):
        upper, lower = res[2 * row * blk : (2 * row + 1) * blk], res[(2 * row + 1) * blk : (2 * row + 2) * blk]
        for j in range(plan.line):
            lanes = slice(2 * j * blk, (2 * j + 2) * blk)
            first, second = split_pair(upper[:, lanes], lower[:, lanes])
            to = jnp.bitwise_xor(col_id // 2, j) * n_row + jnp.bitwise_xor(row_id, row)
            res_ref[to] = jnp.where(first_core, first, second)
    for i, ref in enumerate(out_refs):
        ref[...] = res_ref[i * n_row : (i + 1) * n_row]


def extra_kernel(plan, keep_ref, far_ref, *refs):
    own_refs, (out_ref, m_ref, o_ref) = refs[: plan.n_row], refs[plan.n_row :]
    row_id, col_id = lax.axis_index("row"), lax.axis_index("col")
    first_core = col_id % 2 == 0
    blk, line = plan.blk, plan.line
    for k in range(plan.extra):
        for r, own_ref in enumerate(own_refs):
            start = pl.multiple_of(jnp.bitwise_xor(row_id, r) * 2 * blk, 2 * blk)
            for j in range(line):
                lanes = slice(2 * j * blk, (2 * j + 2) * blk)
                at = k * line + jnp.bitwise_xor(col_id // 2, j)
                own, far = own_ref[at], far_ref[r * plan.extra * line + at]
                pair = split_pair(jnp.where(first_core, own, far), jnp.where(first_core, far, own))
                tile = jnp.concatenate(pair, axis=0)
                m_ref[pl.ds(start, 2 * blk), lanes] = tile
                if r == 0:
                    o_ref[:, lanes] = tile
        m = m_ref[...]
        s = dot(o_ref[...], m)
        kept = []
        for p in range(2):
            keep = keep_ref[2 + k, pl.ds(2 * row_id + p, 1)]
            kept.append(jnp.where(keep > 0, s[p * blk : (p + 1) * blk], 0.0).astype(jnp.bfloat16))
        res = purify(jnp.concatenate(kept, axis=0), m)
        mine = res[:, : 2 * blk]
        for j in range(1, line):
            mine = jnp.where(col_id // 2 == j, res[:, 2 * j * blk : (2 * j + 2) * blk], mine)
        first, second = split_pair(mine[:blk], mine[blk:])
        out_ref[k] = jnp.where(first_core, first, second).astype(jnp.bfloat16)


def unpack_kernel(plan, kept_hbm, shift_hbm, *refs):
    *in_refs, out_hbm, rows_ref, shift_ref, stage, out_ref, sems = refs
    row_id, col_id = lax.axis_index("row"), lax.axis_index("col")
    blk = plan.blk
    chip = row_id * plan.line + col_id // 2
    copies = [
        pltpu.make_async_copy(shift_hbm, shift_ref, sems.at[0]),
        pltpu.make_async_copy(kept_hbm.at[pl.ds(2 * row_id, 2)], rows_ref, sems.at[1]),
    ]
    for copy in copies:
        copy.start()
    first = 0
    for size, ref in zip([plan.ndev] + [plan.line] * (plan.shared // plan.line) + [plan.extra], in_refs):
        stage[first : first + size] = ref[:size]
        first += size
    for copy in copies:
        copy.wait()
    part = rows_ref.shape[2] // 4
    copies = []
    for p in range(2):
        base = PANEL - 1 - shift_ref[2 * row_id + p]
        lanes = slice(p * blk, (p + 1) * blk)
        for e in range(rows_ref.shape[2]):
            tile = stage[plan.back_slot(rows_ref[p, col_id, e] + base, chip)]
            out_ref[p, :, e * blk : (e + 1) * blk] = tile[:, lanes].astype(jnp.float32)
            if e % part == part - 1:
                at = (p, slice(None), pl.ds((e + 1 - part) * blk, part * blk))
                copies.append(pltpu.make_async_copy(out_ref.at[at], out_hbm.at[at], sems.at[2 + len(copies)]))
                copies[-1].start()
    for copy in copies:
        copy.wait()


def swapped(shard, axis, by):
    return lax.ppermute(shard, axis, [(i, i ^ by) for i in range(lax.axis_size(axis))])


def body(density, density_rows, square_rows, panel_shift):
    both = ("row", "col")
    n_row, n_col = lax.axis_size("row"), lax.axis_size("col")
    blk, rh = density.shape[1], density_rows.shape[2]
    npan = density_rows.shape[0]
    plan = Plan(n_row, n_col, blk)
    ndev = plan.ndev
    bf16 = jnp.bfloat16
    size = n_col * blk
    square = pltpu.VMEM((size, size), bf16)
    tables = [pltpu.SMEM((2, npan, rh), jnp.int32), pltpu.SMEM((npan,), jnp.int32)]

    def blocks(*shape):
        return jax.ShapeDtypeStruct((*shape, 2 * blk), bf16)

    shapes = [blocks(ndev, blk)] + ([blocks(plan.slots, blk)] * plan.line if plan.shared else [])
    packed, *line = pl.pallas_call(
        functools.partial(pack_kernel, plan),
        out_shape=shapes,
        in_specs=[HBM] * 3,
        out_specs=[HBM] * len(shapes),
        scratch_shapes=[pltpu.VMEM(density.shape, bf16)]
        + tables
        + [
            pltpu.VMEM((ndev + plan.line * plan.slots, blk, 2 * blk), bf16),
            pltpu.SemaphoreType.DMA((max(4, len(shapes)),)),
        ],
        compiler_params=PACK_PARAMS,
        name="pack",
    )(density, density_rows, panel_shift)
    y = lax.all_to_all(packed, both, 0, 0, tiled=True)
    sets = 1 + (1 if plan.shared else 0) + plan.extra
    keep = pl.pallas_call(
        functools.partial(mask_kernel, plan),
        out_shape=jax.ShapeDtypeStruct((sets, npan, size), jnp.float32),
        in_specs=[SMEM, VMEM],
        out_specs=VMEM,
        compiler_params=PARAMS,
        name="masks",
    )(panel_shift, square_rows)
    back, extra = [], []
    if plan.shared:

        def regroup(kernel, shapes, name, *operands):
            return pl.pallas_call(
                functools.partial(kernel, plan),
                out_shape=shapes,
                in_specs=[VMEM] * len(operands),
                out_specs=[VMEM] * len(shapes),
                compiler_params=PARAMS,
                cost_estimate=pl.CostEstimate(flops=HINT, bytes_accessed=0, transcendentals=0),
                name=name,
            )(*operands)

        line = line[:1] + [swapped(sent, "col", 2 * i) for i, sent in enumerate(line) if i]
        shapes = [blocks(plan.line, blk)] * n_row + [blocks(plan.line * plan.extra, blk)] * min(1, plan.extra)
        plane = list(regroup(regroup_kernel, shapes, "regroup", *line))
        plane, rest = plane[:n_row], plane[n_row:]
        own = jnp.concatenate([plane[0]] + [swapped(sent, "row", r) for r, sent in enumerate(plane) if r])
        far = swapped(own, "col", 1)
        back = pl.pallas_call(
            functools.partial(shared_kernel, plan),
            out_shape=[blocks(n_row, blk)] * plan.line,
            in_specs=[VMEM] * 3,
            out_specs=[VMEM] * plan.line,
            scratch_shapes=[square] * 2 + [pltpu.VMEM((plan.shared, blk, 2 * blk), bf16)],
            compiler_params=PARAMS,
            name="shared",
        )(keep, own, far)
        y, keep, first, *rest = lax.optimization_barrier((y, keep, back[0], *rest))
        back = [first] + list(back[1:])
        back = back[:1] + [swapped(sent, "col", 2 * i) for i, sent in enumerate(back) if i]
        back = list(regroup(return_kernel, shapes, "regroup_back", *back, *rest))
        back, rest = back[:n_row], back[n_row:]
        rest = rest + [swapped(sent, "row", r) for sent in rest for r in range(1, n_row)]
        back = [back[0]] + [swapped(sent, "row", r) for r, sent in enumerate(back) if r]
        if plan.extra:
            tied = lax.optimization_barrier((*rest, *back))
            rest, back = tied[:n_row], tied[n_row:]
    if plan.extra:
        far = swapped(jnp.concatenate(rest), "col", 1)
        extra = pl.pallas_call(
            functools.partial(extra_kernel, plan),
            out_shape=blocks(plan.extra, blk),
            in_specs=[VMEM] * (2 + n_row),
            out_specs=VMEM,
            scratch_shapes=[square, pltpu.VMEM((2 * blk, size), bf16)],
            compiler_params=PARAMS,
            name="extra",
        )(keep, far, *rest)
        extra = [extra]
    out = pl.pallas_call(
        functools.partial(full_kernel, plan),
        out_shape=blocks(ndev, blk),
        in_specs=[VMEM] * 2,
        out_specs=HBM,
        scratch_shapes=[square] * 2 + [pltpu.VMEM((ndev, blk, 2 * blk), bf16), pltpu.SemaphoreType.DMA((n_row,))],
        compiler_params=PARAMS,
        cost_estimate=pl.CostEstimate(flops=4 * size**3, bytes_accessed=8 * ndev * blk * blk, transcendentals=0),
        name="full",
    )(keep, y)
    ret = lax.all_to_all(out, both, 0, 0, tiled=True)
    return pl.pallas_call(
        functools.partial(unpack_kernel, plan),
        out_shape=jax.ShapeDtypeStruct(density.shape, jnp.float32),
        in_specs=[HBM] * 2 + [VMEM] * (1 + len(back) + len(extra)),
        out_specs=HBM,
        scratch_shapes=tables
        + [
            pltpu.VMEM((ndev + plan.shared + plan.extra, blk, 2 * blk), bf16),
            pltpu.VMEM(density.shape, jnp.float32),
            pltpu.SemaphoreType.DMA((10,)),
        ],
        compiler_params=PARAMS,
        name="unpack",
    )(square_rows, panel_shift, ret, *back, *extra)


def solution(mesh):
    placed = (P("row", None, "col"), P(), P(), P())
    return jax.shard_map(
        body, mesh=mesh, in_specs=placed, out_specs=P("row", None, "col"), check_vma=False
    )
```

time: 59.2 us -> 56.9 us (0.961)
  waiting for transfers between devices: 28.5 us -> 16.2 us
  starting transfers between devices: 21.8 us -> 31.7 us
    ppermute x11 -> x17, starting transfers between devices: 13 us -> 21.3 us  [swapped(): lax.ppermute(shard, axis, [(i, i ^ by) for i in range(lax.axis_size(axis))])]
    all_to_all x1, waiting for transfers between devices: 5.21 us -> 0.19 us  [body(): ret = lax.all_to_all(out, both, 0, 0, tiled=True)]
    ppermute x11 -> x17, waiting for transfers between devices: 19.8 us -> 16 us  [swapped(): lax.ppermute(shard, axis, [(i, i ^ by) for i in range(lax.axis_size(axis))])]
    all_to_all x1, waiting for transfers between devices: 3.48 us -> 0.01 us  [body(): y = lax.all_to_all(packed, both, 0, 0, tiled=True)]
    all_to_all x1, starting transfers between devices: 2.64 us -> 4.38 us  [body(): ret = lax.all_to_all(out, both, 0, 0, tiled=True)]
  transfers between devices with their start and end apart: 13 -> 19, of which waited for: 10 -> 13; matrix products, arithmetic and copies ran while one was open for 0% -> 0% of each run, Pallas kernels for 4% -> 7%
where the time goes in v5:
time: 56.9 us; the launch traced here: 56.5 us
  starting transfers between devices  31.7 us (56%)
  waiting for transfers between devices  16.2 us (28%)
  Pallas kernels  8.38 us (15%)
    ppermute x17, starting transfers between devices, swapped(): lax.ppermute(shard, axis, [(i, i ^ by) for i in range(lax.axis_size(axis))])  21.3 us
    ppermute x17, waiting for transfers between devices, swapped(): lax.ppermute(shard, axis, [(i, i ^ by) for i in range(lax.axis_size(axis))])  16 us
    all_to_all x1, starting transfers between devices, body(): y = lax.all_to_all(packed, both, 0, 0, tiled=True)  6.07 us
    all_to_all x1, starting transfers between devices, body(): ret = lax.all_to_all(out, both, 0, 0, tiled=True)  4.38 us
    pallas_call x1, Pallas kernels, body(): pl.pallas_call(functools.partial(pack_kernel, plan), out_shape=shapes, in...  2.39 us
    pallas_call x1, Pallas kernels, body(): pl.pallas_call(functools.partial(unpack_kernel, plan), out_shape=jax.Shap...  1.84 us
    pallas_call x1, Pallas kernels, body(): pl.pallas_call(functools.partial(full_kernel, plan), out_shape=blocks(nde...  1.65 us
  transfers between devices with their start and end apart: 19, of which 13 were waited for; matrix products, arithmetic and copies ran while one was open for 0% of the time, Pallas kernels for 7%

profile of v5, /device:TPU:0, one launch (start us, length us, event | category | flops | bytes accessed | tf_op | source)
XLA Modules:
  0.0 56.5 jit_solution(7264823342794384243)
XLA Ops:
  0.0 2.4 %pack.1 = (bf16[32,64,128]{2,1,0:T(8,128)(2,1)}, bf16[5,64,128]{2,1,0:T(8,128)(2,1)}, bf16[5,64,128]{2,1,0:T(8,128)(2,1)}, bf16[5,64,128]{2,1,0:T(8,128)(2,1)}, bf16[5,64,128]{2,1,0:T(8,128)(2,1)}) custom-call(bf16[2,64,2048]{2,1,0:T(8,128)(2,1)} %x_hbm.1, s32[8,8,32]{2,1,0:T(8,128)} %rows_hbm.1, s32[8]{0:T(128)} %shift_hbm.3), custom_call_target="tpu_custom_call" | custom-call | tf_op jit(solution)/shard_map/pack/pallas_call | solution.py:288
  2.4 3.1 %collective-permute-start = (bf16[5,64,128]{2,1,0:T(8,128)(2,1)}, bf16[5,64,128]{2,1,0:T(8,128)(2,1)S(1)}, u32[]{:S(2)}, u32[]{:S(2)}) collective-permute-start(bf16[5,64,128]{2,1,0:T(8,128)(2,1)} %get-tuple-element.38), channel_id=1, source_target_pairs={{0,2},{1,3},{2,0},{3,1},{4,6},{5,7},{6,4},{7,5},{8,10},{9,11},{10,... | collective-permute-start | bytes 245768 | tf_op jit(solution)/shard_map/ppermute | solution.py:269
  5.5 2.6 %collective-permute-start.1 = (bf16[5,64,128]{2,1,0:T(8,128)(2,1)}, bf16[5,64,128]{2,1,0:T(8,128)(2,1)S(1)}, u32[]{:S(2)}, u32[]{:S(2)}) collective-permute-start(bf16[5,64,128]{2,1,0:T(8,128)(2,1)} %get-tuple-element.39), channel_id=1, source_target_pairs={{0,4},{1,5},{2,6},{3,7},{4,0},{5,1},{6,2},{7,3},{8,12},{9,13},{10,... | collective-permute-start | bytes 245768 | tf_op jit(solution)/shard_map/ppermute | solution.py:269
  8.1 0.0 collective-permute-start.2
  8.1 6.1 %all-to-all-start = ((bf16[32,64,128]{2,1,0:T(8,128)(2,1)}), bf16[32,64,128]{2,1,0:T(8,128)(2,1)S(1)}, u32[]{:S(2)}, u32[]{:S(2)}) async-start(bf16[32,64,128]{2,1,0:T(8,128)(2,1)} %get-tuple-element.36), calls=%async_computation | async-start | bytes 1048576 | tf_op jit(solution)/shard_map/all_to_all | solution.py:302
  14.2 0.0 collective-permute-done.refs_1_
  14.2 0.7 %collective-permute-done.1.refs_2_ = bf16[5,64,128]{2,1,0:T(8,128)(2,1)S(1)} collective-permute-done((bf16[5,64,128]{2,1,0:T(8,128)(2,1)}, bf16[5,64,128]{2,1,0:T(8,128)(2,1)S(1)}, u32[]{:S(2)}, u32[]{:S(2)}) %collective-permute-start.1) | collective-permute-done | bytes 81952 | tf_op jit(solution)/shard_map/ppermute | solution.py:269
  14.9 0.0 collective-permute-done.2.refs_3_
  14.9 0.0 copy-done.2
  14.9 1.6 %collective-permute-start.3 = (bf16[4,64,128]{2,1,0:T(8,128)(2,1)S(1)}, bf16[4,64,128]{2,1,0:T(8,128)(2,1)S(1)}, u32[]{:S(2)}, u32[]{:S(2)}) collective-permute-start(bf16[4,64,128]{2,1,0:T(8,128)(2,1)S(1)} %get-tuple-element.42), channel_id=1, source_target_pairs={{0,8},{8,0},{16,24},{24,16},{1,9},{9,1},{17,25},{25,17},{2,10},{10... | collective-permute-start | bytes 196616 | tf_op jit(solution)/shard_map/ppermute | solution.py:269
  16.5 1.5 %collective-permute-start.4 = (bf16[4,64,128]{2,1,0:T(8,128)(2,1)S(1)}, bf16[4,64,128]{2,1,0:T(8,128)(2,1)S(1)}, u32[]{:S(2)}, u32[]{:S(2)}) collective-permute-start(bf16[4,64,128]{2,1,0:T(8,128)(2,1)S(1)} %get-tuple-element.43), channel_id=1, source_target_pairs={{0,16},{8,24},{16,0},{24,8},{1,17},{9,25},{17,1},{25,9},{2,18},{10... | collective-permute-start | bytes 196616 | tf_op jit(solution)/shard_map/ppermute | solution.py:269
  18.0 0.5 collective-permute-start.5
  18.5 3.8 %collective-permute-done.3 = bf16[4,64,128]{2,1,0:T(8,128)(2,1)S(1)} collective-permute-done((bf16[4,64,128]{2,1,0:T(8,128)(2,1)S(1)}, bf16[4,64,128]{2,1,0:T(8,128)(2,1)S(1)}, u32[]{:S(2)}, u32[]{:S(2)}) %collective-permute-start.3) | collective-permute-done | bytes 65568 | tf_op jit(solution)/shard_map/ppermute | solution.py:269
  22.2 0.4 collective-permute-done.4
  22.6 0.0 copy-start
  22.6 0.0 copy-start.1
  22.7 1.9 %collective-permute-done.5 = bf16[4,64,128]{2,1,0:T(8,128)(2,1)S(1)} collective-permute-done((bf16[4,64,128]{2,1,0:T(8,128)(2,1)S(1)}, bf16[4,64,128]{2,1,0:T(8,128)(2,1)S(1)}, u32[]{:S(2)}, u32[]{:S(2)}) %collective-permute-start.5) | collective-permute-done | bytes 65568 | tf_op jit(solution)/shard_map/ppermute | solution.py:269
  24.6 0.1 collective-permute-start.6
  24.7 0.0 copy-done
  24.7 0.7 %masks.1.keep_ref = f32[3,8,512]{2,1,0:T(8,128)S(1)} custom-call(s32[8]{0:T(128)S(1)} %copy-done.1, s32[8,8,32]{2,1,0:T(8,128)S(1)} %copy-done), custom_call_target="tpu_custom_call" | custom-call | tf_op jit(solution)/shard_map/masks/pallas_call | solution.py:304
  25.5 0.8 %collective-permute-done.6.far_ref = bf16[16,64,128]{2,1,0:T(8,128)(2,1)S(1)} collective-permute-done((bf16[16,64,128]{2,1,0:T(8,128)(2,1)S(1)}, bf16[16,64,128]{2,1,0:T(8,128)(2,1)S(1)}, u32[]{:S(2)}, u32[]{:S(2)}) %collective-permute-start.6) | collective-permute-done | bytes 262176 | tf_op jit(solution)/shard_map/ppermute | solution.py:269
  26.2 1.0 %shared.1 = (bf16[4,64,128]{2,1,0:T(8,128)(2,1)S(1)}, bf16[4,64,128]{2,1,0:T(8,128)(2,1)S(1)}, bf16[4,64,128]{2,1,0:T(8,128)(2,1)S(1)}, bf16[4,64,128]{2,1,0:T(8,128)(2,1)S(1)}) custom-call(f32[3,8,512]{2,1,0:T(8,128)S(1)} %masks.1.keep_ref, bf16[16,64,128]{2,1,0:T(8,128)(2,1)S(1)} %constant_dynamic-update-slice_fusion.own_ref, ...), custom_call_target="tpu_custom_call" | custom-call | tf_op jit(solution)/shard_map/shared/pallas_call | solution.py:332
  27.3 2.0 %collective-permute-start.7 = (bf16[4,64,128]{2,1,0:T(8,128)(2,1)S(1)}, bf16[4,64,128]{2,1,0:T(8,128)(2,1)S(1)}, u32[]{:S(2)}, u32[]{:S(2)}) collective-permute-start(bf16[4,64,128]{2,1,0:T(8,128)(2,1)S(1)} %get-tuple-element.50), channel_id=1, source_target_pairs={{0,2},{1,3},{2,0},{3,1},{4,6},{5,7},{6,4},{7,5},{8,10},{9,11},{10,... | collective-permute-start | bytes 196616 | tf_op jit(solution)/shard_map/ppermute | solution.py:269
  29.2 3.1 %collective-permute-start.8 = (bf16[4,64,128]{2,1,0:T(8,128)(2,1)S(1)}, bf16[4,64,128]{2,1,0:T(8,128)(2,1)S(1)}, u32[]{:S(2)}, u32[]{:S(2)}) collective-permute-start(bf16[4,64,128]{2,1,0:T(8,128)(2,1)S(1)} %get-tuple-element.51), channel_id=1, source_target_pairs={{0,4},{1,5},{2,6},{3,7},{4,0},{5,1},{6,2},{7,3},{8,12},{9,13},{10,... | collective-permute-start | bytes 196616 | tf_op jit(solution)/shard_map/ppermute | solution.py:269
  32.3 0.0 collective-permute-start.9
  32.3 0.0 all-to-all-done.y_ref
  32.3 1.6 %full.1 = bf16[32,64,128]{2,1,0:T(8,128)(2,1)} custom-call(f32[3,8,512]{2,1,0:T(8,128)S(1)} %masks.1.keep_ref, bf16[32,64,128]{2,1,0:T(8,128)(2,1)S(1)} %all-to-all-done.y_ref), custom_call_target="tpu_custom_call" | custom-call | flops 536870912 | bytes 1048576 | tf_op jit(solution)/shard_map/full/pallas_call | solution.py:363
  34.0 4.4 %all-to-all-start.1 = ((bf16[32,64,128]{2,1,0:T(8,128)(2,1)}), bf16[32,64,128]{2,1,0:T(8,128)(2,1)S(1)}, u32[]{:S(2)}, u32[]{:S(2)}) async-start(bf16[32,64,128]{2,1,0:T(8,128)(2,1)} %full.1), calls=%async_computation.1 | async-start | bytes 1048576 | tf_op jit(solution)/shard_map/all_to_all | solution.py:373
  38.3 0.0 collective-permute-done.7.refs_1_
  38.4 0.0 collective-permute-done.8.refs_2_
  38.4 0.1 collective-permute-done.9.refs_3_
  38.5 1.8 %collective-permute-start.13 = (bf16[4,64,128]{2,1,0:T(8,128)(2,1)S(1)}, bf16[4,64,128]{2,1,0:T(8,128)(2,1)S(1)}, u32[]{:S(2)}, u32[]{:S(2)}) collective-permute-start(bf16[4,64,128]{2,1,0:T(8,128)(2,1)S(1)} %get-tuple-element.56), channel_id=1, source_target_pairs={{0,8},{8,0},{16,24},{24,16},{1,9},{9,1},{17,25},{25,17},{2,10},{10... | collective-permute-start | bytes 196616 | tf_op jit(solution)/shard_map/ppermute | solution.py:269
  40.2 1.5 %collective-permute-start.14 = (bf16[4,64,128]{2,1,0:T(8,128)(2,1)S(1)}, bf16[4,64,128]{2,1,0:T(8,128)(2,1)S(1)}, u32[]{:S(2)}, u32[]{:S(2)}) collective-permute-start(bf16[4,64,128]{2,1,0:T(8,128)(2,1)S(1)} %get-tuple-element.57), channel_id=1, source_target_pairs={{0,16},{8,24},{16,0},{24,8},{1,17},{9,25},{17,1},{25,9},{2,18},{10... | collective-permute-start | bytes 196616 | tf_op jit(solution)/shard_map/ppermute | solution.py:269
  41.7 0.3 collective-permute-start.15
  42.0 2.6 %collective-permute-start.12 = (bf16[4,64,128]{2,1,0:T(8,128)(2,1)S(1)}, bf16[4,64,128]{2,1,0:T(8,128)(2,1)S(1)}, u32[]{:S(2)}, u32[]{:S(2)}) collective-permute-start(bf16[4,64,128]{2,1,0:T(8,128)(2,1)S(1)} %get-tuple-element.63.refs_0_), channel_id=1, source_target_pairs={{0,24},{8,16},{16,8},{24,0},{1,25},{9,17},{17,9},{25,1},{2,26},{10... | collective-permute-start | bytes 196616 | tf_op jit(solution)/shard_map/ppermute | solution.py:269
  44.6 0.6 collective-permute-start.11
  45.2 1.2 %collective-permute-done.13.refs_2_ = bf16[4,64,128]{2,1,0:T(8,128)(2,1)S(1)} collective-permute-done((bf16[4,64,128]{2,1,0:T(8,128)(2,1)S(1)}, bf16[4,64,128]{2,1,0:T(8,128)(2,1)S(1)}, u32[]{:S(2)}, u32[]{:S(2)}) %collective-permute-start.13) | collective-permute-done | bytes 65568 | tf_op jit(solution)/shard_map/ppermute | solution.py:269
  46.4 0.2 collective-permute-start.10
  46.6 0.5 collective-permute-done.14.refs_3_
  47.2 2.2 %collective-permute-done.15.refs_4_ = bf16[4,64,128]{2,1,0:T(8,128)(2,1)S(1)} collective-permute-done((bf16[4,64,128]{2,1,0:T(8,128)(2,1)S(1)}, bf16[4,64,128]{2,1,0:T(8,128)(2,1)S(1)}, u32[]{:S(2)}, u32[]{:S(2)}) %collective-permute-start.15) | collective-permute-done | bytes 65568 | tf_op jit(solution)/shard_map/ppermute | solution.py:269
  49.4 1.8 %collective-permute-done.12.refs_3_ = bf16[4,64,128]{2,1,0:T(8,128)(2,1)S(1)} collective-permute-done((bf16[4,64,128]{2,1,0:T(8,128)(2,1)S(1)}, bf16[4,64,128]{2,1,0:T(8,128)(2,1)S(1)}, u32[]{:S(2)}, u32[]{:S(2)}) %collective-permute-start.12) | collective-permute-done | bytes 65568 | tf_op jit(solution)/shard_map/ppermute | solution.py:269
  51.2 1.0 %collective-permute-done.11.refs_2_ = bf16[4,64,128]{2,1,0:T(8,128)(2,1)S(1)} collective-permute-done((bf16[4,64,128]{2,1,0:T(8,128)(2,1)S(1)}, bf16[4,64,128]{2,1,0:T(8,128)(2,1)S(1)}, u32[]{:S(2)}, u32[]{:S(2)}) %collective-permute-start.11) | collective-permute-done | bytes 65568 | tf_op jit(solution)/shard_map/ppermute | solution.py:269
  52.2 0.0 collective-permute-done.10.refs_1_
  52.2 0.1 collective-permute-start.16
  52.3 1.5 %collective-permute-done.16.far_ref = bf16[16,64,128]{2,1,0:T(8,128)(2,1)S(1)} collective-permute-done((bf16[16,64,128]{2,1,0:T(8,128)(2,1)S(1)}, bf16[16,64,128]{2,1,0:T(8,128)(2,1)S(1)}, u32[]{:S(2)}, u32[]{:S(2)}) %collective-permute-start.16) | collective-permute-done | bytes 262176 | tf_op jit(solution)/shard_map/ppermute | solution.py:269
  53.8 0.7 %extra.1.refs_5_ = bf16[1,64,128]{2,1,0:T(8,128)(2,1)S(1)} custom-call(f32[3,8,512]{2,1,0:T(8,128)S(1)} %masks.1.keep_ref, bf16[16,64,128]{2,1,0:T(8,128)(2,1)S(1)} %collective-permute-done.16.far_ref, bf16[4,64,128]{2,1,0:T(8,128)(2,1)S(1)} %get-tuple-element.63.refs_0_, bf16[4,64,128]{2,1,0:T(8,128)(2,1)S(1)} %collective-permute-done.10.refs_1_, ...), custom_call_target="tpu_custom_call" | custom-call | tf_op jit(solution)/shard_map/extra/pallas_call | solution.py:353
  54.5 0.2 all-to-all-done.1.refs_0_
  54.7 1.8 %unpack.1 = f32[2,64,2048]{2,1,0:T(8,128)} custom-call(s32[8,8,32]{2,1,0:T(8,128)S(1)} %copy-done, s32[8]{0:T(128)S(1)} %copy-done.1, bf16[32,64,128]{2,1,0:T(8,128)(2,1)S(1)} %all-to-all-done.1.refs_0_, bf16[4,64,128]{2,1,0:T(8,128)(2,1)S(1)} %get-tuple-element.59.refs_1_, bf16[4,64,128]{2,1,0:T(8,128)(2,1)S(1)} %collective-permute-done.13.refs_2_, ...), custom_call_target="tpu_custom_call" | custom-call | tf_op jit(solution)/shard_map/unpack/pallas_call | solution.py:374
  (9 shorter events, 0.1 us)
Async XLA Ops:
  2.4 11.8 %collective-permute-start = (bf16[5,64,128]{2,1,0:T(8,128)(2,1)}, bf16[5,64,128]{2,1,0:T(8,128)(2,1)S(1)}, u32[]{:S(2)}, u32[]{:S(2)}) collective-permute-start(bf16[5,64,128]{2,1,0:T(8,128)(2,1)} %get-tuple-element.38), channel_id=1, source_target_pairs={{0,2},{1,3},{2,0},{3,1},{4,6},{5,7},{6,4},{7,5},{8,10},{9,11},{10,... | collective-permute-start | bytes 245768 | tf_op jit(solution)/shard_map/ppermute | solution.py:269
  5.5 9.4 %collective-permute-start.1 = (bf16[5,64,128]{2,1,0:T(8,128)(2,1)}, bf16[5,64,128]{2,1,0:T(8,128)(2,1)S(1)}, u32[]{:S(2)}, u32[]{:S(2)}) collective-permute-start(bf16[5,64,128]{2,1,0:T(8,128)(2,1)} %get-tuple-element.39), channel_id=1, source_target_pairs={{0,4},{1,5},{2,6},{3,7},{4,0},{5,1},{6,2},{7,3},{8,12},{9,13},{10,... | collective-permute-start | bytes 245768 | tf_op jit(solution)/shard_map/ppermute | solution.py:269
  8.1 6.8 %collective-permute-start.2 = (bf16[5,64,128]{2,1,0:T(8,128)(2,1)}, bf16[5,64,128]{2,1,0:T(8,128)(2,1)S(1)}, u32[]{:S(2)}, u32[]{:S(2)}) collective-permute-start(bf16[5,64,128]{2,1,0:T(8,128)(2,1)} %get-tuple-element.40), channel_id=1, source_target_pairs={{0,6},{1,7},{2,4},{3,5},{4,2},{5,3},{6,0},{7,1},{8,14},{9,15},{10,... | collective-permute-start | bytes 245768 | tf_op jit(solution)/shard_map/ppermute | solution.py:269
  8.1 6.8 %copy-start.2 = (bf16[5,64,128]{2,1,0:T(8,128)(2,1)S(1)}, bf16[5,64,128]{2,1,0:T(8,128)(2,1)}, u32[]{:S(2)}) copy-start(bf16[5,64,128]{2,1,0:T(8,128)(2,1)} %get-tuple-element.37.refs_0_) | copy-start | bytes 245764
  8.1 24.2 %all-to-all-start = ((bf16[32,64,128]{2,1,0:T(8,128)(2,1)}), bf16[32,64,128]{2,1,0:T(8,128)(2,1)S(1)}, u32[]{:S(2)}, u32[]{:S(2)}) async-start(bf16[32,64,128]{2,1,0:T(8,128)(2,1)} %get-tuple-element.36), calls=%async_computation | async-start | bytes 1048576 | tf_op jit(solution)/shard_map/all_to_all | solution.py:302
  14.9 7.3 %collective-permute-start.3 = (bf16[4,64,128]{2,1,0:T(8,128)(2,1)S(1)}, bf16[4,64,128]{2,1,0:T(8,128)(2,1)S(1)}, u32[]{:S(2)}, u32[]{:S(2)}) collective-permute-start(bf16[4,64,128]{2,1,0:T(8,128)(2,1)S(1)} %get-tuple-element.42), channel_id=1, source_target_pairs={{0,8},{8,0},{16,24},{24,16},{1,9},{9,1},{17,25},{25,17},{2,10},{10... | collective-permute-start | bytes 196616 | tf_op jit(solution)/shard_map/ppermute | solution.py:269
  16.5 6.1 %collective-permute-start.4 = (bf16[4,64,128]{2,1,0:T(8,128)(2,1)S(1)}, bf16[4,64,128]{2,1,0:T(8,128)(2,1)S(1)}, u32[]{:S(2)}, u32[]{:S(2)}) collective-permute-start(bf16[4,64,128]{2,1,0:T(8,128)(2,1)S(1)} %get-tuple-element.43), channel_id=1, source_target_pairs={{0,16},{8,24},{16,0},{24,8},{1,17},{9,25},{17,1},{25,9},{2,18},{10... | collective-permute-start | bytes 196616 | tf_op jit(solution)/shard_map/ppermute | solution.py:269
  18.0 6.6 %collective-permute-start.5 = (bf16[4,64,128]{2,1,0:T(8,128)(2,1)S(1)}, bf16[4,64,128]{2,1,0:T(8,128)(2,1)S(1)}, u32[]{:S(2)}, u32[]{:S(2)}) collective-permute-start(bf16[4,64,128]{2,1,0:T(8,128)(2,1)S(1)} %get-tuple-element.44), channel_id=1, source_target_pairs={{0,24},{8,16},{16,8},{24,0},{1,25},{9,17},{17,9},{25,1},{2,26},{10... | collective-permute-start | bytes 196616 | tf_op jit(solution)/shard_map/ppermute | solution.py:269
  22.6 2.1 %copy-start = (s32[8,8,32]{2,1,0:T(8,128)S(1)}, s32[8,8,32]{2,1,0:T(8,128)}, u32[]{:S(2)}) copy-start(s32[8,8,32]{2,1,0:T(8,128)} %kept_hbm.1) | copy-start | bytes 24580
  22.6 2.1 %copy-start.1 = (s32[8]{0:T(128)S(1)}, s32[8]{0:T(128)}, u32[]{:S(2)}) copy-start(s32[8]{0:T(128)} %shift_hbm.3) | copy-start | bytes 100
  24.6 1.6 %collective-permute-start.6 = (bf16[16,64,128]{2,1,0:T(8,128)(2,1)S(1)}, bf16[16,64,128]{2,1,0:T(8,128)(2,1)S(1)}, u32[]{:S(2)}, u32[]{:S(2)}) collective-permute-start(bf16[16,64,128]{2,1,0:T(8,128)(2,1)S(1)} %constant_dynamic-update-slice_fusion.own_ref), channel_id=1, source_target_pairs={{0,1},{1,0},{2,3},{3,2},{4,5},{5,4},{6,7},{7,6},{8,9},{9,8},{10,11... | collective-permute-start | bytes 786440 | tf_op jit(solution)/shard_map/ppermute | solution.py:269
  27.3 11.1 %collective-permute-start.7 = (bf16[4,64,128]{2,1,0:T(8,128)(2,1)S(1)}, bf16[4,64,128]{2,1,0:T(8,128)(2,1)S(1)}, u32[]{:S(2)}, u32[]{:S(2)}) collective-permute-start(bf16[4,64,128]{2,1,0:T(8,128)(2,1)S(1)} %get-tuple-element.50), channel_id=1, source_target_pairs={{0,2},{1,3},{2,0},{3,1},{4,6},{5,7},{6,4},{7,5},{8,10},{9,11},{10,... | collective-permute-start | bytes 196616 | tf_op jit(solution)/shard_map/ppermute | solution.py:269
  29.2 9.1 %collective-permute-start.8 = (bf16[4,64,128]{2,1,0:T(8,128)(2,1)S(1)}, bf16[4,64,128]{2,1,0:T(8,128)(2,1)S(1)}, u32[]{:S(2)}, u32[]{:S(2)}) collective-permute-start(bf16[4,64,128]{2,1,0:T(8,128)(2,1)S(1)} %get-tuple-element.51), channel_id=1, source_target_pairs={{0,4},{1,5},{2,6},{3,7},{4,0},{5,1},{6,2},{7,3},{8,12},{9,13},{10,... | collective-permute-start | bytes 196616 | tf_op jit(solution)/shard_map/ppermute | solution.py:269
  32.3 6.2 %collective-permute-start.9 = (bf16[4,64,128]{2,1,0:T(8,128)(2,1)S(1)}, bf16[4,64,128]{2,1,0:T(8,128)(2,1)S(1)}, u32[]{:S(2)}, u32[]{:S(2)}) collective-permute-start(bf16[4,64,128]{2,1,0:T(8,128)(2,1)S(1)} %get-tuple-element.52), channel_id=1, source_target_pairs={{0,6},{1,7},{2,4},{3,5},{4,2},{5,3},{6,0},{7,1},{8,14},{9,15},{10,... | collective-permute-start | bytes 196616 | tf_op jit(solution)/shard_map/ppermute | solution.py:269
  34.0 20.7 %all-to-all-start.1 = ((bf16[32,64,128]{2,1,0:T(8,128)(2,1)}), bf16[32,64,128]{2,1,0:T(8,128)(2,1)S(1)}, u32[]{:S(2)}, u32[]{:S(2)}) async-start(bf16[32,64,128]{2,1,0:T(8,128)(2,1)} %full.1), calls=%async_computation.1 | async-start | bytes 1048576 | tf_op jit(solution)/shard_map/all_to_all | solution.py:373
  38.5 7.9 %collective-permute-start.13 = (bf16[4,64,128]{2,1,0:T(8,128)(2,1)S(1)}, bf16[4,64,128]{2,1,0:T(8,128)(2,1)S(1)}, u32[]{:S(2)}, u32[]{:S(2)}) collective-permute-start(bf16[4,64,128]{2,1,0:T(8,128)(2,1)S(1)} %get-tuple-element.56), channel_id=1, source_target_pairs={{0,8},{8,0},{16,24},{24,16},{1,9},{9,1},{17,25},{25,17},{2,10},{10... | collective-permute-start | bytes 196616 | tf_op jit(solution)/shard_map/ppermute | solution.py:269
  40.2 6.9 %collective-permute-start.14 = (bf16[4,64,128]{2,1,0:T(8,128)(2,1)S(1)}, bf16[4,64,128]{2,1,0:T(8,128)(2,1)S(1)}, u32[]{:S(2)}, u32[]{:S(2)}) collective-permute-start(bf16[4,64,128]{2,1,0:T(8,128)(2,1)S(1)} %get-tuple-element.57), channel_id=1, source_target_pairs={{0,16},{8,24},{16,0},{24,8},{1,17},{9,25},{17,1},{25,9},{2,18},{10... | collective-permute-start | bytes 196616 | tf_op jit(solution)/shard_map/ppermute | solution.py:269
  41.7 7.7 %collective-permute-start.15 = (bf16[4,64,128]{2,1,0:T(8,128)(2,1)S(1)}, bf16[4,64,128]{2,1,0:T(8,128)(2,1)S(1)}, u32[]{:S(2)}, u32[]{:S(2)}) collective-permute-start(bf16[4,64,128]{2,1,0:T(8,128)(2,1)S(1)} %get-tuple-element.58), channel_id=1, source_target_pairs={{0,24},{8,16},{16,8},{24,0},{1,25},{9,17},{17,9},{25,1},{2,26},{10... | collective-permute-start | bytes 196616 | tf_op jit(solution)/shard_map/ppermute | solution.py:269
  42.0 9.2 %collective-permute-start.12 = (bf16[4,64,128]{2,1,0:T(8,128)(2,1)S(1)}, bf16[4,64,128]{2,1,0:T(8,128)(2,1)S(1)}, u32[]{:S(2)}, u32[]{:S(2)}) collective-permute-start(bf16[4,64,128]{2,1,0:T(8,128)(2,1)S(1)} %get-tuple-element.63.refs_0_), channel_id=1, source_target_pairs={{0,24},{8,16},{16,8},{24,0},{1,25},{9,17},{17,9},{25,1},{2,26},{10... | collective-permute-start | bytes 196616 | tf_op jit(solution)/shard_map/ppermute | solution.py:269
  44.6 7.5 %collective-permute-start.11 = (bf16[4,64,128]{2,1,0:T(8,128)(2,1)S(1)}, bf16[4,64,128]{2,1,0:T(8,128)(2,1)S(1)}, u32[]{:S(2)}, u32[]{:S(2)}) collective-permute-start(bf16[4,64,128]{2,1,0:T(8,128)(2,1)S(1)} %get-tuple-element.63.refs_0_), channel_id=1, source_target_pairs={{0,16},{8,24},{16,0},{24,8},{1,17},{9,25},{17,1},{25,9},{2,18},{10... | collective-permute-start | bytes 196616 | tf_op jit(solution)/shard_map/ppermute | solution.py:269
  46.4 5.7 %collective-permute-start.10 = (bf16[4,64,128]{2,1,0:T(8,128)(2,1)S(1)}, bf16[4,64,128]{2,1,0:T(8,128)(2,1)S(1)}, u32[]{:S(2)}, u32[]{:S(2)}) collective-permute-start(bf16[4,64,128]{2,1,0:T(8,128)(2,1)S(1)} %get-tuple-element.63.refs_0_), channel_id=1, source_target_pairs={{0,8},{8,0},{16,24},{24,16},{1,9},{9,1},{17,25},{25,17},{2,10},{10... | collective-permute-start | bytes 196616 | tf_op jit(solution)/shard_map/ppermute | solution.py:269
  52.2 1.6 %collective-permute-start.16 = (bf16[16,64,128]{2,1,0:T(8,128)(2,1)S(1)}, bf16[16,64,128]{2,1,0:T(8,128)(2,1)S(1)}, u32[]{:S(2)}, u32[]{:S(2)}) collective-permute-start(bf16[16,64,128]{2,1,0:T(8,128)(2,1)S(1)} %pad_maximum_fusion), channel_id=1, source_target_pairs={{0,1},{1,0},{2,3},{3,2},{4,5},{5,4},{6,7},{7,6},{8,9},{9,8},{10,11... | collective-permute-start | bytes 786440 | tf_op jit(solution)/shard_map/ppermute | solution.py:269

commit v6 on v5

--- a/solution.py
+++ b/solution.py
@@ -166,12 +166,31 @@
 
 
 def return_kernel(plan, *refs):
-    ins, outs = refs[: len(refs) // 2], refs[len(refs) // 2 :]
-    for i in range(plan.line):
-        for r in range(plan.n_row):
-            outs[r][i] = ins[i][r]
-    for ref, to in zip(ins[plan.line :], outs[plan.n_row :]):
+    passed = (len(refs) - 2 - plan.n_row) // 2
+    ins, outs = refs[: 2 + passed], refs[2 + passed :]
+    half = plan.line // 2
+    for r in range(plan.n_row):
+        for s in range(2):
+            for i in range(half):
+                outs[r][s * half + i] = ins[s][i * plan.n_row + r]
+    for ref, to in zip(ins[2:], outs[plan.n_row :]):
         to[...] = ref[...]
+
+
+def join_kernel(plan, *refs):
+    *parts, out_ref = refs
+    first = 0
+    for ref in parts:
+        out_ref[first : first + ref.shape[0]] = ref[...]
+        first += ref.shape[0]
+
+
+def sort_kernel(plan, *refs):
+    plane, outs = refs[: plan.n_row], refs[plan.n_row :]
+    for r, sent in enumerate(plane):
+        for s in range(2):
+            for i, ref in enumerate(outs):
+                ref[2 * r + s] = sent[2 * s + i]
 
 
 def shared_kernel(plan, keep_ref, own_ref, far_ref, *refs):
@@ -198,7 +217,7 @@
             to = jnp.bitwise_xor(col_id // 2, j) * n_row + jnp.bitwise_xor(row_id, row)
             res_ref[to] = jnp.where(first_core, first, second)
     for i, ref in enumerate(out_refs):
-        ref[...] = res_ref[i * n_row : (i + 1) * n_row]
+        ref[...] = res_ref[i * ref.shape[0] : (i + 1) * ref.shape[0]]
 
 
 def extra_kernel(plan, keep_ref, far_ref, *refs):
@@ -243,10 +262,15 @@
     ]
     for copy in copies:
         copy.start()
-    first = 0
-    for size, ref in zip([plan.ndev] + [plan.line] * (plan.shared // plan.line) + [plan.extra], in_refs):
-        stage[first : first + size] = ref[:size]
-        first += size
+    ret_ref, *more_refs = in_refs
+    stage[: plan.ndev] = ret_ref[...]
+    if plan.shared:
+        half = plan.shared // 2
+        for k in range(half):
+            for i in range(2):
+                stage[plan.ndev + 2 * k + i] = more_refs[0][i * half + k]
+        for ref in more_refs[1:]:
+            stage[plan.ndev + plan.shared :] = ref[...]
     for copy in copies:
         copy.wait()
     part = rows_ref.shape[2] // 4
@@ -331,25 +355,46 @@
         far = swapped(own, "col", 1)
         back = pl.pallas_call(
             functools.partial(shared_kernel, plan),
-            out_shape=[blocks(n_row, blk)] * plan.line,
+            out_shape=[blocks(plan.shared // 2, blk)] * 2,
             in_specs=[VMEM] * 3,
-            out_specs=[VMEM] * plan.line,
+            out_specs=[VMEM] * 2,
             scratch_shapes=[square] * 2 + [pltpu.VMEM((plan.shared, blk, 2 * blk), bf16)],
             compiler_params=PARAMS,
             name="shared",
         )(keep, own, far)
         y, keep, first, *rest = lax.optimization_barrier((y, keep, back[0], *rest))
-        back = [first] + list(back[1:])
-        back = back[:1] + [swapped(sent, "col", 2 * i) for i, sent in enumerate(back) if i]
+        back = [first, swapped(back[1], "col", plan.line)]
+        shapes = [blocks(plan.line, blk)] * n_row + [blocks(plan.line * plan.extra, blk)] * min(1, plan.extra)
         back = list(regroup(return_kernel, shapes, "regroup_back", *back, *rest))
         back, rest = back[:n_row], back[n_row:]
         rest = rest + [swapped(sent, "row", r) for sent in rest for r in range(1, n_row)]
         back = [back[0]] + [swapped(sent, "row", r) for r, sent in enumerate(back) if r]
-        if plan.extra:
-            tied = lax.optimization_barrier((*rest, *back))
-            rest, back = tied[:n_row], tied[n_row:]
+        back = pl.pallas_call(
+            functools.partial(sort_kernel, plan),
+            out_shape=[blocks(plan.shared // 2, blk)] * 2,
+            in_specs=[VMEM] * n_row,
+            out_specs=[VMEM] * 2,
+            compiler_params=PARAMS,
+            cost_estimate=pl.CostEstimate(flops=500_000_000, bytes_accessed=0, transcendentals=0),
+            name="sort",
+        )(*back)
+        back = [back[0], swapped(back[1], "col", 2)]
+
+        def join(hint, name, *parts):
+            return pl.pallas_call(
+                functools.partial(join_kernel, plan),
+                out_shape=blocks(sum(part.shape[0] for part in parts), blk),
+                in_specs=[VMEM] * len(parts),
+                out_specs=VMEM,
+                compiler_params=PARAMS,
+                cost_estimate=pl.CostEstimate(flops=hint, bytes_accessed=0, transcendentals=0),
+                name=name,
+            )(*parts)
+
+        back = [join(4_000_000_000, "join_back", *back)]
     if plan.extra:
-        far = swapped(jnp.concatenate(rest), "col", 1)
+        far = swapped(join(1_500_000_000, "join", *rest), "col", 1)
+        far, *back = lax.optimization_barrier((far, *back))
         extra = pl.pallas_call(
             functools.partial(extra_kernel, plan),
             out_shape=blocks(plan.extra, blk),

time: 56.9 us -> 54.8 us (0.963)
  starting transfers between devices: 31.7 us -> 29.5 us
    all_to_all x1, starting transfers between devices: 4.38 us -> 2.62 us  [body(): ret = lax.all_to_all(out, both, 0, 0, tiled=True)]
    ppermute x17 -> x16, starting transfers between devices: 21.3 us -> 20.8 us  [swapped(): lax.ppermute(shard, axis, [(i, i ^ by) for i in range(lax.axis_size(axis))])]
    ppermute x17 -> x16, waiting for transfers between devices: 16 us -> 15.6 us  [swapped(): lax.ppermute(shard, axis, [(i, i ^ by) for i in range(lax.axis_size(axis))])]
  transfers between devices with their start and end apart: 19 -> 18, of which waited for: 13 -> 11; matrix products, arithmetic and copies ran while one was open for 0% -> 0% of each run, Pallas kernels for 7% -> 8%
where the time goes in v6:
time: 54.8 us; the launch traced here: 54 us
  starting transfers between devices  29.5 us (54%)
  waiting for transfers between devices  15.9 us (29%)
  Pallas kernels  8.44 us (15%)
    ppermute x16, starting transfers between devices, swapped(): lax.ppermute(shard, axis, [(i, i ^ by) for i in range(lax.axis_size(axis))])  20.8 us
    ppermute x16, waiting for transfers between devices, swapped(): lax.ppermute(shard, axis, [(i, i ^ by) for i in range(lax.axis_size(axis))])  15.6 us
    all_to_all x1, starting transfers between devices, body(): y = lax.all_to_all(packed, both, 0, 0, tiled=True)  6.07 us
    all_to_all x1, starting transfers between devices, body(): ret = lax.all_to_all(out, both, 0, 0, tiled=True)  2.62 us
    pallas_call x1, Pallas kernels, body(): pl.pallas_call(functools.partial(pack_kernel, plan), out_shape=shapes, in...  2.38 us
    pallas_call x1, Pallas kernels, body(): pl.pallas_call(functools.partial(unpack_kernel, plan), out_shape=jax.Shap...  1.84 us
    pallas_call x1, Pallas kernels, body(): pl.pallas_call(functools.partial(full_kernel, plan), out_shape=blocks(nde...  1.65 us
  transfers between devices with their start and end apart: 18, of which 11 were waited for; matrix products, arithmetic and copies ran while one was open for 0% of the time, Pallas kernels for 8%

profile of v6, /device:TPU:0, one launch (start us, length us, event | category | flops | bytes accessed | tf_op | source)
XLA Modules:
  0.0 54.0 jit_solution(6447377400420186695)
XLA Ops:
  0.0 2.4 %pack.1 = (bf16[32,64,128]{2,1,0:T(8,128)(2,1)}, bf16[5,64,128]{2,1,0:T(8,128)(2,1)}, bf16[5,64,128]{2,1,0:T(8,128)(2,1)}, bf16[5,64,128]{2,1,0:T(8,128)(2,1)}, bf16[5,64,128]{2,1,0:T(8,128)(2,1)}) custom-call(bf16[2,64,2048]{2,1,0:T(8,128)(2,1)} %x_hbm.1, s32[8,8,32]{2,1,0:T(8,128)} %rows_hbm.1, s32[8]{0:T(128)} %shift_hbm.3), custom_call_target="tpu_custom_call" | custom-call | tf_op jit(solution)/shard_map/pack/pallas_call | solution.py:312
  2.4 3.1 %collective-permute-start = (bf16[5,64,128]{2,1,0:T(8,128)(2,1)}, bf16[5,64,128]{2,1,0:T(8,128)(2,1)S(1)}, u32[]{:S(2)}, u32[]{:S(2)}) collective-permute-start(bf16[5,64,128]{2,1,0:T(8,128)(2,1)} %get-tuple-element.32), channel_id=1, source_target_pairs={{0,2},{1,3},{2,0},{3,1},{4,6},{5,7},{6,4},{7,5},{8,10},{9,11},{10,... | collective-permute-start | bytes 245768 | tf_op jit(solution)/shard_map/ppermute | solution.py:293
  5.5 2.6 %collective-permute-start.1 = (bf16[5,64,128]{2,1,0:T(8,128)(2,1)}, bf16[5,64,128]{2,1,0:T(8,128)(2,1)S(1)}, u32[]{:S(2)}, u32[]{:S(2)}) collective-permute-start(bf16[5,64,128]{2,1,0:T(8,128)(2,1)} %get-tuple-element.33), channel_id=1, source_target_pairs={{0,4},{1,5},{2,6},{3,7},{4,0},{5,1},{6,2},{7,3},{8,12},{9,13},{10,... | collective-permute-start | bytes 245768 | tf_op jit(solution)/shard_map/ppermute | solution.py:293
  8.1 0.0 collective-permute-start.2
  8.1 0.0 copy-start.2
  8.1 6.1 %all-to-all-start = ((bf16[32,64,128]{2,1,0:T(8,128)(2,1)}), bf16[32,64,128]{2,1,0:T(8,128)(2,1)S(1)}, u32[]{:S(2)}, u32[]{:S(2)}) async-start(bf16[32,64,128]{2,1,0:T(8,128)(2,1)} %get-tuple-element.30), calls=%async_computation | async-start | bytes 1048576 | tf_op jit(solution)/shard_map/all_to_all | solution.py:326
  14.2 0.0 collective-permute-done.refs_1_
  14.2 0.7 %collective-permute-done.1.refs_2_ = bf16[5,64,128]{2,1,0:T(8,128)(2,1)S(1)} collective-permute-done((bf16[5,64,128]{2,1,0:T(8,128)(2,1)}, bf16[5,64,128]{2,1,0:T(8,128)(2,1)S(1)}, u32[]{:S(2)}, u32[]{:S(2)}) %collective-permute-start.1) | collective-permute-done | bytes 81952 | tf_op jit(solution)/shard_map/ppermute | solution.py:293
  14.9 0.0 collective-permute-done.2.refs_3_
  14.9 0.0 copy-done.2
  14.9 1.6 %collective-permute-start.3 = (bf16[4,64,128]{2,1,0:T(8,128)(2,1)S(1)}, bf16[4,64,128]{2,1,0:T(8,128)(2,1)S(1)}, u32[]{:S(2)}, u32[]{:S(2)}) collective-permute-start(bf16[4,64,128]{2,1,0:T(8,128)(2,1)S(1)} %get-tuple-element.36), channel_id=1, source_target_pairs={{0,8},{8,0},{16,24},{24,16},{1,9},{9,1},{17,25},{25,17},{2,10},{10... | collective-permute-start | bytes 196616 | tf_op jit(solution)/shard_map/ppermute | solution.py:293
  16.5 1.5 %collective-permute-start.4 = (bf16[4,64,128]{2,1,0:T(8,128)(2,1)S(1)}, bf16[4,64,128]{2,1,0:T(8,128)(2,1)S(1)}, u32[]{:S(2)}, u32[]{:S(2)}) collective-permute-start(bf16[4,64,128]{2,1,0:T(8,128)(2,1)S(1)} %get-tuple-element.37), channel_id=1, source_target_pairs={{0,16},{8,24},{16,0},{24,8},{1,17},{9,25},{17,1},{25,9},{2,18},{10... | collective-permute-start | bytes 196616 | tf_op jit(solution)/shard_map/ppermute | solution.py:293
  18.0 0.5 collective-permute-start.5
  18.5 3.8 %collective-permute-done.3 = bf16[4,64,128]{2,1,0:T(8,128)(2,1)S(1)} collective-permute-done((bf16[4,64,128]{2,1,0:T(8,128)(2,1)S(1)}, bf16[4,64,128]{2,1,0:T(8,128)(2,1)S(1)}, u32[]{:S(2)}, u32[]{:S(2)}) %collective-permute-start.3) | collective-permute-done | bytes 65568 | tf_op jit(solution)/shard_map/ppermute | solution.py:293
  22.2 0.4 collective-permute-done.4
  22.6 0.0 copy-start
  22.6 0.0 copy-start.1
  22.7 1.9 %collective-permute-done.5 = bf16[4,64,128]{2,1,0:T(8,128)(2,1)S(1)} collective-permute-done((bf16[4,64,128]{2,1,0:T(8,128)(2,1)S(1)}, bf16[4,64,128]{2,1,0:T(8,128)(2,1)S(1)}, u32[]{:S(2)}, u32[]{:S(2)}) %collective-permute-start.5) | collective-permute-done | bytes 65568 | tf_op jit(solution)/shard_map/ppermute | solution.py:293
  24.6 0.1 collective-permute-start.6
  24.7 0.0 copy-done
  24.7 0.0 copy-done.1
  24.7 0.7 %masks.1.keep_ref = f32[3,8,512]{2,1,0:T(8,128)S(1)} custom-call(s32[8]{0:T(128)S(1)} %copy-done.1, s32[8,8,32]{2,1,0:T(8,128)S(1)} %copy-done), custom_call_target="tpu_custom_call" | custom-call | tf_op jit(solution)/shard_map/masks/pallas_call | solution.py:328
  25.5 0.8 %collective-permute-done.6.far_ref = bf16[16,64,128]{2,1,0:T(8,128)(2,1)S(1)} collective-permute-done((bf16[16,64,128]{2,1,0:T(8,128)(2,1)S(1)}, bf16[16,64,128]{2,1,0:T(8,128)(2,1)S(1)}, u32[]{:S(2)}, u32[]{:S(2)}) %collective-permute-start.6) | collective-permute-done | bytes 262176 | tf_op jit(solution)/shard_map/ppermute | solution.py:293
  26.2 1.0 %shared.1 = (bf16[8,64,128]{2,1,0:T(8,128)(2,1)S(1)}, bf16[8,64,128]{2,1,0:T(8,128)(2,1)S(1)}) custom-call(f32[3,8,512]{2,1,0:T(8,128)S(1)} %masks.1.keep_ref, bf16[16,64,128]{2,1,0:T(8,128)(2,1)S(1)} %constant_dynamic-update-slice_fusion.own_ref, bf16[16,64,128]{2,1,0:T(8,128)(2,1)S(1)} %collective-permute-done.6.far_ref), custom_call_target="tpu_custom_call" | custom-call | tf_op jit(solution)/shard_map/shared/pallas_call | solution.py:356
  27.3 2.9 %collective-permute-start.7 = (bf16[8,64,128]{2,1,0:T(8,128)(2,1)S(1)}, bf16[8,64,128]{2,1,0:T(8,128)(2,1)S(1)}, u32[]{:S(2)}, u32[]{:S(2)}) collective-permute-start(bf16[8,64,128]{2,1,0:T(8,128)(2,1)S(1)} %get-tuple-element.44), channel_id=1, source_target_pairs={{0,4},{1,5},{2,6},{3,7},{4,0},{5,1},{6,2},{7,3},{8,12},{9,13},{10,... | collective-permute-start | bytes 393224 | tf_op jit(solution)/shard_map/ppermute | solution.py:293
  30.2 0.3 all-to-all-done.y_ref
  30.5 1.6 %full.1 = bf16[32,64,128]{2,1,0:T(8,128)(2,1)} custom-call(f32[3,8,512]{2,1,0:T(8,128)S(1)} %masks.1.keep_ref, bf16[32,64,128]{2,1,0:T(8,128)(2,1)S(1)} %all-to-all-done.y_ref), custom_call_target="tpu_custom_call" | custom-call | flops 536870912 | bytes 1048576 | tf_op jit(solution)/shard_map/full/pallas_call | solution.py:408
  32.2 2.6 %all-to-all-start.1 = ((bf16[32,64,128]{2,1,0:T(8,128)(2,1)}), bf16[32,64,128]{2,1,0:T(8,128)(2,1)S(1)}, u32[]{:S(2)}, u32[]{:S(2)}) async-start(bf16[32,64,128]{2,1,0:T(8,128)(2,1)} %full.1), calls=%async_computation.1 | async-start | bytes 1048576 | tf_op jit(solution)/shard_map/all_to_all | solution.py:418
  34.8 2.0 %collective-permute-done.7.refs_1_ = bf16[8,64,128]{2,1,0:T(8,128)(2,1)S(1)} collective-permute-done((bf16[8,64,128]{2,1,0:T(8,128)(2,1)S(1)}, bf16[8,64,128]{2,1,0:T(8,128)(2,1)S(1)}, u32[]{:S(2)}, u32[]{:S(2)}) %collective-permute-start.7) | collective-permute-done | bytes 131104 | tf_op jit(solution)/shard_map/ppermute | solution.py:293
  36.8 0.5 collective-permute-start.12
  37.4 0.7 %collective-permute-start.13 = (bf16[4,64,128]{2,1,0:T(8,128)(2,1)S(1)}, bf16[4,64,128]{2,1,0:T(8,128)(2,1)S(1)}, u32[]{:S(2)}, u32[]{:S(2)}) collective-permute-start(bf16[4,64,128]{2,1,0:T(8,128)(2,1)S(1)} %get-tuple-element.49), channel_id=1, source_target_pairs={{0,16},{8,24},{16,0},{24,8},{1,17},{9,25},{17,1},{25,9},{2,18},{10... | collective-permute-start | bytes 196616 | tf_op jit(solution)/shard_map/ppermute | solution.py:293
  38.0 2.4 %collective-permute-start.14 = (bf16[4,64,128]{2,1,0:T(8,128)(2,1)S(1)}, bf16[4,64,128]{2,1,0:T(8,128)(2,1)S(1)}, u32[]{:S(2)}, u32[]{:S(2)}) collective-permute-start(bf16[4,64,128]{2,1,0:T(8,128)(2,1)S(1)} %get-tuple-element.50), channel_id=1, source_target_pairs={{0,24},{8,16},{16,8},{24,0},{1,25},{9,17},{17,9},{25,1},{2,26},{10... | collective-permute-start | bytes 196616 | tf_op jit(solution)/shard_map/ppermute | solution.py:293
  40.4 0.6 %collective-permute-start.10 = (bf16[4,64,128]{2,1,0:T(8,128)(2,1)S(1)}, bf16[4,64,128]{2,1,0:T(8,128)(2,1)S(1)}, u32[]{:S(2)}, u32[]{:S(2)}) collective-permute-start(bf16[4,64,128]{2,1,0:T(8,128)(2,1)S(1)} %get-tuple-element.46.refs_0_), channel_id=1, source_target_pairs={{0,24},{8,16},{16,8},{24,0},{1,25},{9,17},{17,9},{25,1},{2,26},{10... | collective-permute-start | bytes 196616 | tf_op jit(solution)/shard_map/ppermute | solution.py:293
  41.0 1.3 %collective-permute-start.9 = (bf16[4,64,128]{2,1,0:T(8,128)(2,1)S(1)}, bf16[4,64,128]{2,1,0:T(8,128)(2,1)S(1)}, u32[]{:S(2)}, u32[]{:S(2)}) collective-permute-start(bf16[4,64,128]{2,1,0:T(8,128)(2,1)S(1)} %get-tuple-element.46.refs_0_), channel_id=1, source_target_pairs={{0,16},{8,24},{16,0},{24,8},{1,17},{9,25},{17,1},{25,9},{2,18},{10... | collective-permute-start | bytes 196616 | tf_op jit(solution)/shard_map/ppermute | solution.py:293
  42.3 0.7 %collective-permute-done.12.refs_1_ = bf16[4,64,128]{2,1,0:T(8,128)(2,1)S(1)} collective-permute-done((bf16[4,64,128]{2,1,0:T(8,128)(2,1)S(1)}, bf16[4,64,128]{2,1,0:T(8,128)(2,1)S(1)}, u32[]{:S(2)}, u32[]{:S(2)}) %collective-permute-start.12) | collective-permute-done | bytes 65568 | tf_op jit(solution)/shard_map/ppermute | solution.py:293
  43.0 0.9 %collective-permute-start.8 = (bf16[4,64,128]{2,1,0:T(8,128)(2,1)S(1)}, bf16[4,64,128]{2,1,0:T(8,128)(2,1)S(1)}, u32[]{:S(2)}, u32[]{:S(2)}) collective-permute-start(bf16[4,64,128]{2,1,0:T(8,128)(2,1)S(1)} %get-tuple-element.46.refs_0_), channel_id=1, source_target_pairs={{0,8},{8,0},{16,24},{24,16},{1,9},{9,1},{17,25},{25,17},{2,10},{10... | collective-permute-start | bytes 196616 | tf_op jit(solution)/shard_map/ppermute | solution.py:293
  43.9 0.0 collective-permute-done.13.refs_2_
  43.9 1.8 %collective-permute-done.14.refs_3_ = bf16[4,64,128]{2,1,0:T(8,128)(2,1)S(1)} collective-permute-done((bf16[4,64,128]{2,1,0:T(8,128)(2,1)S(1)}, bf16[4,64,128]{2,1,0:T(8,128)(2,1)S(1)}, u32[]{:S(2)}, u32[]{:S(2)}) %collective-permute-start.14) | collective-permute-done | bytes 65568 | tf_op jit(solution)/shard_map/ppermute | solution.py:293
  45.7 2.1 %collective-permute-start.15 = (bf16[8,64,128]{2,1,0:T(8,128)(2,1)S(1)}, bf16[8,64,128]{2,1,0:T(8,128)(2,1)S(1)}, u32[]{:S(2)}, u32[]{:S(2)}) collective-permute-start(bf16[8,64,128]{2,1,0:T(8,128)(2,1)S(1)} %get-tuple-element.52), channel_id=1, source_target_pairs={{0,2},{1,3},{2,0},{3,1},{4,6},{5,7},{6,4},{7,5},{8,10},{9,11},{10,... | collective-permute-start | bytes 393224 | tf_op jit(solution)/shard_map/ppermute | solution.py:293
  47.9 0.0 collective-permute-done.10.refs_3_
  47.9 0.7 %collective-permute-done.9.refs_2_ = bf16[4,64,128]{2,1,0:T(8,128)(2,1)S(1)} collective-permute-done((bf16[4,64,128]{2,1,0:T(8,128)(2,1)S(1)}, bf16[4,64,128]{2,1,0:T(8,128)(2,1)S(1)}, u32[]{:S(2)}, u32[]{:S(2)}) %collective-permute-start.9) | collective-permute-done | bytes 65568 | tf_op jit(solution)/shard_map/ppermute | solution.py:293
  48.6 0.0 collective-permute-done.8.refs_1_
  48.6 0.1 collective-permute-start.11
  48.7 2.8 %collective-permute-done.15.refs_1_ = bf16[8,64,128]{2,1,0:T(8,128)(2,1)S(1)} collective-permute-done((bf16[8,64,128]{2,1,0:T(8,128)(2,1)S(1)}, bf16[8,64,128]{2,1,0:T(8,128)(2,1)S(1)}, u32[]{:S(2)}, u32[]{:S(2)}) %collective-permute-start.15) | collective-permute-done | bytes 131104 | tf_op jit(solution)/shard_map/ppermute | solution.py:293
  51.5 0.0 collective-permute-done.11.far_ref
  51.5 0.7 %extra.1.refs_2_ = bf16[1,64,128]{2,1,0:T(8,128)(2,1)S(1)} custom-call(f32[3,8,512]{2,1,0:T(8,128)S(1)} %masks.1.keep_ref, bf16[16,64,128]{2,1,0:T(8,128)(2,1)S(1)} %collective-permute-done.11.far_ref, bf16[4,64,128]{2,1,0:T(8,128)(2,1)S(1)} %get-tuple-element.46.refs_0_, bf16[4,64,128]{2,1,0:T(8,128)(2,1)S(1)} %collective-permute-done.8.refs_1_, ...), custom_call_target="tpu_custom_call" | custom-call | tf_op jit(solution)/shard_map/extra/pallas_call | solution.py:398
  52.2 0.0 all-to-all-done.1.refs_0_
  52.2 1.8 %unpack.1 = f32[2,64,2048]{2,1,0:T(8,128)} custom-call(s32[8,8,32]{2,1,0:T(8,128)S(1)} %copy-done, s32[8]{0:T(128)S(1)} %copy-done.1, bf16[32,64,128]{2,1,0:T(8,128)(2,1)S(1)} %all-to-all-done.1.refs_0_, bf16[16,64,128]{2,1,0:T(8,128)(2,1)S(1)} %join_back.1.refs_1_, bf16[1,64,128]{2,1,0:T(8,128)(2,1)S(1)} %extra.1.refs_2_), custom_call_target="tpu_custom_call" | custom-call | tf_op jit(solution)/shard_map/unpack/pallas_call | solution.py:419
  (9 shorter events, 0.1 us)
Async XLA Ops:
  2.4 11.8 %collective-permute-start = (bf16[5,64,128]{2,1,0:T(8,128)(2,1)}, bf16[5,64,128]{2,1,0:T(8,128)(2,1)S(1)}, u32[]{:S(2)}, u32[]{:S(2)}) collective-permute-start(bf16[5,64,128]{2,1,0:T(8,128)(2,1)} %get-tuple-element.32), channel_id=1, source_target_pairs={{0,2},{1,3},{2,0},{3,1},{4,6},{5,7},{6,4},{7,5},{8,10},{9,11},{10,... | collective-permute-start | bytes 245768 | tf_op jit(solution)/shard_map/ppermute | solution.py:293
  5.5 9.4 %collective-permute-start.1 = (bf16[5,64,128]{2,1,0:T(8,128)(2,1)}, bf16[5,64,128]{2,1,0:T(8,128)(2,1)S(1)}, u32[]{:S(2)}, u32[]{:S(2)}) collective-permute-start(bf16[5,64,128]{2,1,0:T(8,128)(2,1)} %get-tuple-element.33), channel_id=1, source_target_pairs={{0,4},{1,5},{2,6},{3,7},{4,0},{5,1},{6,2},{7,3},{8,12},{9,13},{10,... | collective-permute-start | bytes 245768 | tf_op jit(solution)/shard_map/ppermute | solution.py:293
  8.1 6.8 %collective-permute-start.2 = (bf16[5,64,128]{2,1,0:T(8,128)(2,1)}, bf16[5,64,128]{2,1,0:T(8,128)(2,1)S(1)}, u32[]{:S(2)}, u32[]{:S(2)}) collective-permute-start(bf16[5,64,128]{2,1,0:T(8,128)(2,1)} %get-tuple-element.34), channel_id=1, source_target_pairs={{0,6},{1,7},{2,4},{3,5},{4,2},{5,3},{6,0},{7,1},{8,14},{9,15},{10,... | collective-permute-start | bytes 245768 | tf_op jit(solution)/shard_map/ppermute | solution.py:293
  8.1 6.8 %copy-start.2 = (bf16[5,64,128]{2,1,0:T(8,128)(2,1)S(1)}, bf16[5,64,128]{2,1,0:T(8,128)(2,1)}, u32[]{:S(2)}) copy-start(bf16[5,64,128]{2,1,0:T(8,128)(2,1)} %get-tuple-element.31.refs_0_) | copy-start | bytes 245764
  8.1 22.4 %all-to-all-start = ((bf16[32,64,128]{2,1,0:T(8,128)(2,1)}), bf16[32,64,128]{2,1,0:T(8,128)(2,1)S(1)}, u32[]{:S(2)}, u32[]{:S(2)}) async-start(bf16[32,64,128]{2,1,0:T(8,128)(2,1)} %get-tuple-element.30), calls=%async_computation | async-start | bytes 1048576 | tf_op jit(solution)/shard_map/all_to_all | solution.py:326
  14.9 7.3 %collective-permute-start.3 = (bf16[4,64,128]{2,1,0:T(8,128)(2,1)S(1)}, bf16[4,64,128]{2,1,0:T(8,128)(2,1)S(1)}, u32[]{:S(2)}, u32[]{:S(2)}) collective-permute-start(bf16[4,64,128]{2,1,0:T(8,128)(2,1)S(1)} %get-tuple-element.36), channel_id=1, source_target_pairs={{0,8},{8,0},{16,24},{24,16},{1,9},{9,1},{17,25},{25,17},{2,10},{10... | collective-permute-start | bytes 196616 | tf_op jit(solution)/shard_map/ppermute | solution.py:293
  16.5 6.1 %collective-permute-start.4 = (bf16[4,64,128]{2,1,0:T(8,128)(2,1)S(1)}, bf16[4,64,128]{2,1,0:T(8,128)(2,1)S(1)}, u32[]{:S(2)}, u32[]{:S(2)}) collective-permute-start(bf16[4,64,128]{2,1,0:T(8,128)(2,1)S(1)} %get-tuple-element.37), channel_id=1, source_target_pairs={{0,16},{8,24},{16,0},{24,8},{1,17},{9,25},{17,1},{25,9},{2,18},{10... | collective-permute-start | bytes 196616 | tf_op jit(solution)/shard_map/ppermute | solution.py:293
  18.0 6.6 %collective-permute-start.5 = (bf16[4,64,128]{2,1,0:T(8,128)(2,1)S(1)}, bf16[4,64,128]{2,1,0:T(8,128)(2,1)S(1)}, u32[]{:S(2)}, u32[]{:S(2)}) collective-permute-start(bf16[4,64,128]{2,1,0:T(8,128)(2,1)S(1)} %get-tuple-element.38), channel_id=1, source_target_pairs={{0,24},{8,16},{16,8},{24,0},{1,25},{9,17},{17,9},{25,1},{2,26},{10... | collective-permute-start | bytes 196616 | tf_op jit(solution)/shard_map/ppermute | solution.py:293
  22.6 2.1 %copy-start = (s32[8,8,32]{2,1,0:T(8,128)S(1)}, s32[8,8,32]{2,1,0:T(8,128)}, u32[]{:S(2)}) copy-start(s32[8,8,32]{2,1,0:T(8,128)} %kept_hbm.1) | copy-start | bytes 24580
  22.6 2.1 %copy-start.1 = (s32[8]{0:T(128)S(1)}, s32[8]{0:T(128)}, u32[]{:S(2)}) copy-start(s32[8]{0:T(128)} %shift_hbm.3) | copy-start | bytes 100
  24.6 1.6 %collective-permute-start.6 = (bf16[16,64,128]{2,1,0:T(8,128)(2,1)S(1)}, bf16[16,64,128]{2,1,0:T(8,128)(2,1)S(1)}, u32[]{:S(2)}, u32[]{:S(2)}) collective-permute-start(bf16[16,64,128]{2,1,0:T(8,128)(2,1)S(1)} %constant_dynamic-update-slice_fusion.own_ref), channel_id=1, source_target_pairs={{0,1},{1,0},{2,3},{3,2},{4,5},{5,4},{6,7},{7,6},{8,9},{9,8},{10,11... | collective-permute-start | bytes 786440 | tf_op jit(solution)/shard_map/ppermute | solution.py:293
  27.3 9.6 %collective-permute-start.7 = (bf16[8,64,128]{2,1,0:T(8,128)(2,1)S(1)}, bf16[8,64,128]{2,1,0:T(8,128)(2,1)S(1)}, u32[]{:S(2)}, u32[]{:S(2)}) collective-permute-start(bf16[8,64,128]{2,1,0:T(8,128)(2,1)S(1)} %get-tuple-element.44), channel_id=1, source_target_pairs={{0,4},{1,5},{2,6},{3,7},{4,0},{5,1},{6,2},{7,3},{8,12},{9,13},{10,... | collective-permute-start | bytes 393224 | tf_op jit(solution)/shard_map/ppermute | solution.py:293
  32.2 20.0 %all-to-all-start.1 = ((bf16[32,64,128]{2,1,0:T(8,128)(2,1)}), bf16[32,64,128]{2,1,0:T(8,128)(2,1)S(1)}, u32[]{:S(2)}, u32[]{:S(2)}) async-start(bf16[32,64,128]{2,1,0:T(8,128)(2,1)} %full.1), calls=%async_computation.1 | async-start | bytes 1048576 | tf_op jit(solution)/shard_map/all_to_all | solution.py:418
  36.8 6.1 %collective-permute-start.12 = (bf16[4,64,128]{2,1,0:T(8,128)(2,1)S(1)}, bf16[4,64,128]{2,1,0:T(8,128)(2,1)S(1)}, u32[]{:S(2)}, u32[]{:S(2)}) collective-permute-start(bf16[4,64,128]{2,1,0:T(8,128)(2,1)S(1)} %get-tuple-element.48), channel_id=1, source_target_pairs={{0,8},{8,0},{16,24},{24,16},{1,9},{9,1},{17,25},{25,17},{2,10},{10... | collective-permute-start | bytes 196616 | tf_op jit(solution)/shard_map/ppermute | solution.py:293
  37.4 6.5 %collective-permute-start.13 = (bf16[4,64,128]{2,1,0:T(8,128)(2,1)S(1)}, bf16[4,64,128]{2,1,0:T(8,128)(2,1)S(1)}, u32[]{:S(2)}, u32[]{:S(2)}) collective-permute-start(bf16[4,64,128]{2,1,0:T(8,128)(2,1)S(1)} %get-tuple-element.49), channel_id=1, source_target_pairs={{0,16},{8,24},{16,0},{24,8},{1,17},{9,25},{17,1},{25,9},{2,18},{10... | collective-permute-start | bytes 196616 | tf_op jit(solution)/shard_map/ppermute | solution.py:293
  38.0 7.7 %collective-permute-start.14 = (bf16[4,64,128]{2,1,0:T(8,128)(2,1)S(1)}, bf16[4,64,128]{2,1,0:T(8,128)(2,1)S(1)}, u32[]{:S(2)}, u32[]{:S(2)}) collective-permute-start(bf16[4,64,128]{2,1,0:T(8,128)(2,1)S(1)} %get-tuple-element.50), channel_id=1, source_target_pairs={{0,24},{8,16},{16,8},{24,0},{1,25},{9,17},{17,9},{25,1},{2,26},{10... | collective-permute-start | bytes 196616 | tf_op jit(solution)/shard_map/ppermute | solution.py:293
  40.4 7.5 %collective-permute-start.10 = (bf16[4,64,128]{2,1,0:T(8,128)(2,1)S(1)}, bf16[4,64,128]{2,1,0:T(8,128)(2,1)S(1)}, u32[]{:S(2)}, u32[]{:S(2)}) collective-permute-start(bf16[4,64,128]{2,1,0:T(8,128)(2,1)S(1)} %get-tuple-element.46.refs_0_), channel_id=1, source_target_pairs={{0,24},{8,16},{16,8},{24,0},{1,25},{9,17},{17,9},{25,1},{2,26},{10... | collective-permute-start | bytes 196616 | tf_op jit(solution)/shard_map/ppermute | solution.py:293
  41.0 7.6 %collective-permute-start.9 = (bf16[4,64,128]{2,1,0:T(8,128)(2,1)S(1)}, bf16[4,64,128]{2,1,0:T(8,128)(2,1)S(1)}, u32[]{:S(2)}, u32[]{:S(2)}) collective-permute-start(bf16[4,64,128]{2,1,0:T(8,128)(2,1)S(1)} %get-tuple-element.46.refs_0_), channel_id=1, source_target_pairs={{0,16},{8,24},{16,0},{24,8},{1,17},{9,25},{17,1},{25,9},{2,18},{10... | collective-permute-start | bytes 196616 | tf_op jit(solution)/shard_map/ppermute | solution.py:293
  43.0 5.6 %collective-permute-start.8 = (bf16[4,64,128]{2,1,0:T(8,128)(2,1)S(1)}, bf16[4,64,128]{2,1,0:T(8,128)(2,1)S(1)}, u32[]{:S(2)}, u32[]{:S(2)}) collective-permute-start(bf16[4,64,128]{2,1,0:T(8,128)(2,1)S(1)} %get-tuple-element.46.refs_0_), channel_id=1, source_target_pairs={{0,8},{8,0},{16,24},{24,16},{1,9},{9,1},{17,25},{25,17},{2,10},{10... | collective-permute-start | bytes 196616 | tf_op jit(solution)/shard_map/ppermute | solution.py:293
  45.7 5.7 %collective-permute-start.15 = (bf16[8,64,128]{2,1,0:T(8,128)(2,1)S(1)}, bf16[8,64,128]{2,1,0:T(8,128)(2,1)S(1)}, u32[]{:S(2)}, u32[]{:S(2)}) collective-permute-start(bf16[8,64,128]{2,1,0:T(8,128)(2,1)S(1)} %get-tuple-element.52), channel_id=1, source_target_pairs={{0,2},{1,3},{2,0},{3,1},{4,6},{5,7},{6,4},{7,5},{8,10},{9,11},{10,... | collective-permute-start | bytes 393224 | tf_op jit(solution)/shard_map/ppermute | solution.py:293
  48.6 2.9 %collective-permute-start.11 = (bf16[16,64,128]{2,1,0:T(8,128)(2,1)S(1)}, bf16[16,64,128]{2,1,0:T(8,128)(2,1)S(1)}, u32[]{:S(2)}, u32[]{:S(2)}) collective-permute-start(bf16[16,64,128]{2,1,0:T(8,128)(2,1)S(1)} %join.1), channel_id=1, source_target_pairs={{0,1},{1,0},{2,3},{3,2},{4,5},{5,4},{6,7},{7,6},{8,9},{9,8},{10,11... | collective-permute-start | bytes 786440 | tf_op jit(solution)/shard_map/ppermute | solution.py:293

commit v7 on v6

--- a/solution.py
+++ b/solution.py
@@ -130,7 +130,7 @@
         s_ref[at] = jnp.where(keep_ref[k, panel : panel + 1] > 0, s[at], 0.0).astype(jnp.bfloat16)
 
 
-def full_kernel(plan, keep_ref, y_ref, out_hbm, m_ref, s_ref, res_ref, sems):
+def full_kernel(plan, keep_ref, y_ref, res_ref, m_ref, s_ref):
     blk, n_col = plan.blk, plan.n_col
     for r in range(plan.n_row):
         for j in range(n_col // 2):
@@ -141,18 +141,12 @@
             m_ref[(2 * r + 1) * blk : (2 * r + 2) * blk, lanes] = second
     m = m_ref[...]
     mask_square(plan, dot(m, m), keep_ref, 0, s_ref)
-    copies = []
     for r in range(plan.n_row):
         res = purify(s_ref[2 * r * blk : (2 * r + 2) * blk], m).astype(jnp.bfloat16)
         for j in range(n_col // 2):
             lanes = slice(2 * j * blk, (2 * j + 2) * blk)
             to = r * n_col + 2 * j
             res_ref[to], res_ref[to + 1] = split_pair(res[:blk, lanes], res[blk:, lanes])
-        at = pl.ds(r * n_col, n_col)
-        copies.append(pltpu.make_async_copy(res_ref.at[at], out_hbm.at[at], sems.at[r]))
-        copies[-1].start()
-    for copy in copies:
-        copy.wait()
 
 
 def regroup_kernel(plan, *refs):
@@ -220,39 +214,38 @@
         ref[...] = res_ref[i * ref.shape[0] : (i + 1) * ref.shape[0]]
 
 
-def extra_kernel(plan, keep_ref, far_ref, *refs):
-    own_refs, (out_ref, m_ref, o_ref) = refs[: plan.n_row], refs[plan.n_row :]
+def extra_block(plan, k, keep_ref, far_ref, *refs):
+    own_refs, (m_ref, o_ref) = refs[: plan.n_row], refs[plan.n_row :]
     row_id, col_id = lax.axis_index("row"), lax.axis_index("col")
     first_core = col_id % 2 == 0
     blk, line = plan.blk, plan.line
-    for k in range(plan.extra):
-        for r, own_ref in enumerate(own_refs):
-            start = pl.multiple_of(jnp.bitwise_xor(row_id, r) * 2 * blk, 2 * blk)
-            for j in range(line):
-                lanes = slice(2 * j * blk, (2 * j + 2) * blk)
-                at = k * line + jnp.bitwise_xor(col_id // 2, j)
-                own, far = own_ref[at], far_ref[r * plan.extra * line + at]
-                pair = split_pair(jnp.where(first_core, own, far), jnp.where(first_core, far, own))
-                tile = jnp.concatenate(pair, axis=0)
-                m_ref[pl.ds(start, 2 * blk), lanes] = tile
-                if r == 0:
-                    o_ref[:, lanes] = tile
-        m = m_ref[...]
-        s = dot(o_ref[...], m)
-        kept = []
-        for p in range(2):
-            keep = keep_ref[2 + k, pl.ds(2 * row_id + p, 1)]
-            kept.append(jnp.where(keep > 0, s[p * blk : (p + 1) * blk], 0.0).astype(jnp.bfloat16))
-        res = purify(jnp.concatenate(kept, axis=0), m)
-        mine = res[:, : 2 * blk]
-        for j in range(1, line):
-            mine = jnp.where(col_id // 2 == j, res[:, 2 * j * blk : (2 * j + 2) * blk], mine)
-        first, second = split_pair(mine[:blk], mine[blk:])
-        out_ref[k] = jnp.where(first_core, first, second).astype(jnp.bfloat16)
-
-
-def unpack_kernel(plan, kept_hbm, shift_hbm, *refs):
-    *in_refs, out_hbm, rows_ref, shift_ref, stage, out_ref, sems = refs
+    for r, own_ref in enumerate(own_refs):
+        start = pl.multiple_of(jnp.bitwise_xor(row_id, r) * 2 * blk, 2 * blk)
+        for j in range(line):
+            lanes = slice(2 * j * blk, (2 * j + 2) * blk)
+            at = k * line + jnp.bitwise_xor(col_id // 2, j)
+            own, far = own_ref[at], far_ref[r * plan.extra * line + at]
+            pair = split_pair(jnp.where(first_core, own, far), jnp.where(first_core, far, own))
+            tile = jnp.concatenate(pair, axis=0)
+            m_ref[pl.ds(start, 2 * blk), lanes] = tile
+            if r == 0:
+                o_ref[:, lanes] = tile
+    m = m_ref[...]
+    s = dot(o_ref[...], m)
+    kept = []
+    for p in range(2):
+        keep = keep_ref[2 + k, pl.ds(2 * row_id + p, 1)]
+        kept.append(jnp.where(keep > 0, s[p * blk : (p + 1) * blk], 0.0).astype(jnp.bfloat16))
+    res = purify(jnp.concatenate(kept, axis=0), m)
+    mine = res[:, : 2 * blk]
+    for j in range(1, line):
+        mine = jnp.where(col_id // 2 == j, res[:, 2 * j * blk : (2 * j + 2) * blk], mine)
+    first, second = split_pair(mine[:blk], mine[blk:])
+    return jnp.where(first_core, first, second).astype(jnp.bfloat16)
+
+
+def unpack_kernel(plan, kept_hbm, shift_hbm, ret_ref, *refs):
+    *more_refs, out_hbm, rows_ref, shift_ref, stage, out_ref, m_ref, o_ref, sems = refs
     row_id, col_id = lax.axis_index("row"), lax.axis_index("col")
     blk = plan.blk
     chip = row_id * plan.line + col_id // 2
@@ -262,15 +255,14 @@
     ]
     for copy in copies:
         copy.start()
-    ret_ref, *more_refs = in_refs
     stage[: plan.ndev] = ret_ref[...]
     if plan.shared:
         half = plan.shared // 2
         for k in range(half):
             for i in range(2):
                 stage[plan.ndev + 2 * k + i] = more_refs[0][i * half + k]
-        for ref in more_refs[1:]:
-            stage[plan.ndev + plan.shared :] = ref[...]
+    for k in range(plan.extra):
+        stage[plan.ndev + plan.shared + k] = extra_block(plan, k, *more_refs[1:], m_ref, o_ref)
     for copy in copies:
         copy.wait()
     part = rows_ref.shape[2] // 4
@@ -395,22 +387,13 @@
     if plan.extra:
         far = swapped(join(1_500_000_000, "join", *rest), "col", 1)
         far, *back = lax.optimization_barrier((far, *back))
-        extra = pl.pallas_call(
-            functools.partial(extra_kernel, plan),
-            out_shape=blocks(plan.extra, blk),
-            in_specs=[VMEM] * (2 + n_row),
-            out_specs=VMEM,
-            scratch_shapes=[square, pltpu.VMEM((2 * blk, size), bf16)],
-            compiler_params=PARAMS,
-            name="extra",
-        )(keep, far, *rest)
-        extra = [extra]
+        extra = [keep, far, *rest]
     out = pl.pallas_call(
         functools.partial(full_kernel, plan),
         out_shape=blocks(ndev, blk),
         in_specs=[VMEM] * 2,
-        out_specs=HBM,
-        scratch_shapes=[square] * 2 + [pltpu.VMEM((ndev, blk, 2 * blk), bf16), pltpu.SemaphoreType.DMA((n_row,))],
+        out_specs=VMEM,
+        scratch_shapes=[square] * 2,
         compiler_params=PARAMS,
         cost_estimate=pl.CostEstimate(flops=4 * size**3, bytes_accessed=8 * ndev * blk * blk, transcendentals=0),
         name="full",
@@ -425,6 +408,8 @@
         + [
             pltpu.VMEM((ndev + plan.shared + plan.extra, blk, 2 * blk), bf16),
             pltpu.VMEM(density.shape, jnp.float32),
+            square,
+            pltpu.VMEM((2 * blk, size), bf16),
             pltpu.SemaphoreType.DMA((10,)),
         ],
         compiler_params=PARAMS,

time: 54.8 us -> 54.2 us (0.989)
    pallas_call x1 -> x0, Pallas kernels: 0.7 us -> none  [body(): pl.pallas_call(functools.partial(extra_kernel, plan), out_shape=blocks(pl...]
  transfers between devices with their start and end apart: 18 -> 18, of which waited for: 11 -> 11; matrix products, arithmetic and copies ran while one was open for 0% -> 0% of each run, Pallas kernels for 8% -> 7%
where the time goes in v7:
time: 54.2 us; the launch traced here: 53.9 us
  starting transfers between devices  29.4 us (54%)
  waiting for transfers between devices  15.9 us (29%)
  Pallas kernels  8.33 us (15%)
    ppermute x16, starting transfers between devices, swapped(): lax.ppermute(shard, axis, [(i, i ^ by) for i in range(lax.axis_size(axis))])  20.7 us
    ppermute x16, waiting for transfers between devices, swapped(): lax.ppermute(shard, axis, [(i, i ^ by) for i in range(lax.axis_size(axis))])  15.6 us
    all_to_all x1, starting transfers between devices, body(): y = lax.all_to_all(packed, both, 0, 0, tiled=True)  6.07 us
    all_to_all x1, starting transfers between devices, body(): ret = lax.all_to_all(out, both, 0, 0, tiled=True)  2.61 us
    pallas_call x1, Pallas kernels, body(): pl.pallas_call(functools.partial(pack_kernel, plan), out_shape=shapes, in...  2.39 us
    pallas_call x1, Pallas kernels, body(): pl.pallas_call(functools.partial(unpack_kernel, plan), out_shape=jax.Shap...  2.33 us
    pallas_call x1, Pallas kernels, body(): pl.pallas_call(functools.partial(full_kernel, plan), out_shape=blocks(nde...  1.75 us
  transfers between devices with their start and end apart: 18, of which 11 were waited for; matrix products, arithmetic and copies ran while one was open for 0% of the time, Pallas kernels for 7%

profile of v7, /device:TPU:0, one launch (start us, length us, event | category | flops | bytes accessed | tf_op | source)
XLA Modules:
  0.0 53.9 jit_solution(8330583474586653888)
XLA Ops:
  0.0 2.4 %pack.1 = (bf16[32,64,128]{2,1,0:T(8,128)(2,1)}, bf16[5,64,128]{2,1,0:T(8,128)(2,1)}, bf16[5,64,128]{2,1,0:T(8,128)(2,1)}, bf16[5,64,128]{2,1,0:T(8,128)(2,1)}, bf16[5,64,128]{2,1,0:T(8,128)(2,1)}) custom-call(bf16[2,64,2048]{2,1,0:T(8,128)(2,1)} %x_hbm.1, s32[8,8,32]{2,1,0:T(8,128)} %rows_hbm.1, s32[8]{0:T(128)} %shift_hbm.3), custom_call_target="tpu_custom_call" | custom-call | tf_op jit(solution)/shard_map/pack/pallas_call | solution.py:304
  2.4 3.1 %collective-permute-start = (bf16[5,64,128]{2,1,0:T(8,128)(2,1)}, bf16[5,64,128]{2,1,0:T(8,128)(2,1)S(1)}, u32[]{:S(2)}, u32[]{:S(2)}) collective-permute-start(bf16[5,64,128]{2,1,0:T(8,128)(2,1)} %get-tuple-element.32), channel_id=1, source_target_pairs={{0,2},{1,3},{2,0},{3,1},{4,6},{5,7},{6,4},{7,5},{8,10},{9,11},{10,... | collective-permute-start | bytes 245768 | tf_op jit(solution)/shard_map/ppermute | solution.py:285
  5.5 2.6 %collective-permute-start.1 = (bf16[5,64,128]{2,1,0:T(8,128)(2,1)}, bf16[5,64,128]{2,1,0:T(8,128)(2,1)S(1)}, u32[]{:S(2)}, u32[]{:S(2)}) collective-permute-start(bf16[5,64,128]{2,1,0:T(8,128)(2,1)} %get-tuple-element.33), channel_id=1, source_target_pairs={{0,4},{1,5},{2,6},{3,7},{4,0},{5,1},{6,2},{7,3},{8,12},{9,13},{10,... | collective-permute-start | bytes 245768 | tf_op jit(solution)/shard_map/ppermute | solution.py:285
  8.1 0.0 collective-permute-start.2
  8.1 0.0 copy-start.2
  8.1 6.1 %all-to-all-start = ((bf16[32,64,128]{2,1,0:T(8,128)(2,1)}), bf16[32,64,128]{2,1,0:T(8,128)(2,1)S(1)}, u32[]{:S(2)}, u32[]{:S(2)}) async-start(bf16[32,64,128]{2,1,0:T(8,128)(2,1)} %get-tuple-element.30), calls=%async_computation | async-start | bytes 1048576 | tf_op jit(solution)/shard_map/all_to_all | solution.py:318
  14.2 0.0 collective-permute-done.refs_1_
  14.2 0.7 %collective-permute-done.1.refs_2_ = bf16[5,64,128]{2,1,0:T(8,128)(2,1)S(1)} collective-permute-done((bf16[5,64,128]{2,1,0:T(8,128)(2,1)}, bf16[5,64,128]{2,1,0:T(8,128)(2,1)S(1)}, u32[]{:S(2)}, u32[]{:S(2)}) %collective-permute-start.1) | collective-permute-done | bytes 81952 | tf_op jit(solution)/shard_map/ppermute | solution.py:285
  14.9 0.0 collective-permute-done.2.refs_3_
  14.9 0.0 copy-done.2
  14.9 1.6 %collective-permute-start.3 = (bf16[4,64,128]{2,1,0:T(8,128)(2,1)S(1)}, bf16[4,64,128]{2,1,0:T(8,128)(2,1)S(1)}, u32[]{:S(2)}, u32[]{:S(2)}) collective-permute-start(bf16[4,64,128]{2,1,0:T(8,128)(2,1)S(1)} %get-tuple-element.36), channel_id=1, source_target_pairs={{0,8},{8,0},{16,24},{24,16},{1,9},{9,1},{17,25},{25,17},{2,10},{10... | collective-permute-start | bytes 196616 | tf_op jit(solution)/shard_map/ppermute | solution.py:285
  16.5 1.5 %collective-permute-start.4 = (bf16[4,64,128]{2,1,0:T(8,128)(2,1)S(1)}, bf16[4,64,128]{2,1,0:T(8,128)(2,1)S(1)}, u32[]{:S(2)}, u32[]{:S(2)}) collective-permute-start(bf16[4,64,128]{2,1,0:T(8,128)(2,1)S(1)} %get-tuple-element.37), channel_id=1, source_target_pairs={{0,16},{8,24},{16,0},{24,8},{1,17},{9,25},{17,1},{25,9},{2,18},{10... | collective-permute-start | bytes 196616 | tf_op jit(solution)/shard_map/ppermute | solution.py:285
  18.0 0.5 collective-permute-start.5
  18.5 3.8 %collective-permute-done.3 = bf16[4,64,128]{2,1,0:T(8,128)(2,1)S(1)} collective-permute-done((bf16[4,64,128]{2,1,0:T(8,128)(2,1)S(1)}, bf16[4,64,128]{2,1,0:T(8,128)(2,1)S(1)}, u32[]{:S(2)}, u32[]{:S(2)}) %collective-permute-start.3) | collective-permute-done | bytes 65568 | tf_op jit(solution)/shard_map/ppermute | solution.py:285
  22.2 0.4 collective-permute-done.4
  22.6 0.0 copy-start
  22.6 0.0 copy-start.1
  22.7 1.9 %collective-permute-done.5 = bf16[4,64,128]{2,1,0:T(8,128)(2,1)S(1)} collective-permute-done((bf16[4,64,128]{2,1,0:T(8,128)(2,1)S(1)}, bf16[4,64,128]{2,1,0:T(8,128)(2,1)S(1)}, u32[]{:S(2)}, u32[]{:S(2)}) %collective-permute-start.5) | collective-permute-done | bytes 65568 | tf_op jit(solution)/shard_map/ppermute | solution.py:285
  24.6 0.1 collective-permute-start.6
  24.7 0.0 copy-done
  24.7 0.0 copy-done.1
  24.7 0.7 %masks.1.keep_ref.refs_1_ = f32[3,8,512]{2,1,0:T(8,128)S(1)} custom-call(s32[8]{0:T(128)S(1)} %copy-done.1, s32[8,8,32]{2,1,0:T(8,128)S(1)} %copy-done), custom_call_target="tpu_custom_call" | custom-call | tf_op jit(solution)/shard_map/masks/pallas_call | solution.py:320
  25.5 0.8 %collective-permute-done.6.far_ref = bf16[16,64,128]{2,1,0:T(8,128)(2,1)S(1)} collective-permute-done((bf16[16,64,128]{2,1,0:T(8,128)(2,1)S(1)}, bf16[16,64,128]{2,1,0:T(8,128)(2,1)S(1)}, u32[]{:S(2)}, u32[]{:S(2)}) %collective-permute-start.6) | collective-permute-done | bytes 262176 | tf_op jit(solution)/shard_map/ppermute | solution.py:285
  26.2 1.0 %shared.1 = (bf16[8,64,128]{2,1,0:T(8,128)(2,1)S(1)}, bf16[8,64,128]{2,1,0:T(8,128)(2,1)S(1)}) custom-call(f32[3,8,512]{2,1,0:T(8,128)S(1)} %masks.1.keep_ref.refs_1_, bf16[16,64,128]{2,1,0:T(8,128)(2,1)S(1)} %constant_dynamic-update-slice_fusion.own_ref, bf16[16,64,128]{2,1,0:T(8,128)(2,1)S(1)} %collective-permute-done.6.far_ref), custom_call_target="tpu_custom_call" | custom-call | tf_op jit(solution)/shard_map/shared/pallas_call | solution.py:348
  27.3 2.9 %collective-permute-start.7 = (bf16[8,64,128]{2,1,0:T(8,128)(2,1)S(1)}, bf16[8,64,128]{2,1,0:T(8,128)(2,1)S(1)}, u32[]{:S(2)}, u32[]{:S(2)}) collective-permute-start(bf16[8,64,128]{2,1,0:T(8,128)(2,1)S(1)} %get-tuple-element.44), channel_id=1, source_target_pairs={{0,4},{1,5},{2,6},{3,7},{4,0},{5,1},{6,2},{7,3},{8,12},{9,13},{10,... | collective-permute-start | bytes 393224 | tf_op jit(solution)/shard_map/ppermute | solution.py:285
  30.2 0.3 all-to-all-done.y_ref
  30.5 1.8 %full.1 = bf16[32,64,128]{2,1,0:T(8,128)(2,1)} custom-call(f32[3,8,512]{2,1,0:T(8,128)S(1)} %masks.1.keep_ref.refs_1_, bf16[32,64,128]{2,1,0:T(8,128)(2,1)S(1)} %all-to-all-done.y_ref), custom_call_target="tpu_custom_call" | custom-call | flops 536870912 | bytes 1048576 | tf_op jit(solution)/shard_map/full/pallas_call | solution.py:391
  32.3 2.6 %all-to-all-start.1 = ((bf16[32,64,128]{2,1,0:T(8,128)(2,1)}), bf16[32,64,128]{2,1,0:T(8,128)(2,1)S(1)}, u32[]{:S(2)}, u32[]{:S(2)}) async-start(bf16[32,64,128]{2,1,0:T(8,128)(2,1)} %full.1), calls=%async_computation.1 | async-start | bytes 1048576 | tf_op jit(solution)/shard_map/all_to_all | solution.py:401
  34.9 1.9 %collective-permute-done.7.refs_1_ = bf16[8,64,128]{2,1,0:T(8,128)(2,1)S(1)} collective-permute-done((bf16[8,64,128]{2,1,0:T(8,128)(2,1)S(1)}, bf16[8,64,128]{2,1,0:T(8,128)(2,1)S(1)}, u32[]{:S(2)}, u32[]{:S(2)}) %collective-permute-start.7) | collective-permute-done | bytes 131104 | tf_op jit(solution)/shard_map/ppermute | solution.py:285
  36.8 0.5 collective-permute-start.12
  37.4 0.8 %collective-permute-start.13 = (bf16[4,64,128]{2,1,0:T(8,128)(2,1)S(1)}, bf16[4,64,128]{2,1,0:T(8,128)(2,1)S(1)}, u32[]{:S(2)}, u32[]{:S(2)}) collective-permute-start(bf16[4,64,128]{2,1,0:T(8,128)(2,1)S(1)} %get-tuple-element.49), channel_id=1, source_target_pairs={{0,16},{8,24},{16,0},{24,8},{1,17},{9,25},{17,1},{25,9},{2,18},{10... | collective-permute-start | bytes 196616 | tf_op jit(solution)/shard_map/ppermute | solution.py:285
  38.1 2.3 %collective-permute-start.14 = (bf16[4,64,128]{2,1,0:T(8,128)(2,1)S(1)}, bf16[4,64,128]{2,1,0:T(8,128)(2,1)S(1)}, u32[]{:S(2)}, u32[]{:S(2)}) collective-permute-start(bf16[4,64,128]{2,1,0:T(8,128)(2,1)S(1)} %get-tuple-element.50), channel_id=1, source_target_pairs={{0,24},{8,16},{16,8},{24,0},{1,25},{9,17},{17,9},{25,1},{2,26},{10... | collective-permute-start | bytes 196616 | tf_op jit(solution)/shard_map/ppermute | solution.py:285
  40.4 0.6 %collective-permute-start.10 = (bf16[4,64,128]{2,1,0:T(8,128)(2,1)S(1)}, bf16[4,64,128]{2,1,0:T(8,128)(2,1)S(1)}, u32[]{:S(2)}, u32[]{:S(2)}) collective-permute-start(bf16[4,64,128]{2,1,0:T(8,128)(2,1)S(1)} %get-tuple-element.46.refs_0_.refs_3_), channel_id=1, source_target_pairs={{0,24},{8,16},{16,8},{24,0},{1,25},{9,17},{17,9},{25,1},{2,26},{10... | collective-permute-start | bytes 196616 | tf_op jit(solution)/shard_map/ppermute | solution.py:285
  41.0 1.3 %collective-permute-start.9 = (bf16[4,64,128]{2,1,0:T(8,128)(2,1)S(1)}, bf16[4,64,128]{2,1,0:T(8,128)(2,1)S(1)}, u32[]{:S(2)}, u32[]{:S(2)}) collective-permute-start(bf16[4,64,128]{2,1,0:T(8,128)(2,1)S(1)} %get-tuple-element.46.refs_0_.refs_3_), channel_id=1, source_target_pairs={{0,16},{8,24},{16,0},{24,8},{1,17},{9,25},{17,1},{25,9},{2,18},{10... | collective-permute-start | bytes 196616 | tf_op jit(solution)/shard_map/ppermute | solution.py:285
  42.3 0.8 %collective-permute-done.12.refs_1_ = bf16[4,64,128]{2,1,0:T(8,128)(2,1)S(1)} collective-permute-done((bf16[4,64,128]{2,1,0:T(8,128)(2,1)S(1)}, bf16[4,64,128]{2,1,0:T(8,128)(2,1)S(1)}, u32[]{:S(2)}, u32[]{:S(2)}) %collective-permute-start.12) | collective-permute-done | bytes 65568 | tf_op jit(solution)/shard_map/ppermute | solution.py:285
  43.1 0.8 %collective-permute-start.8 = (bf16[4,64,128]{2,1,0:T(8,128)(2,1)S(1)}, bf16[4,64,128]{2,1,0:T(8,128)(2,1)S(1)}, u32[]{:S(2)}, u32[]{:S(2)}) collective-permute-start(bf16[4,64,128]{2,1,0:T(8,128)(2,1)S(1)} %get-tuple-element.46.refs_0_.refs_3_), channel_id=1, source_target_pairs={{0,8},{8,0},{16,24},{24,16},{1,9},{9,1},{17,25},{25,17},{2,10},{10... | collective-permute-start | bytes 196616 | tf_op jit(solution)/shard_map/ppermute | solution.py:285
  43.9 0.0 collective-permute-done.13.refs_2_
  43.9 1.9 %collective-permute-done.14.refs_3_ = bf16[4,64,128]{2,1,0:T(8,128)(2,1)S(1)} collective-permute-done((bf16[4,64,128]{2,1,0:T(8,128)(2,1)S(1)}, bf16[4,64,128]{2,1,0:T(8,128)(2,1)S(1)}, u32[]{:S(2)}, u32[]{:S(2)}) %collective-permute-start.14) | collective-permute-done | bytes 65568 | tf_op jit(solution)/shard_map/ppermute | solution.py:285
  45.8 2.1 %collective-permute-start.15 = (bf16[8,64,128]{2,1,0:T(8,128)(2,1)S(1)}, bf16[8,64,128]{2,1,0:T(8,128)(2,1)S(1)}, u32[]{:S(2)}, u32[]{:S(2)}) collective-permute-start(bf16[8,64,128]{2,1,0:T(8,128)(2,1)S(1)} %get-tuple-element.52), channel_id=1, source_target_pairs={{0,2},{1,3},{2,0},{3,1},{4,6},{5,7},{6,4},{7,5},{8,10},{9,11},{10,... | collective-permute-start | bytes 393224 | tf_op jit(solution)/shard_map/ppermute | solution.py:285
  47.9 0.0 collective-permute-done.10.refs_3_.refs_6_
  47.9 0.7 %collective-permute-done.9.refs_2_.refs_5_ = bf16[4,64,128]{2,1,0:T(8,128)(2,1)S(1)} collective-permute-done((bf16[4,64,128]{2,1,0:T(8,128)(2,1)S(1)}, bf16[4,64,128]{2,1,0:T(8,128)(2,1)S(1)}, u32[]{:S(2)}, u32[]{:S(2)}) %collective-permute-start.9) | collective-permute-done | bytes 65568 | tf_op jit(solution)/shard_map/ppermute | solution.py:285
  48.6 0.0 collective-permute-done.8.refs_1_.refs_4_
  48.6 0.1 collective-permute-start.11
  48.7 2.8 %collective-permute-done.15.refs_1_ = bf16[8,64,128]{2,1,0:T(8,128)(2,1)S(1)} collective-permute-done((bf16[8,64,128]{2,1,0:T(8,128)(2,1)S(1)}, bf16[8,64,128]{2,1,0:T(8,128)(2,1)S(1)}, u32[]{:S(2)}, u32[]{:S(2)}) %collective-permute-start.15) | collective-permute-done | bytes 131104 | tf_op jit(solution)/shard_map/ppermute | solution.py:285
  51.5 0.0 collective-permute-done.11.refs_2_
  51.6 0.0 all-to-all-done.1.ret_ref
  51.6 2.3 %unpack.1 = f32[2,64,2048]{2,1,0:T(8,128)} custom-call(s32[8,8,32]{2,1,0:T(8,128)S(1)} %copy-done, s32[8]{0:T(128)S(1)} %copy-done.1, bf16[32,64,128]{2,1,0:T(8,128)(2,1)S(1)} %all-to-all-done.1.ret_ref, bf16[16,64,128]{2,1,0:T(8,128)(2,1)S(1)} %join_back.1.refs_0_, f32[3,8,512]{2,1,0:T(8,128)S(1)} %masks.1.keep_ref.refs_1_, ...), custom_call_target="tpu_custom_call" | custom-call | tf_op jit(solution)/shard_map/unpack/pallas_call | solution.py:402
  (9 shorter events, 0.1 us)
Async XLA Ops:
  2.4 11.8 %collective-permute-start = (bf16[5,64,128]{2,1,0:T(8,128)(2,1)}, bf16[5,64,128]{2,1,0:T(8,128)(2,1)S(1)}, u32[]{:S(2)}, u32[]{:S(2)}) collective-permute-start(bf16[5,64,128]{2,1,0:T(8,128)(2,1)} %get-tuple-element.32), channel_id=1, source_target_pairs={{0,2},{1,3},{2,0},{3,1},{4,6},{5,7},{6,4},{7,5},{8,10},{9,11},{10,... | collective-permute-start | bytes 245768 | tf_op jit(solution)/shard_map/ppermute | solution.py:285
  5.5 9.4 %collective-permute-start.1 = (bf16[5,64,128]{2,1,0:T(8,128)(2,1)}, bf16[5,64,128]{2,1,0:T(8,128)(2,1)S(1)}, u32[]{:S(2)}, u32[]{:S(2)}) collective-permute-start(bf16[5,64,128]{2,1,0:T(8,128)(2,1)} %get-tuple-element.33), channel_id=1, source_target_pairs={{0,4},{1,5},{2,6},{3,7},{4,0},{5,1},{6,2},{7,3},{8,12},{9,13},{10,... | collective-permute-start | bytes 245768 | tf_op jit(solution)/shard_map/ppermute | solution.py:285
  8.1 6.8 %collective-permute-start.2 = (bf16[5,64,128]{2,1,0:T(8,128)(2,1)}, bf16[5,64,128]{2,1,0:T(8,128)(2,1)S(1)}, u32[]{:S(2)}, u32[]{:S(2)}) collective-permute-start(bf16[5,64,128]{2,1,0:T(8,128)(2,1)} %get-tuple-element.34), channel_id=1, source_target_pairs={{0,6},{1,7},{2,4},{3,5},{4,2},{5,3},{6,0},{7,1},{8,14},{9,15},{10,... | collective-permute-start | bytes 245768 | tf_op jit(solution)/shard_map/ppermute | solution.py:285
  8.1 6.8 %copy-start.2 = (bf16[5,64,128]{2,1,0:T(8,128)(2,1)S(1)}, bf16[5,64,128]{2,1,0:T(8,128)(2,1)}, u32[]{:S(2)}) copy-start(bf16[5,64,128]{2,1,0:T(8,128)(2,1)} %get-tuple-element.31.refs_0_) | copy-start | bytes 245764
  8.1 22.4 %all-to-all-start = ((bf16[32,64,128]{2,1,0:T(8,128)(2,1)}), bf16[32,64,128]{2,1,0:T(8,128)(2,1)S(1)}, u32[]{:S(2)}, u32[]{:S(2)}) async-start(bf16[32,64,128]{2,1,0:T(8,128)(2,1)} %get-tuple-element.30), calls=%async_computation | async-start | bytes 1048576 | tf_op jit(solution)/shard_map/all_to_all | solution.py:318
  14.9 7.3 %collective-permute-start.3 = (bf16[4,64,128]{2,1,0:T(8,128)(2,1)S(1)}, bf16[4,64,128]{2,1,0:T(8,128)(2,1)S(1)}, u32[]{:S(2)}, u32[]{:S(2)}) collective-permute-start(bf16[4,64,128]{2,1,0:T(8,128)(2,1)S(1)} %get-tuple-element.36), channel_id=1, source_target_pairs={{0,8},{8,0},{16,24},{24,16},{1,9},{9,1},{17,25},{25,17},{2,10},{10... | collective-permute-start | bytes 196616 | tf_op jit(solution)/shard_map/ppermute | solution.py:285
  16.5 6.1 %collective-permute-start.4 = (bf16[4,64,128]{2,1,0:T(8,128)(2,1)S(1)}, bf16[4,64,128]{2,1,0:T(8,128)(2,1)S(1)}, u32[]{:S(2)}, u32[]{:S(2)}) collective-permute-start(bf16[4,64,128]{2,1,0:T(8,128)(2,1)S(1)} %get-tuple-element.37), channel_id=1, source_target_pairs={{0,16},{8,24},{16,0},{24,8},{1,17},{9,25},{17,1},{25,9},{2,18},{10... | collective-permute-start | bytes 196616 | tf_op jit(solution)/shard_map/ppermute | solution.py:285
  18.0 6.6 %collective-permute-start.5 = (bf16[4,64,128]{2,1,0:T(8,128)(2,1)S(1)}, bf16[4,64,128]{2,1,0:T(8,128)(2,1)S(1)}, u32[]{:S(2)}, u32[]{:S(2)}) collective-permute-start(bf16[4,64,128]{2,1,0:T(8,128)(2,1)S(1)} %get-tuple-element.38), channel_id=1, source_target_pairs={{0,24},{8,16},{16,8},{24,0},{1,25},{9,17},{17,9},{25,1},{2,26},{10... | collective-permute-start | bytes 196616 | tf_op jit(solution)/shard_map/ppermute | solution.py:285
  22.6 2.1 %copy-start = (s32[8,8,32]{2,1,0:T(8,128)S(1)}, s32[8,8,32]{2,1,0:T(8,128)}, u32[]{:S(2)}) copy-start(s32[8,8,32]{2,1,0:T(8,128)} %kept_hbm.1) | copy-start | bytes 24580
  22.6 2.1 %copy-start.1 = (s32[8]{0:T(128)S(1)}, s32[8]{0:T(128)}, u32[]{:S(2)}) copy-start(s32[8]{0:T(128)} %shift_hbm.3) | copy-start | bytes 100
  24.6 1.6 %collective-permute-start.6 = (bf16[16,64,128]{2,1,0:T(8,128)(2,1)S(1)}, bf16[16,64,128]{2,1,0:T(8,128)(2,1)S(1)}, u32[]{:S(2)}, u32[]{:S(2)}) collective-permute-start(bf16[16,64,128]{2,1,0:T(8,128)(2,1)S(1)} %constant_dynamic-update-slice_fusion.own_ref), channel_id=1, source_target_pairs={{0,1},{1,0},{2,3},{3,2},{4,5},{5,4},{6,7},{7,6},{8,9},{9,8},{10,11... | collective-permute-start | bytes 786440 | tf_op jit(solution)/shard_map/ppermute | solution.py:285
  27.3 9.6 %collective-permute-start.7 = (bf16[8,64,128]{2,1,0:T(8,128)(2,1)S(1)}, bf16[8,64,128]{2,1,0:T(8,128)(2,1)S(1)}, u32[]{:S(2)}, u32[]{:S(2)}) collective-permute-start(bf16[8,64,128]{2,1,0:T(8,128)(2,1)S(1)} %get-tuple-element.44), channel_id=1, source_target_pairs={{0,4},{1,5},{2,6},{3,7},{4,0},{5,1},{6,2},{7,3},{8,12},{9,13},{10,... | collective-permute-start | bytes 393224 | tf_op jit(solution)/shard_map/ppermute | solution.py:285
  32.3 19.3 %all-to-all-start.1 = ((bf16[32,64,128]{2,1,0:T(8,128)(2,1)}), bf16[32,64,128]{2,1,0:T(8,128)(2,1)S(1)}, u32[]{:S(2)}, u32[]{:S(2)}) async-start(bf16[32,64,128]{2,1,0:T(8,128)(2,1)} %full.1), calls=%async_computation.1 | async-start | bytes 1048576 | tf_op jit(solution)/shard_map/all_to_all | solution.py:401
  36.8 6.2 %collective-permute-start.12 = (bf16[4,64,128]{2,1,0:T(8,128)(2,1)S(1)}, bf16[4,64,128]{2,1,0:T(8,128)(2,1)S(1)}, u32[]{:S(2)}, u32[]{:S(2)}) collective-permute-start(bf16[4,64,128]{2,1,0:T(8,128)(2,1)S(1)} %get-tuple-element.48), channel_id=1, source_target_pairs={{0,8},{8,0},{16,24},{24,16},{1,9},{9,1},{17,25},{25,17},{2,10},{10... | collective-permute-start | bytes 196616 | tf_op jit(solution)/shard_map/ppermute | solution.py:285
  37.4 6.5 %collective-permute-start.13 = (bf16[4,64,128]{2,1,0:T(8,128)(2,1)S(1)}, bf16[4,64,128]{2,1,0:T(8,128)(2,1)S(1)}, u32[]{:S(2)}, u32[]{:S(2)}) collective-permute-start(bf16[4,64,128]{2,1,0:T(8,128)(2,1)S(1)} %get-tuple-element.49), channel_id=1, source_target_pairs={{0,16},{8,24},{16,0},{24,8},{1,17},{9,25},{17,1},{25,9},{2,18},{10... | collective-permute-start | bytes 196616 | tf_op jit(solution)/shard_map/ppermute | solution.py:285
  38.1 7.7 %collective-permute-start.14 = (bf16[4,64,128]{2,1,0:T(8,128)(2,1)S(1)}, bf16[4,64,128]{2,1,0:T(8,128)(2,1)S(1)}, u32[]{:S(2)}, u32[]{:S(2)}) collective-permute-start(bf16[4,64,128]{2,1,0:T(8,128)(2,1)S(1)} %get-tuple-element.50), channel_id=1, source_target_pairs={{0,24},{8,16},{16,8},{24,0},{1,25},{9,17},{17,9},{25,1},{2,26},{10... | collective-permute-start | bytes 196616 | tf_op jit(solution)/shard_map/ppermute | solution.py:285
  40.4 7.5 %collective-permute-start.10 = (bf16[4,64,128]{2,1,0:T(8,128)(2,1)S(1)}, bf16[4,64,128]{2,1,0:T(8,128)(2,1)S(1)}, u32[]{:S(2)}, u32[]{:S(2)}) collective-permute-start(bf16[4,64,128]{2,1,0:T(8,128)(2,1)S(1)} %get-tuple-element.46.refs_0_.refs_3_), channel_id=1, source_target_pairs={{0,24},{8,16},{16,8},{24,0},{1,25},{9,17},{17,9},{25,1},{2,26},{10... | collective-permute-start | bytes 196616 | tf_op jit(solution)/shard_map/ppermute | solution.py:285
  41.0 7.6 %collective-permute-start.9 = (bf16[4,64,128]{2,1,0:T(8,128)(2,1)S(1)}, bf16[4,64,128]{2,1,0:T(8,128)(2,1)S(1)}, u32[]{:S(2)}, u32[]{:S(2)}) collective-permute-start(bf16[4,64,128]{2,1,0:T(8,128)(2,1)S(1)} %get-tuple-element.46.refs_0_.refs_3_), channel_id=1, source_target_pairs={{0,16},{8,24},{16,0},{24,8},{1,17},{9,25},{17,1},{25,9},{2,18},{10... | collective-permute-start | bytes 196616 | tf_op jit(solution)/shard_map/ppermute | solution.py:285
  43.1 5.6 %collective-permute-start.8 = (bf16[4,64,128]{2,1,0:T(8,128)(2,1)S(1)}, bf16[4,64,128]{2,1,0:T(8,128)(2,1)S(1)}, u32[]{:S(2)}, u32[]{:S(2)}) collective-permute-start(bf16[4,64,128]{2,1,0:T(8,128)(2,1)S(1)} %get-tuple-element.46.refs_0_.refs_3_), channel_id=1, source_target_pairs={{0,8},{8,0},{16,24},{24,16},{1,9},{9,1},{17,25},{25,17},{2,10},{10... | collective-permute-start | bytes 196616 | tf_op jit(solution)/shard_map/ppermute | solution.py:285
  45.8 5.7 %collective-permute-start.15 = (bf16[8,64,128]{2,1,0:T(8,128)(2,1)S(1)}, bf16[8,64,128]{2,1,0:T(8,128)(2,1)S(1)}, u32[]{:S(2)}, u32[]{:S(2)}) collective-permute-start(bf16[8,64,128]{2,1,0:T(8,128)(2,1)S(1)} %get-tuple-element.52), channel_id=1, source_target_pairs={{0,2},{1,3},{2,0},{3,1},{4,6},{5,7},{6,4},{7,5},{8,10},{9,11},{10,... | collective-permute-start | bytes 393224 | tf_op jit(solution)/shard_map/ppermute | solution.py:285
  48.6 2.9 %collective-permute-start.11 = (bf16[16,64,128]{2,1,0:T(8,128)(2,1)S(1)}, bf16[16,64,128]{2,1,0:T(8,128)(2,1)S(1)}, u32[]{:S(2)}, u32[]{:S(2)}) collective-permute-start(bf16[16,64,128]{2,1,0:T(8,128)(2,1)S(1)} %join.1), channel_id=1, source_target_pairs={{0,1},{1,0},{2,3},{3,2},{4,5},{5,4},{6,7},{7,6},{8,9},{9,8},{10,11... | collective-permute-start | bytes 786440 | tf_op jit(solution)/shard_map/ppermute | solution.py:285

commit v8 on v7

--- a/solution.py
+++ b/solution.py
@@ -282,7 +282,10 @@
 
 
 def swapped(shard, axis, by):
-    return lax.ppermute(shard, axis, [(i, i ^ by) for i in range(lax.axis_size(axis))])
+    n_col = lax.axis_size("col")
+    total = lax.axis_size("row") * n_col
+    apart = by * (n_col if axis == "row" else 1)
+    return lax.ppermute(shard, ("row", "col"), [(i, i ^ apart) for i in reversed(range(total))])
 
 
 def body(density, density_rows, square_rows, panel_shift):

time: 54.2 us -> 54.2 us (level)
  no operation moved by 1% of the time
where the time goes in v8:
time: 54.2 us; the launch traced here: 53.9 us
  starting transfers between devices  29.4 us (54%)
  waiting for transfers between devices  15.9 us (29%)
  Pallas kernels  8.33 us (15%)
    ppermute x16, starting transfers between devices, swapped(): lax.ppermute(shard, ('row', 'col'), [(i, i ^ apart) for i in reversed(ran...  20.7 us
    ppermute x16, waiting for transfers between devices, swapped(): lax.ppermute(shard, ('row', 'col'), [(i, i ^ apart) for i in reversed(ran...  15.6 us
    all_to_all x1, starting transfers between devices, body(): y = lax.all_to_all(packed, both, 0, 0, tiled=True)  6.07 us
    all_to_all x1, starting transfers between devices, body(): ret = lax.all_to_all(out, both, 0, 0, tiled=True)  2.61 us
    pallas_call x1, Pallas kernels, body(): pl.pallas_call(functools.partial(pack_kernel, plan), out_shape=shapes, in...  2.38 us
    pallas_call x1, Pallas kernels, body(): pl.pallas_call(functools.partial(unpack_kernel, plan), out_shape=jax.Shap...  2.33 us
    pallas_call x1, Pallas kernels, body(): pl.pallas_call(functools.partial(full_kernel, plan), out_shape=blocks(nde...  1.75 us
  transfers between devices with their start and end apart: 18, of which 11 were waited for; matrix products, arithmetic and copies ran while one was open for 0% of the time, Pallas kernels for 7%

profile of v8, /device:TPU:0, one launch (start us, length us, event | category | flops | bytes accessed | tf_op | source)
XLA Modules:
  0.0 53.9 jit_solution(8330583474586653888)
XLA Ops:
  0.0 2.4 %pack.1 = (bf16[32,64,128]{2,1,0:T(8,128)(2,1)}, bf16[5,64,128]{2,1,0:T(8,128)(2,1)}, bf16[5,64,128]{2,1,0:T(8,128)(2,1)}, bf16[5,64,128]{2,1,0:T(8,128)(2,1)}, bf16[5,64,128]{2,1,0:T(8,128)(2,1)}) custom-call(bf16[2,64,2048]{2,1,0:T(8,128)(2,1)} %x_hbm.1, s32[8,8,32]{2,1,0:T(8,128)} %rows_hbm.1, s32[8]{0:T(128)} %shift_hbm.3), custom_call_target="tpu_custom_call" | custom-call | tf_op jit(solution)/shard_map/pack/pallas_call | solution.py:307
  2.4 3.1 %collective-permute-start = (bf16[5,64,128]{2,1,0:T(8,128)(2,1)}, bf16[5,64,128]{2,1,0:T(8,128)(2,1)S(1)}, u32[]{:S(2)}, u32[]{:S(2)}) collective-permute-start(bf16[5,64,128]{2,1,0:T(8,128)(2,1)} %get-tuple-element.32), channel_id=1, source_target_pairs={{31,29},{30,28},{29,31},{28,30},{27,25},{26,24},{25,27},{24,26},{2... | collective-permute-start | bytes 245768 | tf_op jit(solution)/shard_map/ppermute | solution.py:288
  5.5 2.6 %collective-permute-start.1 = (bf16[5,64,128]{2,1,0:T(8,128)(2,1)}, bf16[5,64,128]{2,1,0:T(8,128)(2,1)S(1)}, u32[]{:S(2)}, u32[]{:S(2)}) collective-permute-start(bf16[5,64,128]{2,1,0:T(8,128)(2,1)} %get-tuple-element.33), channel_id=1, source_target_pairs={{31,27},{30,26},{29,25},{28,24},{27,31},{26,30},{25,29},{24,28},{2... | collective-permute-start | bytes 245768 | tf_op jit(solution)/shard_map/ppermute | solution.py:288
  8.1 0.0 collective-permute-start.2
  8.1 0.0 copy-start.2
  8.1 6.1 %all-to-all-start = ((bf16[32,64,128]{2,1,0:T(8,128)(2,1)}), bf16[32,64,128]{2,1,0:T(8,128)(2,1)S(1)}, u32[]{:S(2)}, u32[]{:S(2)}) async-start(bf16[32,64,128]{2,1,0:T(8,128)(2,1)} %get-tuple-element.30), calls=%async_computation | async-start | bytes 1048576 | tf_op jit(solution)/shard_map/all_to_all | solution.py:321
  14.2 0.0 collective-permute-done.refs_1_
  14.2 0.7 %collective-permute-done.1.refs_2_ = bf16[5,64,128]{2,1,0:T(8,128)(2,1)S(1)} collective-permute-done((bf16[5,64,128]{2,1,0:T(8,128)(2,1)}, bf16[5,64,128]{2,1,0:T(8,128)(2,1)S(1)}, u32[]{:S(2)}, u32[]{:S(2)}) %collective-permute-start.1) | collective-permute-done | bytes 81952 | tf_op jit(solution)/shard_map/ppermute | solution.py:288
  14.9 0.0 collective-permute-done.2.refs_3_
  14.9 0.0 copy-done.2
  14.9 1.6 %collective-permute-start.3 = (bf16[4,64,128]{2,1,0:T(8,128)(2,1)S(1)}, bf16[4,64,128]{2,1,0:T(8,128)(2,1)S(1)}, u32[]{:S(2)}, u32[]{:S(2)}) collective-permute-start(bf16[4,64,128]{2,1,0:T(8,128)(2,1)S(1)} %get-tuple-element.36), channel_id=1, source_target_pairs={{31,23},{30,22},{29,21},{28,20},{27,19},{26,18},{25,17},{24,16},{2... | collective-permute-start | bytes 196616 | tf_op jit(solution)/shard_map/ppermute | solution.py:288
  16.5 1.5 %collective-permute-start.4 = (bf16[4,64,128]{2,1,0:T(8,128)(2,1)S(1)}, bf16[4,64,128]{2,1,0:T(8,128)(2,1)S(1)}, u32[]{:S(2)}, u32[]{:S(2)}) collective-permute-start(bf16[4,64,128]{2,1,0:T(8,128)(2,1)S(1)} %get-tuple-element.37), channel_id=1, source_target_pairs={{31,15},{30,14},{29,13},{28,12},{27,11},{26,10},{25,9},{24,8},{23,... | collective-permute-start | bytes 196616 | tf_op jit(solution)/shard_map/ppermute | solution.py:288
  18.0 0.5 collective-permute-start.5
  18.5 3.8 %collective-permute-done.3 = bf16[4,64,128]{2,1,0:T(8,128)(2,1)S(1)} collective-permute-done((bf16[4,64,128]{2,1,0:T(8,128)(2,1)S(1)}, bf16[4,64,128]{2,1,0:T(8,128)(2,1)S(1)}, u32[]{:S(2)}, u32[]{:S(2)}) %collective-permute-start.3) | collective-permute-done | bytes 65568 | tf_op jit(solution)/shard_map/ppermute | solution.py:288
  22.2 0.4 collective-permute-done.4
  22.6 0.0 copy-start
  22.6 0.0 copy-start.1
  22.7 1.9 %collective-permute-done.5 = bf16[4,64,128]{2,1,0:T(8,128)(2,1)S(1)} collective-permute-done((bf16[4,64,128]{2,1,0:T(8,128)(2,1)S(1)}, bf16[4,64,128]{2,1,0:T(8,128)(2,1)S(1)}, u32[]{:S(2)}, u32[]{:S(2)}) %collective-permute-start.5) | collective-permute-done | bytes 65568 | tf_op jit(solution)/shard_map/ppermute | solution.py:288
  24.6 0.1 collective-permute-start.6
  24.7 0.0 copy-done
  24.7 0.0 copy-done.1
  24.7 0.7 %masks.1.keep_ref.refs_1_ = f32[3,8,512]{2,1,0:T(8,128)S(1)} custom-call(s32[8]{0:T(128)S(1)} %copy-done.1, s32[8,8,32]{2,1,0:T(8,128)S(1)} %copy-done), custom_call_target="tpu_custom_call" | custom-call | tf_op jit(solution)/shard_map/masks/pallas_call | solution.py:323
  25.5 0.8 %collective-permute-done.6.far_ref = bf16[16,64,128]{2,1,0:T(8,128)(2,1)S(1)} collective-permute-done((bf16[16,64,128]{2,1,0:T(8,128)(2,1)S(1)}, bf16[16,64,128]{2,1,0:T(8,128)(2,1)S(1)}, u32[]{:S(2)}, u32[]{:S(2)}) %collective-permute-start.6) | collective-permute-done | bytes 262176 | tf_op jit(solution)/shard_map/ppermute | solution.py:288
  26.2 1.0 %shared.1 = (bf16[8,64,128]{2,1,0:T(8,128)(2,1)S(1)}, bf16[8,64,128]{2,1,0:T(8,128)(2,1)S(1)}) custom-call(f32[3,8,512]{2,1,0:T(8,128)S(1)} %masks.1.keep_ref.refs_1_, bf16[16,64,128]{2,1,0:T(8,128)(2,1)S(1)} %constant_dynamic-update-slice_fusion.own_ref, bf16[16,64,128]{2,1,0:T(8,128)(2,1)S(1)} %collective-permute-done.6.far_ref), custom_call_target="tpu_custom_call" | custom-call | tf_op jit(solution)/shard_map/shared/pallas_call | solution.py:351
  27.3 2.9 %collective-permute-start.7 = (bf16[8,64,128]{2,1,0:T(8,128)(2,1)S(1)}, bf16[8,64,128]{2,1,0:T(8,128)(2,1)S(1)}, u32[]{:S(2)}, u32[]{:S(2)}) collective-permute-start(bf16[8,64,128]{2,1,0:T(8,128)(2,1)S(1)} %get-tuple-element.44), channel_id=1, source_target_pairs={{31,27},{30,26},{29,25},{28,24},{27,31},{26,30},{25,29},{24,28},{2... | collective-permute-start | bytes 393224 | tf_op jit(solution)/shard_map/ppermute | solution.py:288
  30.2 0.3 all-to-all-done.y_ref
  30.5 1.8 %full.1 = bf16[32,64,128]{2,1,0:T(8,128)(2,1)} custom-call(f32[3,8,512]{2,1,0:T(8,128)S(1)} %masks.1.keep_ref.refs_1_, bf16[32,64,128]{2,1,0:T(8,128)(2,1)S(1)} %all-to-all-done.y_ref), custom_call_target="tpu_custom_call" | custom-call | flops 536870912 | bytes 1048576 | tf_op jit(solution)/shard_map/full/pallas_call | solution.py:394
  32.3 2.6 %all-to-all-start.1 = ((bf16[32,64,128]{2,1,0:T(8,128)(2,1)}), bf16[32,64,128]{2,1,0:T(8,128)(2,1)S(1)}, u32[]{:S(2)}, u32[]{:S(2)}) async-start(bf16[32,64,128]{2,1,0:T(8,128)(2,1)} %full.1), calls=%async_computation.1 | async-start | bytes 1048576 | tf_op jit(solution)/shard_map/all_to_all | solution.py:404
  34.9 1.9 %collective-permute-done.7.refs_1_ = bf16[8,64,128]{2,1,0:T(8,128)(2,1)S(1)} collective-permute-done((bf16[8,64,128]{2,1,0:T(8,128)(2,1)S(1)}, bf16[8,64,128]{2,1,0:T(8,128)(2,1)S(1)}, u32[]{:S(2)}, u32[]{:S(2)}) %collective-permute-start.7) | collective-permute-done | bytes 131104 | tf_op jit(solution)/shard_map/ppermute | solution.py:288
  36.8 0.5 collective-permute-start.12
  37.4 0.8 %collective-permute-start.13 = (bf16[4,64,128]{2,1,0:T(8,128)(2,1)S(1)}, bf16[4,64,128]{2,1,0:T(8,128)(2,1)S(1)}, u32[]{:S(2)}, u32[]{:S(2)}) collective-permute-start(bf16[4,64,128]{2,1,0:T(8,128)(2,1)S(1)} %get-tuple-element.49), channel_id=1, source_target_pairs={{31,15},{30,14},{29,13},{28,12},{27,11},{26,10},{25,9},{24,8},{23,... | collective-permute-start | bytes 196616 | tf_op jit(solution)/shard_map/ppermute | solution.py:288
  38.1 2.3 %collective-permute-start.14 = (bf16[4,64,128]{2,1,0:T(8,128)(2,1)S(1)}, bf16[4,64,128]{2,1,0:T(8,128)(2,1)S(1)}, u32[]{:S(2)}, u32[]{:S(2)}) collective-permute-start(bf16[4,64,128]{2,1,0:T(8,128)(2,1)S(1)} %get-tuple-element.50), channel_id=1, source_target_pairs={{31,7},{30,6},{29,5},{28,4},{27,3},{26,2},{25,1},{24,0},{23,15},{2... | collective-permute-start | bytes 196616 | tf_op jit(solution)/shard_map/ppermute | solution.py:288
  40.4 0.6 %collective-permute-start.10 = (bf16[4,64,128]{2,1,0:T(8,128)(2,1)S(1)}, bf16[4,64,128]{2,1,0:T(8,128)(2,1)S(1)}, u32[]{:S(2)}, u32[]{:S(2)}) collective-permute-start(bf16[4,64,128]{2,1,0:T(8,128)(2,1)S(1)} %get-tuple-element.46.refs_0_.refs_3_), channel_id=1, source_target_pairs={{31,7},{30,6},{29,5},{28,4},{27,3},{26,2},{25,1},{24,0},{23,15},{2... | collective-permute-start | bytes 196616 | tf_op jit(solution)/shard_map/ppermute | solution.py:288
  41.0 1.3 %collective-permute-start.9 = (bf16[4,64,128]{2,1,0:T(8,128)(2,1)S(1)}, bf16[4,64,128]{2,1,0:T(8,128)(2,1)S(1)}, u32[]{:S(2)}, u32[]{:S(2)}) collective-permute-start(bf16[4,64,128]{2,1,0:T(8,128)(2,1)S(1)} %get-tuple-element.46.refs_0_.refs_3_), channel_id=1, source_target_pairs={{31,15},{30,14},{29,13},{28,12},{27,11},{26,10},{25,9},{24,8},{23,... | collective-permute-start | bytes 196616 | tf_op jit(solution)/shard_map/ppermute | solution.py:288
  42.3 0.8 %collective-permute-done.12.refs_1_ = bf16[4,64,128]{2,1,0:T(8,128)(2,1)S(1)} collective-permute-done((bf16[4,64,128]{2,1,0:T(8,128)(2,1)S(1)}, bf16[4,64,128]{2,1,0:T(8,128)(2,1)S(1)}, u32[]{:S(2)}, u32[]{:S(2)}) %collective-permute-start.12) | collective-permute-done | bytes 65568 | tf_op jit(solution)/shard_map/ppermute | solution.py:288
  43.1 0.8 %collective-permute-start.8 = (bf16[4,64,128]{2,1,0:T(8,128)(2,1)S(1)}, bf16[4,64,128]{2,1,0:T(8,128)(2,1)S(1)}, u32[]{:S(2)}, u32[]{:S(2)}) collective-permute-start(bf16[4,64,128]{2,1,0:T(8,128)(2,1)S(1)} %get-tuple-element.46.refs_0_.refs_3_), channel_id=1, source_target_pairs={{31,23},{30,22},{29,21},{28,20},{27,19},{26,18},{25,17},{24,16},{2... | collective-permute-start | bytes 196616 | tf_op jit(solution)/shard_map/ppermute | solution.py:288
  43.9 0.0 collective-permute-done.13.refs_2_
  43.9 1.9 %collective-permute-done.14.refs_3_ = bf16[4,64,128]{2,1,0:T(8,128)(2,1)S(1)} collective-permute-done((bf16[4,64,128]{2,1,0:T(8,128)(2,1)S(1)}, bf16[4,64,128]{2,1,0:T(8,128)(2,1)S(1)}, u32[]{:S(2)}, u32[]{:S(2)}) %collective-permute-start.14) | collective-permute-done | bytes 65568 | tf_op jit(solution)/shard_map/ppermute | solution.py:288
  45.8 2.1 %collective-permute-start.15 = (bf16[8,64,128]{2,1,0:T(8,128)(2,1)S(1)}, bf16[8,64,128]{2,1,0:T(8,128)(2,1)S(1)}, u32[]{:S(2)}, u32[]{:S(2)}) collective-permute-start(bf16[8,64,128]{2,1,0:T(8,128)(2,1)S(1)} %get-tuple-element.52), channel_id=1, source_target_pairs={{31,29},{30,28},{29,31},{28,30},{27,25},{26,24},{25,27},{24,26},{2... | collective-permute-start | bytes 393224 | tf_op jit(solution)/shard_map/ppermute | solution.py:288
  47.9 0.0 collective-permute-done.10.refs_3_.refs_6_
  47.9 0.7 %collective-permute-done.9.refs_2_.refs_5_ = bf16[4,64,128]{2,1,0:T(8,128)(2,1)S(1)} collective-permute-done((bf16[4,64,128]{2,1,0:T(8,128)(2,1)S(1)}, bf16[4,64,128]{2,1,0:T(8,128)(2,1)S(1)}, u32[]{:S(2)}, u32[]{:S(2)}) %collective-permute-start.9) | collective-permute-done | bytes 65568 | tf_op jit(solution)/shard_map/ppermute | solution.py:288
  48.6 0.0 collective-permute-done.8.refs_1_.refs_4_
  48.6 0.1 collective-permute-start.11
  48.7 2.8 %collective-permute-done.15.refs_1_ = bf16[8,64,128]{2,1,0:T(8,128)(2,1)S(1)} collective-permute-done((bf16[8,64,128]{2,1,0:T(8,128)(2,1)S(1)}, bf16[8,64,128]{2,1,0:T(8,128)(2,1)S(1)}, u32[]{:S(2)}, u32[]{:S(2)}) %collective-permute-start.15) | collective-permute-done | bytes 131104 | tf_op jit(solution)/shard_map/ppermute | solution.py:288
  51.5 0.0 collective-permute-done.11.refs_2_
  51.6 0.0 all-to-all-done.1.ret_ref
  51.6 2.3 %unpack.1 = f32[2,64,2048]{2,1,0:T(8,128)} custom-call(s32[8,8,32]{2,1,0:T(8,128)S(1)} %copy-done, s32[8]{0:T(128)S(1)} %copy-done.1, bf16[32,64,128]{2,1,0:T(8,128)(2,1)S(1)} %all-to-all-done.1.ret_ref, bf16[16,64,128]{2,1,0:T(8,128)(2,1)S(1)} %join_back.1.refs_0_, f32[3,8,512]{2,1,0:T(8,128)S(1)} %masks.1.keep_ref.refs_1_, ...), custom_call_target="tpu_custom_call" | custom-call | tf_op jit(solution)/shard_map/unpack/pallas_call | solution.py:405
  (9 shorter events, 0.1 us)
Async XLA Ops:
  2.4 11.8 %collective-permute-start = (bf16[5,64,128]{2,1,0:T(8,128)(2,1)}, bf16[5,64,128]{2,1,0:T(8,128)(2,1)S(1)}, u32[]{:S(2)}, u32[]{:S(2)}) collective-permute-start(bf16[5,64,128]{2,1,0:T(8,128)(2,1)} %get-tuple-element.32), channel_id=1, source_target_pairs={{31,29},{30,28},{29,31},{28,30},{27,25},{26,24},{25,27},{24,26},{2... | collective-permute-start | bytes 245768 | tf_op jit(solution)/shard_map/ppermute | solution.py:288
  5.5 9.4 %collective-permute-start.1 = (bf16[5,64,128]{2,1,0:T(8,128)(2,1)}, bf16[5,64,128]{2,1,0:T(8,128)(2,1)S(1)}, u32[]{:S(2)}, u32[]{:S(2)}) collective-permute-start(bf16[5,64,128]{2,1,0:T(8,128)(2,1)} %get-tuple-element.33), channel_id=1, source_target_pairs={{31,27},{30,26},{29,25},{28,24},{27,31},{26,30},{25,29},{24,28},{2... | collective-permute-start | bytes 245768 | tf_op jit(solution)/shard_map/ppermute | solution.py:288
  8.1 6.8 %collective-permute-start.2 = (bf16[5,64,128]{2,1,0:T(8,128)(2,1)}, bf16[5,64,128]{2,1,0:T(8,128)(2,1)S(1)}, u32[]{:S(2)}, u32[]{:S(2)}) collective-permute-start(bf16[5,64,128]{2,1,0:T(8,128)(2,1)} %get-tuple-element.34), channel_id=1, source_target_pairs={{31,25},{30,24},{29,27},{28,26},{27,29},{26,28},{25,31},{24,30},{2... | collective-permute-start | bytes 245768 | tf_op jit(solution)/shard_map/ppermute | solution.py:288
  8.1 6.8 %copy-start.2 = (bf16[5,64,128]{2,1,0:T(8,128)(2,1)S(1)}, bf16[5,64,128]{2,1,0:T(8,128)(2,1)}, u32[]{:S(2)}) copy-start(bf16[5,64,128]{2,1,0:T(8,128)(2,1)} %get-tuple-element.31.refs_0_) | copy-start | bytes 245764
  8.1 22.4 %all-to-all-start = ((bf16[32,64,128]{2,1,0:T(8,128)(2,1)}), bf16[32,64,128]{2,1,0:T(8,128)(2,1)S(1)}, u32[]{:S(2)}, u32[]{:S(2)}) async-start(bf16[32,64,128]{2,1,0:T(8,128)(2,1)} %get-tuple-element.30), calls=%async_computation | async-start | bytes 1048576 | tf_op jit(solution)/shard_map/all_to_all | solution.py:321
  14.9 7.3 %collective-permute-start.3 = (bf16[4,64,128]{2,1,0:T(8,128)(2,1)S(1)}, bf16[4,64,128]{2,1,0:T(8,128)(2,1)S(1)}, u32[]{:S(2)}, u32[]{:S(2)}) collective-permute-start(bf16[4,64,128]{2,1,0:T(8,128)(2,1)S(1)} %get-tuple-element.36), channel_id=1, source_target_pairs={{31,23},{30,22},{29,21},{28,20},{27,19},{26,18},{25,17},{24,16},{2... | collective-permute-start | bytes 196616 | tf_op jit(solution)/shard_map/ppermute | solution.py:288
  16.5 6.1 %collective-permute-start.4 = (bf16[4,64,128]{2,1,0:T(8,128)(2,1)S(1)}, bf16[4,64,128]{2,1,0:T(8,128)(2,1)S(1)}, u32[]{:S(2)}, u32[]{:S(2)}) collective-permute-start(bf16[4,64,128]{2,1,0:T(8,128)(2,1)S(1)} %get-tuple-element.37), channel_id=1, source_target_pairs={{31,15},{30,14},{29,13},{28,12},{27,11},{26,10},{25,9},{24,8},{23,... | collective-permute-start | bytes 196616 | tf_op jit(solution)/shard_map/ppermute | solution.py:288
  18.0 6.6 %collective-permute-start.5 = (bf16[4,64,128]{2,1,0:T(8,128)(2,1)S(1)}, bf16[4,64,128]{2,1,0:T(8,128)(2,1)S(1)}, u32[]{:S(2)}, u32[]{:S(2)}) collective-permute-start(bf16[4,64,128]{2,1,0:T(8,128)(2,1)S(1)} %get-tuple-element.38), channel_id=1, source_target_pairs={{31,7},{30,6},{29,5},{28,4},{27,3},{26,2},{25,1},{24,0},{23,15},{2... | collective-permute-start | bytes 196616 | tf_op jit(solution)/shard_map/ppermute | solution.py:288
  22.6 2.1 %copy-start = (s32[8,8,32]{2,1,0:T(8,128)S(1)}, s32[8,8,32]{2,1,0:T(8,128)}, u32[]{:S(2)}) copy-start(s32[8,8,32]{2,1,0:T(8,128)} %kept_hbm.1) | copy-start | bytes 24580
  22.6 2.1 %copy-start.1 = (s32[8]{0:T(128)S(1)}, s32[8]{0:T(128)}, u32[]{:S(2)}) copy-start(s32[8]{0:T(128)} %shift_hbm.3) | copy-start | bytes 100
  24.6 1.6 %collective-permute-start.6 = (bf16[16,64,128]{2,1,0:T(8,128)(2,1)S(1)}, bf16[16,64,128]{2,1,0:T(8,128)(2,1)S(1)}, u32[]{:S(2)}, u32[]{:S(2)}) collective-permute-start(bf16[16,64,128]{2,1,0:T(8,128)(2,1)S(1)} %constant_dynamic-update-slice_fusion.own_ref), channel_id=1, source_target_pairs={{31,30},{30,31},{29,28},{28,29},{27,26},{26,27},{25,24},{24,25},{2... | collective-permute-start | bytes 786440 | tf_op jit(solution)/shard_map/ppermute | solution.py:288
  27.3 9.6 %collective-permute-start.7 = (bf16[8,64,128]{2,1,0:T(8,128)(2,1)S(1)}, bf16[8,64,128]{2,1,0:T(8,128)(2,1)S(1)}, u32[]{:S(2)}, u32[]{:S(2)}) collective-permute-start(bf16[8,64,128]{2,1,0:T(8,128)(2,1)S(1)} %get-tuple-element.44), channel_id=1, source_target_pairs={{31,27},{30,26},{29,25},{28,24},{27,31},{26,30},{25,29},{24,28},{2... | collective-permute-start | bytes 393224 | tf_op jit(solution)/shard_map/ppermute | solution.py:288
  32.3 19.3 %all-to-all-start.1 = ((bf16[32,64,128]{2,1,0:T(8,128)(2,1)}), bf16[32,64,128]{2,1,0:T(8,128)(2,1)S(1)}, u32[]{:S(2)}, u32[]{:S(2)}) async-start(bf16[32,64,128]{2,1,0:T(8,128)(2,1)} %full.1), calls=%async_computation.1 | async-start | bytes 1048576 | tf_op jit(solution)/shard_map/all_to_all | solution.py:404
  36.8 6.2 %collective-permute-start.12 = (bf16[4,64,128]{2,1,0:T(8,128)(2,1)S(1)}, bf16[4,64,128]{2,1,0:T(8,128)(2,1)S(1)}, u32[]{:S(2)}, u32[]{:S(2)}) collective-permute-start(bf16[4,64,128]{2,1,0:T(8,128)(2,1)S(1)} %get-tuple-element.48), channel_id=1, source_target_pairs={{31,23},{30,22},{29,21},{28,20},{27,19},{26,18},{25,17},{24,16},{2... | collective-permute-start | bytes 196616 | tf_op jit(solution)/shard_map/ppermute | solution.py:288
  37.4 6.5 %collective-permute-start.13 = (bf16[4,64,128]{2,1,0:T(8,128)(2,1)S(1)}, bf16[4,64,128]{2,1,0:T(8,128)(2,1)S(1)}, u32[]{:S(2)}, u32[]{:S(2)}) collective-permute-start(bf16[4,64,128]{2,1,0:T(8,128)(2,1)S(1)} %get-tuple-element.49), channel_id=1, source_target_pairs={{31,15},{30,14},{29,13},{28,12},{27,11},{26,10},{25,9},{24,8},{23,... | collective-permute-start | bytes 196616 | tf_op jit(solution)/shard_map/ppermute | solution.py:288
  38.1 7.7 %collective-permute-start.14 = (bf16[4,64,128]{2,1,0:T(8,128)(2,1)S(1)}, bf16[4,64,128]{2,1,0:T(8,128)(2,1)S(1)}, u32[]{:S(2)}, u32[]{:S(2)}) collective-permute-start(bf16[4,64,128]{2,1,0:T(8,128)(2,1)S(1)} %get-tuple-element.50), channel_id=1, source_target_pairs={{31,7},{30,6},{29,5},{28,4},{27,3},{26,2},{25,1},{24,0},{23,15},{2... | collective-permute-start | bytes 196616 | tf_op jit(solution)/shard_map/ppermute | solution.py:288
  40.4 7.5 %collective-permute-start.10 = (bf16[4,64,128]{2,1,0:T(8,128)(2,1)S(1)}, bf16[4,64,128]{2,1,0:T(8,128)(2,1)S(1)}, u32[]{:S(2)}, u32[]{:S(2)}) collective-permute-start(bf16[4,64,128]{2,1,0:T(8,128)(2,1)S(1)} %get-tuple-element.46.refs_0_.refs_3_), channel_id=1, source_target_pairs={{31,7},{30,6},{29,5},{28,4},{27,3},{26,2},{25,1},{24,0},{23,15},{2... | collective-permute-start | bytes 196616 | tf_op jit(solution)/shard_map/ppermute | solution.py:288
  41.0 7.6 %collective-permute-start.9 = (bf16[4,64,128]{2,1,0:T(8,128)(2,1)S(1)}, bf16[4,64,128]{2,1,0:T(8,128)(2,1)S(1)}, u32[]{:S(2)}, u32[]{:S(2)}) collective-permute-start(bf16[4,64,128]{2,1,0:T(8,128)(2,1)S(1)} %get-tuple-element.46.refs_0_.refs_3_), channel_id=1, source_target_pairs={{31,15},{30,14},{29,13},{28,12},{27,11},{26,10},{25,9},{24,8},{23,... | collective-permute-start | bytes 196616 | tf_op jit(solution)/shard_map/ppermute | solution.py:288
  43.1 5.6 %collective-permute-start.8 = (bf16[4,64,128]{2,1,0:T(8,128)(2,1)S(1)}, bf16[4,64,128]{2,1,0:T(8,128)(2,1)S(1)}, u32[]{:S(2)}, u32[]{:S(2)}) collective-permute-start(bf16[4,64,128]{2,1,0:T(8,128)(2,1)S(1)} %get-tuple-element.46.refs_0_.refs_3_), channel_id=1, source_target_pairs={{31,23},{30,22},{29,21},{28,20},{27,19},{26,18},{25,17},{24,16},{2... | collective-permute-start | bytes 196616 | tf_op jit(solution)/shard_map/ppermute | solution.py:288
  45.8 5.7 %collective-permute-start.15 = (bf16[8,64,128]{2,1,0:T(8,128)(2,1)S(1)}, bf16[8,64,128]{2,1,0:T(8,128)(2,1)S(1)}, u32[]{:S(2)}, u32[]{:S(2)}) collective-permute-start(bf16[8,64,128]{2,1,0:T(8,128)(2,1)S(1)} %get-tuple-element.52), channel_id=1, source_target_pairs={{31,29},{30,28},{29,31},{28,30},{27,25},{26,24},{25,27},{24,26},{2... | collective-permute-start | bytes 393224 | tf_op jit(solution)/shard_map/ppermute | solution.py:288
  48.6 2.9 %collective-permute-start.11 = (bf16[16,64,128]{2,1,0:T(8,128)(2,1)S(1)}, bf16[16,64,128]{2,1,0:T(8,128)(2,1)S(1)}, u32[]{:S(2)}, u32[]{:S(2)}) collective-permute-start(bf16[16,64,128]{2,1,0:T(8,128)(2,1)S(1)} %join.1), channel_id=1, source_target_pairs={{31,30},{30,31},{29,28},{28,29},{27,26},{26,27},{25,24},{24,25},{2... | collective-permute-start | bytes 786440 | tf_op jit(solution)/shard_map/ppermute | solution.py:288
